TPU v7x, 32 devices: a whole 2x2x4 slice. The times are simulated.
32 devices in a mesh: ens: 2 (over y), pw: 8 (over z, x), band: 2 (over core).
Axes of the slice: x: 2, y: 2, z: 4, core: 2. Of those that a mesh axis runs over, the one named last changes fastest.
Arguments:
- trial_block: bfloat16 [4, 8, 6144], P('ens', 'band', 'pw'), parts along dimension 0, may hold values from -12 to 12
- all_bands: bfloat16 [4, 2048, 6144], P('ens', 'band', 'pw'), parts along dimension 0, may hold values from -0.078125 to 0.078125
- potential: float32 [256, 128, 128], P('ens', 'pw'), parts along dimension 0, may hold values from -8 to 8
- rest_density: float32 [256, 128, 128], P(('ens', 'band'), 'pw'), parts along dimension 0, may hold values from 0.05 to 0.4
- wave_cells: int32 [6144], P('pw'), may hold values from 0 to 262143, as said below
- kinetic: float32 [6144], P('pw'), may hold values from 0.1 to 8.4
- occupation: int32 [16], P(('ens', 'band')), parts along dimension 0, may hold values from 0 to 2
Outputs:
- correction: float32 [4, 8, 6144], P('ens', 'band', 'pw'), parts along dimension 0
- subspace_block: float32 [4, 2048, 8], P('ens', 'band'), parts along dimension 0
- density: float32 [256, 128, 128], P(('ens', 'band'), 'pw'), parts along dimension 0
There are 2 independent parts, one for each index of `ens`. A program takes and returns all parts, laid end to end along the dimension named above; an argument that names none is the same for every part. Nothing has to cross between parts.
Inputs may be any that keep to these rules, and one draw needn't show every extreme that they name: `wave_cells`: within the 768 plane waves of one device the values are distinct, and 0 and 262143 occur among them.
All inputs are finite; a program needn't handle non-finite values.
Results may differ from a plain program's by a relative error of at most 0.0056.
Values may be sent and summed in bfloat16 or wider, within the bound.
No kernel may reach another device: no remote copies, remote signals or barrier semaphores. Data moves between devices by JAX's collectives and lax.ppermute only.
A program may use at most 576 MiB of HBM per device.

v0:
```python
import math

import jax
import jax.numpy as jnp
from jax import lax
from jax.sharding import PartitionSpec as P

EPSILON = 1e-06
HIGHEST = lax.Precision.HIGHEST


def tables(length):
    positions = jnp.arange(length, dtype=jnp.int32)
    products = positions[:, None] * positions[None, :] % length
    angles = products.astype(jnp.float32) * (2.0 * math.pi / length)
    factor = 1.0 / math.sqrt(length)
    cosines = jnp.cos(angles) * factor
    sines = jnp.sin(angles) * factor
    backward = jnp.stack([jnp.stack([cosines, -sines]), jnp.stack([sines, cosines])])
    forward = jnp.stack([jnp.stack([cosines, sines]), jnp.stack([-sines, cosines])])
    return (backward, forward)


def transform(fields, table, formula):
    return jnp.einsum(formula, table, fields, precision=HIGHEST)


def inner(left, right):
    contract = (((1,), (1,)), ((), ()))
    first = lax.dot_general(left[0], right[0], contract, preferred_element_type=jnp.float32)
    second = lax.dot_general(left[1], right[1], contract, preferred_element_type=jnp.float32)
    cross_one = lax.dot_general(left[0], right[1], contract, preferred_element_type=jnp.float32)
    cross_two = lax.dot_general(left[1], right[0], contract, preferred_element_type=jnp.float32)
    return jnp.stack([first + second, cross_one - cross_two])


def on_device(trial_block, all_bands, potential, rest_density, wave_cells, kinetic, occupation):
    devices = lax.axis_size("pw")
    width_first, rows_second, width_third = potential.shape
    width_second = rows_second * devices
    slab_rows = width_first // devices
    blocks = trial_block.shape[1]
    back_first, fore_first = tables(width_first)
    back_second, fore_second = tables(width_second)
    back_third, fore_third = tables(width_third)
    along_third = "pqkc,qnabc->pnabk"
    along_second = "pqkb,qnabc->pnakc"
    along_first = "pqka,qnabc->pnkbc"
    trial_float = trial_block.astype(jnp.float32)
    filled = jnp.zeros((2, blocks, slab_rows * width_second * width_third), jnp.float32)
    filled = filled.at[:, :, wave_cells].set(trial_float)
    filled = filled.reshape(2, blocks, slab_rows, width_second, width_third)
    filled = transform(filled, back_third, along_third)
    filled = transform(filled, back_second, along_second)
    spatial = transform(
        lax.all_to_all(filled, "pw", split_axis=3, concat_axis=2, tiled=True),
        back_first,
        along_first,
    )
    power = spatial[0] * spatial[0] + spatial[1] * spatial[1]
    acted = transform(spatial * potential, fore_first, along_first)
    returned = lax.all_to_all(acted, "pw", split_axis=2, concat_axis=3, tiled=True)
    columns, power = (returned, power[None])
    columns = transform(columns, fore_second, along_second)
    columns = transform(columns, fore_third, along_third)
    applied = columns.reshape(2, blocks, slab_rows * width_second * width_third)[:, :, wave_cells]
    weights = occupation.astype(jnp.float32)
    density_part = jnp.einsum("n,nabc->abc", weights, power[0], precision=HIGHEST)
    summed_density = lax.psum(density_part.astype(jnp.bfloat16), "band").astype(jnp.float32)
    share = width_first // lax.axis_size("band")
    block_density = lax.dynamic_slice_in_dim(
        summed_density, lax.axis_index("band") * share, share, 0
    )
    density = rest_density + block_density
    action = kinetic * trial_float + applied
    damping = 1.0 / (1.0 + kinetic)
    action_half = action.astype(jnp.bfloat16)
    damped = (action * damping).astype(jnp.bfloat16)
    softened = (trial_float * damping).astype(jnp.bfloat16)
    every_trial, every_action, every_damped, every_softened = (
        lax.all_gather(trial_block, "band", axis=1, tiled=True),
        lax.all_gather(action_half, "band", axis=1, tiled=True),
        lax.all_gather(damped, "band", axis=1, tiled=True),
        lax.all_gather(softened, "band", axis=1, tiled=True),
    )
    trial_wide = every_trial.astype(jnp.float32)
    numerator = jnp.sum(trial_wide * every_action.astype(jnp.float32), axis=(0, 2))
    denominator = jnp.sum(trial_wide * trial_wide, axis=(0, 2))
    correlation = inner(all_bands, every_action)
    correlation, numerator, denominator = lax.psum((correlation, numerator, denominator), "pw")
    rayleigh = numerator / (denominator + EPSILON)
    local_terms = inner(all_bands, every_damped) - rayleigh * inner(all_bands, every_softened)
    coefficients = lax.psum(local_terms, "pw")
    coefficient_half = coefficients.astype(jnp.bfloat16)
    real_piece = coefficient_half[0]
    imag_piece = coefficient_half[1]
    contract = (((0,), (0,)), ((), ()))
    real_real = lax.dot_general(
        real_piece, all_bands[0], contract, preferred_element_type=jnp.float32
    )
    imag_imag = lax.dot_general(
        imag_piece, all_bands[1], contract, preferred_element_type=jnp.float32
    )
    imag_real = lax.dot_general(
        imag_piece, all_bands[0], contract, preferred_element_type=jnp.float32
    )
    real_imag = lax.dot_general(
        real_piece, all_bands[1], contract, preferred_element_type=jnp.float32
    )
    projected = lax.psum_scatter(
        jnp.concatenate(
            [(real_real - imag_imag)[:, None], (imag_real + real_imag)[:, None]], axis=1
        ),
        "band",
        scatter_dimension=0,
        tiled=True,
    )
    own_ratio = lax.dynamic_slice_in_dim(rayleigh, lax.axis_index("band") * blocks, blocks, 0)
    real_correction = (
        damped[0].astype(jnp.float32)
        - own_ratio[:, None] * softened[0].astype(jnp.float32)
        - projected[:, 0]
    )
    imag_correction = (
        damped[1].astype(jnp.float32)
        - own_ratio[:, None] * softened[1].astype(jnp.float32)
        - projected[:, 1]
    )
    correction = jnp.stack([real_correction, imag_correction])
    return (correction, correlation, density)


def solution(mesh):
    placed = (
        P("ens", "band", "pw"),
        P("ens", "band", "pw"),
        P("ens", "pw", None),
        P(("ens", "band"), "pw", None),
        P("pw"),
        P("pw"),
        P(("ens", "band")),
    )
    return jax.shard_map(
        on_device,
        mesh=mesh,
        in_specs=placed,
        out_specs=(P("ens", "band", "pw"), P("ens", "band", None), P(("ens", "band"), "pw", None)),
        check_vma=False,
    )
```

profile of v0, /device:TPU:0, one launch (start us, length us, event | category | flops | bytes accessed | tf_op | source)
XLA Modules:
  0.0 1043.3 jit_solution(1024732490909292013)
XLA Ops:
  8.0 0.9 sine_multiply_fusion
  8.9 0.9 fusion.135
  9.8 0.7 compare_select_fusion
  10.5 0.7 convert_bitcast_fusion
  11.7 81.1 %broadcast_in_dim.8 = f32[2,4,262144]{1,0,2:T(2,128)} broadcast(f32[]{:T(128)} %constant.15.clone.1), dimensions={} | broadcast | bytes 8388612 | tf_op jit(solution)/shard_map/broadcast_in_dim | solution.py:50
  92.8 70.4 %scatter_fusion = f32[2,4,262144]{1,0,2:T(2,128)} fusion(f32[2,4,262144]{1,0,2:T(2,128)} %broadcast_in_dim.8, s32[768]{0:T(1024)S(1)} %compare_select_fusion, f32[768,2,4]{2,1,0:T(2,128)S(1)} %copy.39), kind=kCustom, calls=%fused_computation.1 | custom fusion | bytes 76800 | tf_op jit(solution)/shard_map/scatter | solution.py:51
  163.2 211.8 %copy.63 = f32[2,4,16,128,128,1]{4,3,0,5,2,1:T(8,128)} copy(f32[2,4,16,128,128,1]{1,0,4,3,2,5:T(2,128)} %bitcast.2) | data formatting | bytes 16777216 | tf_op jit(solution)/shard_map/reshape | solution.py:52
  375.1 9.4 fusion.122
  384.5 16.1 %fusion.20 = f32[2,4,16,128,128]{3,4,0,2,1:T(8,128)} fusion(f32[4,16,128,2,128,1]{4,2,5,3,1,0:T(8,128)S(1)} %fusion.122, f32[1,2,128,128]{3,2,1,0:T(8,128)S(1)} %get-tuple-element.8, f32[1,2,128,128]{3,2,1,0:T(8,128)S(1)} %get-tuple-element.13), kind=kOutput, calls=%fused_computation.20 | convolution fusion | flops 6442516480 | bytes 17039360 | tf_op jit(solution)/shard_map/pqkb,qnabc->pnakc/dot_general | solution.py:25
  400.5 13.2 %copy.42 = f32[2,4,16,128,128]{4,0,2,1,3:T(2,128)} copy(f32[2,4,16,128,128]{3,4,0,2,1:T(8,128)} %fusion.20) | data formatting | bytes 16777216 | tf_op jit(solution)/shard_map/pqkb,qnabc->pnakc/transpose | solution.py:25
  413.7 7.5 all-to-all-start
  421.7 182.6 %all-to-all-done = f32[2,4,16,128,128]{4,0,2,1,3:T(2,128)} async-done(((f32[2,4,16,128,128]{4,0,2,1,3:T(2,128)}), f32[2,4,16,128,128]{4,0,2,1,3:T(2,128)}, u32[]{:S(2)}, u32[]{:S(2)}) %all-to-all-start) | async-done | bytes 8388640 | tf_op jit(solution)/shard_map/all_to_all | solution.py:56
  604.3 8.2 copy.43
  612.5 1.2 copy.44
  613.8 15.9 %fusion.14 = f32[2,4,128,16,128]{2,4,0,3,1:T(8,128)S(1)} fusion(f32[2,4,128,16,128,1]{4,3,2,1,0,5:T(8,128)S(1)} %bitcast.244, f32[1,2,128,128]{3,2,1,0:T(8,128)S(1)} %get-tuple-element.8, f32[1,2,128,128]{3,2,1,0:T(8,128)S(1)} %get-tuple-element.13), kind=kOutput, calls=%fused_computation.18 | convolution fusion | flops 6442516480 | bytes 17039360 | tf_op jit(solution)/shard_map/pqka,qnabc->pnkbc/dot_general | solution.py:25
  629.6 3.2 copy-done.1
  632.9 9.3 fusion.17
  642.2 13.2 %copy.47 = f32[2,4,128,16,128]{4,0,3,1,2:T(2,128)} copy(f32[2,4,128,16,128]{2,4,0,3,1:T(8,128)} %fusion.17) | data formatting | bytes 16777216 | tf_op jit(solution)/shard_map/pqka,qnabc->pnkbc/transpose | solution.py:25
  655.4 5.0 all-to-all-start.1
  660.5 6.7 fusion.12
  667.2 5.5 copy.77
  672.7 9.1 fusion.141
  681.8 0.9 convert_element_type.93
  682.8 0.6 dynamic-slice
  684.0 2.0 all_gather.12
  686.1 16.8 %all-reduce.7.cloned.1.call-done = bf16[128,16,128]{2,1,0:T(8,128)(2,1)} async-done(((bf16[128,16,128]{2,1,0:T(8,128)(2,1)}), bf16[128,16,128]{2,1,0:T(8,128)(2,1)}) %all-reduce.7.cloned.1.call-update) | async-done | bytes 524304 | tf_op jit(solution)/shard_map/psum | solution.py:69
  702.9 1.8 convert_add_fusion
  704.7 137.9 %all-to-all-done.1 = f32[2,4,128,16,128]{4,0,3,1,2:T(2,128)} async-done(((f32[2,4,128,16,128]{4,0,3,1,2:T(2,128)}), f32[2,4,128,16,128]{4,0,3,1,2:T(2,128)}, u32[]{:S(2)}, u32[]{:S(2)}) %all-to-all-start.1) | async-done | bytes 8388640 | tf_op jit(solution)/shard_map/all_to_all | solution.py:62
  842.6 4.1 copy.48
  846.7 1.3 copy.49
  848.0 15.2 %fusion.6 = f32[4,16,128,2,128,1]{4,2,5,3,1,0:T(8,128)S(1)} fusion(f32[2,4,16,128,128,1]{4,3,2,1,0,5:T(8,128)S(1)} %bitcast.247, f32[1,2,128,128]{3,2,1,0:T(8,128)S(1)} %get-tuple-element.14, f32[1,2,128,128]{3,2,1,0:T(8,128)S(1)} %get-tuple-element.7), kind=kOutput, calls=%fused_computation.8 | convolution fusion | flops 6442516480 | bytes 17039360 | tf_op jit(solution)/shard_map/pqkb,qnabc->pnakc/dot_general | solution.py:25
  863.3 14.9 %fusion.23 = f32[2,4,16,128,128]{4,3,0,2,1:T(8,128)S(1)} fusion(f32[4,16,128,2,128,1]{4,2,5,3,1,0:T(8,128)S(1)} %fusion.6, f32[1,2,128,128]{3,2,1,0:T(8,128)S(1)} %get-tuple-element.14, f32[1,2,128,128]{3,2,1,0:T(8,128)S(1)} %get-tuple-element.7), kind=kOutput, calls=%fused_computation.21 | convolution fusion | flops 6442516480 | bytes 17039360 | tf_op jit(solution)/shard_map/pqkc,qnabc->pnabk/dot_general | solution.py:25
  878.2 3.8 copy.52
  882.0 8.0 reshape.116
  890.1 6.3 gather_fusion
  896.4 1.8 all_gather.14
  899.3 0.5 fusion.67
  900.4 1.8 all_gather.15
  903.8 0.5 fusion.73
  904.3 1.8 all_gather.13
  906.3 19.5 %all-reduce.1 = (f32[8]{0:T(128)S(1)}, f32[8]{0:T(128)S(1)}) all-reduce(f32[8]{0:T(128)S(1)} %get-tuple-element.4, f32[8]{0:T(128)S(1)} %get-tuple-element.3), channel_id=1, replica_groups=mesh['ens'=2,'pw'=8,'band'=2] {'pw'}, use_global_device_ids=true, to_apply=%region_2.3 | all-reduce | flops 16 | bytes 128 | tf_op jit(solution)/shard_map/psum | solution.py:90
  925.9 33.4 %psum.37 = bf16[2,1024,8]{1,2,0:T(8,128)(2,1)S(1)} all-reduce(f32[2,1024,8]{1,2,0:T(8,128)S(1)} %maximum_subtract_fusion), channel_id=1, replica_groups=mesh['ens'=2,'pw'=8,'band'=2] {'pw'}, use_global_device_ids=true, to_apply=%region_5.6 | all-reduce | flops 16384 | bytes 98304 | tf_op jit(solution)/shard_map/psum | solution.py:93
  960.6 3.5 all-reduce
  965.3 0.5 fusion.91
  966.3 0.6 pad_maximum_fusion.4
  967.1 0.6 pad_maximum_fusion.6
  967.7 66.3 %all-reduce.5.cloned.1.call-done = f32[2,1024,8]{1,2,0:T(8,128)} async-done(((f32[2,1024,8]{1,2,0:T(8,128)}), f32[2,1024,8]{1,2,0:T(8,128)}) %all-reduce.5.cloned.1.call-update) | async-done | bytes 65552 | tf_op jit(solution)/shard_map/psum | solution.py:90
  1034.0 1.5 copy.125
  (57 shorter events, 7.6 us)
Async XLA Ops:
  163.2 211.8 %copy-start.4 = (f32[1,128,128]{2,1,0:T(8,128)S(1)}, f32[1,128,128]{2,1,0:T(8,128)}, u32[]{:S(2)}) copy-start(f32[1,128,128]{2,1,0:T(8,128)} %get-tuple-element.24) | copy-start | bytes 196612
  163.2 211.8 %copy-start.5 = (f32[1,128,128]{2,1,0:T(8,128)S(1)}, f32[1,128,128]{2,1,0:T(8,128)}, u32[]{:S(2)}) copy-start(f32[1,128,128]{2,1,0:T(8,128)} %get-tuple-element.25) | copy-start | bytes 196612
  163.2 211.8 %copy-start.6 = (f32[1,128,128]{2,1,0:T(8,128)S(1)}, f32[1,128,128]{2,1,0:T(8,128)}, u32[]{:S(2)}) copy-start(f32[1,128,128]{2,1,0:T(8,128)} %fusion.135) | copy-start | bytes 196612
  413.7 7.5 copy-start.2
  413.7 190.5 %all-to-all-start = ((f32[2,4,16,128,128]{4,0,2,1,3:T(2,128)}), f32[2,4,16,128,128]{4,0,2,1,3:T(2,128)}, u32[]{:S(2)}, u32[]{:S(2)}) async-start(f32[2,4,16,128,128]{4,0,2,1,3:T(2,128)} %copy.42), calls=%async_computation | async-start | bytes 16777216 | tf_op jit(solution)/shard_map/all_to_all | solution.py:56
  629.6 3.2 copy-start.1
  655.4 187.2 %all-to-all-start.1 = ((f32[2,4,128,16,128]{4,0,3,1,2:T(2,128)}), f32[2,4,128,16,128]{4,0,3,1,2:T(2,128)}, u32[]{:S(2)}, u32[]{:S(2)}) async-start(f32[2,4,128,16,128]{4,0,3,1,2:T(2,128)} %copy.47), calls=%async_computation.1 | async-start | bytes 16777216 | tf_op jit(solution)/shard_map/all_to_all | solution.py:62
  660.4 42.5 %all-reduce.7.cloned.1.call-start = ((), (), s32[]{:S(2)}) async-start(), calls=%async_computation.3 | async-start | bytes 1048576 | tf_op jit(solution)/shard_map/psum | solution.py:69
  667.2 5.5 copy-start.9
  672.7 10.1 copy-start.7
  672.7 10.1 copy-start.10
  672.7 13.4 %copy-start.8 = (f32[768]{0:T(1024)S(1)}, f32[768]{0:T(1024)}, u32[]{:S(2)}) copy-start(f32[768]{0:T(1024)} %param.12) | copy-start | bytes 9220
  672.7 30.2 %copy-start.3 = (f32[64,16,128]{2,1,0:T(8,128)S(1)}, f32[64,16,128]{2,1,0:T(8,128)}, u32[]{:S(2)}) copy-start(f32[64,16,128]{2,1,0:T(8,128)} %param.10) | copy-start | bytes 1572868
  682.7 351.3 %all-reduce.5.cloned.1.call-start = ((), (), s32[]{:S(2)}) async-start(), calls=%async_computation.2 | async-start | bytes 131072 | tf_op jit(solution)/shard_map/psum | solution.py:90
  890.1 8.2 copy-start
Sparse Core Ops, SparseCore 0:
  682.8 20.0 all-reduce.6
Sparse Core Ops, SparseCore 1:
  967.1 66.9 all-reduce.4
where the time goes:
time: 1060 us; the launch traced here: 1040 us
  local copies, waits for them, and re-layouts  435 us (41%)
  waiting for transfers between devices  404 us (38%)
  matrix products  97.4 us (9%)
  blocking collectives  63.9 us (6%)
  between operations  16.8 us (2%)
  other arithmetic  14.2 us (1%)
  starting transfers between devices  12.6 us (1%)
    reshape x1, local copies, waits for them, and re-layouts, on_device(): filled = filled.reshape(2, blocks, slab_rows, width_second, width_third)  212 us
    all_to_all x1, waiting for transfers between devices, on_device(): lax.all_to_all(filled, 'pw', split_axis=3, concat_axis=2, tiled=True)  183 us
    all_to_all x1, waiting for transfers between devices, on_device(): lax.all_to_all(acted, 'pw', split_axis=2, concat_axis=3, tiled=True)  138 us
    broadcast_in_dim x1, local copies, waits for them, and re-layouts, on_device(): jnp.zeros((2, blocks, slab_rows * width_second * width_third), jnp.float32)  81.1 us
    dot_general x6, matrix products, transform(): return jnp.einsum(formula, table, fields, precision=HIGHEST)  80.8 us
    scatter x1, local copies, waits for them, and re-layouts, on_device(): filled = filled.at[:, :, wave_cells].set(trial_float)  70.4 us
    psum x1, waiting for transfers between devices, on_device(): lax.psum((correlation, numerator, denominator), 'pw')  66.3 us
    psum x1, blocking collectives, on_device(): coefficients = lax.psum(local_terms, 'pw')  33.4 us
  transfers between devices with their start and end apart: 4, of which 4 were waited for; matrix products, arithmetic and copies ran while one was open for 2% of the time, Pallas kernels for 0%

commit v1 on v0

--- a/solution.py
+++ b/solution.py
@@ -1,12 +1,389 @@
+import functools
 import math
 
 import jax
 import jax.numpy as jnp
+import numpy as np
 from jax import lax
+from jax.experimental import pallas as pl
+from jax.experimental.pallas import tpu as pltpu
 from jax.sharding import PartitionSpec as P
 
 EPSILON = 1e-06
 HIGHEST = lax.Precision.HIGHEST
+BF16 = jnp.bfloat16
+F32 = jnp.float32
+LANES = 128
+
+
+def split_pair(values):
+    high = values.astype(BF16)
+    low = (values - high.astype(np.float64)).astype(BF16)
+    return high, low
+
+
+def wave_tables(devices, rows, width_first, width_second, width_third):
+    half = rows // 2
+    second = np.arange(width_second)
+    steps = np.outer(2 * np.arange(half) + 1, second) % (2 * width_second)
+    angles = steps * (math.pi / width_second)
+    near = np.concatenate([np.cos(angles), np.sin(angles)])
+    blocks = []
+    for device in range(devices):
+        middle = 2 * rows * device + rows - 1
+        turns = (middle * second % (2 * width_second)) * (math.pi / width_second)
+        centre = np.stack([np.cos(turns), np.sin(turns)])
+        high, low = split_pair(centre)
+        blocks.append(np.concatenate([near.astype(BF16), high, low]))
+    second_table = np.stack(blocks)
+    missing = -second_table.shape[1] % 16
+    second_table = np.pad(second_table, ((0, 0), (0, missing), (0, 0)))
+    third = np.arange(width_third)
+    angles = (np.outer(third, third) % width_third) * (2 * math.pi / width_third)
+    factor = 1.0 / math.sqrt(width_second * width_third)
+    values = np.concatenate([np.cos(angles), np.sin(angles)]) * factor
+    third_table = np.concatenate(split_pair(values), axis=1)
+    first = np.arange(width_first)
+    angles = (np.outer(first, first) % width_first) * (2 * math.pi / width_first)
+    cosines = np.cos(angles) / math.sqrt(width_first)
+    sines = np.sin(angles) / math.sqrt(width_first)
+    back = np.block([[cosines, -sines], [sines, cosines]]).astype(BF16)
+    fore = np.block([[cosines, sines], [-sines, cosines]]).astype(BF16)
+    return second_table, third_table, back, fore
+
+
+def grid_kernel(
+    bands,
+    waves_ref,
+    second_ref,
+    third_ref,
+    back_ref,
+    fore_ref,
+    potential_ref,
+    rest_ref,
+    kinetic_ref,
+    occupation_ref,
+    sent_ref,
+    own_ref,
+    other_ref,
+    phase_s,
+    select_s,
+    centre_s,
+    coef_s,
+    slab_s,
+    acted_s,
+    density_s,
+    energy_s,
+    square_s,
+):
+    devices, _, count = waves_ref.shape
+    width_first, rows, width_third = potential_ref.shape
+    slab = width_first // devices
+    half = rows // 2
+    wide = bands * width_third
+    me = lax.axis_index("pw")
+    side = lax.axis_index("band")
+    nt = (((1,), (1,)), ((), ()))
+    tn = (((0,), (0,)), ((), ()))
+    near = second_ref[me]
+    square_s[...] = jnp.zeros_like(square_s)
+    energy_s[...] = jnp.zeros_like(energy_s)
+
+    def spread(p, carry):
+        waves = waves_ref[p].astype(F32)
+        place = waves[2 * bands : 2 * bands + 8].astype(jnp.int32)
+        first, second, third = place[0:1], place[1:2], place[2:3]
+        line = lax.broadcasted_iota(jnp.int32, (LANES, count), 0)
+        pick = jnp.where(line == second, 1.0, 0.0).astype(BF16)
+        turn = jnp.dot(near, pick, preferred_element_type=F32)
+        pick = jnp.where(line == third, 1.0, 0.0).astype(BF16)
+        phase = jnp.dot(third_ref[...], jnp.concatenate([pick, pick]), preferred_element_type=F32)
+        phase_s[p] = phase
+        centre = turn[rows : rows + 2] + turn[rows + 2 : rows + 4]
+        centre_s[p] = centre
+        real, imag = waves[:bands], waves[bands : 2 * bands]
+        square_s[...] += real * real + imag * imag
+        turned_real = real * centre[0:1] - imag * centre[1:2]
+        turned_imag = real * centre[1:2] + imag * centre[0:1]
+        inside = lax.broadcasted_iota(jnp.int32, (slab, count), 0) == first
+        for k in range(rows):
+            select_s[p, k * slab : (k + 1) * slab, :] = jnp.where(
+                inside, turn[k : k + 1], 0.0
+            ).astype(BF16)
+        cosines, sines = phase[:width_third], phase[width_third:]
+        for n in range(bands):
+            a, b = turned_real[n : n + 1], turned_imag[n : n + 1]
+            at = n * width_third
+            coef_s[at : at + width_third, :] = (a * cosines - b * sines).astype(BF16)
+            coef_s[wide + at : wide + at + width_third, :] = (a * sines + b * cosines).astype(BF16)
+        planes = lax.dot_general(select_s[p], coef_s[...], nt, preferred_element_type=F32)
+        for k in range(half):
+            even = planes[k * slab : (k + 1) * slab]
+            odd = planes[(half + k) * slab : (half + k + 1) * slab]
+            even_real, even_imag = even[:, :wide], even[:, wide:]
+            odd_real, odd_imag = odd[:, :wide], odd[:, wide:]
+            real_rows = pl.ds(pl.multiple_of(p * slab, slab), slab)
+            imag_rows = pl.ds(pl.multiple_of(width_first + p * slab, slab), slab)
+            slab_s[half + k, real_rows, :] = (even_real - odd_imag).astype(BF16)
+            slab_s[half + k, imag_rows, :] = (even_imag + odd_real).astype(BF16)
+            slab_s[half - 1 - k, real_rows, :] = (even_real + odd_imag).astype(BF16)
+            slab_s[half - 1 - k, imag_rows, :] = (even_imag - odd_real).astype(BF16)
+        return carry
+
+    lax.fori_loop(0, devices, spread, 0)
+
+    weights = [occupation_ref[n].astype(F32) for n in range(bands)]
+
+    def one_row(row):
+        spatial = jnp.dot(back_ref[...], slab_s[row], preferred_element_type=F32)
+        local = potential_ref[:, row, :]
+        density = jnp.zeros((width_first, width_third), F32)
+        moved_real, moved_imag = [], []
+        for n in range(bands):
+            real = spatial[:width_first, n * width_third : (n + 1) * width_third]
+            imag = spatial[width_first:, n * width_third : (n + 1) * width_third]
+            power = real * real + imag * imag
+            density = density + weights[n] * power
+            energy = (power * local).reshape(width_first // 8, 8, width_third)
+            energy_s[n] += jnp.sum(energy, axis=0)
+            moved_real.append((real * local).astype(BF16))
+            moved_imag.append((imag * local).astype(BF16))
+        density_s[:, row, :] = density
+        moved = jnp.concatenate(
+            [jnp.concatenate(moved_real, axis=1), jnp.concatenate(moved_imag, axis=1)]
+        )
+        return jnp.dot(fore_ref[...], moved, preferred_element_type=F32)
+
+    def pair(k, carry):
+        plus = one_row(half + k)
+        minus = one_row(half - 1 - k)
+        total = (plus + minus).astype(BF16)
+        gap = plus - minus
+        gap_real = gap[width_first:].astype(BF16)
+        gap_imag = (-gap[:width_first]).astype(BF16)
+        for p in range(devices):
+            even_rows = pl.ds(pl.multiple_of(k * slab, slab), slab)
+            odd_rows = pl.ds(pl.multiple_of((half + k) * slab, slab), slab)
+            mine = slice(p * slab, (p + 1) * slab)
+            acted_s[p, even_rows, :wide] = total[mine]
+            acted_s[p, even_rows, wide:] = total[width_first + p * slab : width_first + (p + 1) * slab]
+            acted_s[p, odd_rows, :wide] = gap_real[mine]
+            acted_s[p, odd_rows, wide:] = gap_imag[mine]
+        return carry
+
+    lax.fori_loop(0, half, pair, 0)
+
+    share = width_first // 2
+    own_ref[...] = density_s[pl.ds(side * share, share)] + rest_ref[...]
+    other_ref[...] = density_s[pl.ds((1 - side) * share, share)].astype(BF16)
+
+    waves = waves_ref[me].astype(F32)
+    real, imag = waves[:bands], waves[bands : 2 * bands]
+    moving = jnp.sum((real * real + imag * imag) * kinetic_ref[...], axis=1, keepdims=True)
+    energy = jnp.concatenate(
+        [jnp.sum(energy_s[n], axis=(0, 1), keepdims=True) for n in range(bands)]
+    )
+    numerator = moving + energy
+    denominator = jnp.sum(square_s[...], axis=1, keepdims=True) * (1.0 / devices)
+    scalars = []
+    for value in (numerator, denominator):
+        high = value.astype(BF16)
+        low = (value - high.astype(F32)).astype(BF16)
+        both = jnp.concatenate([high.astype(F32), low.astype(F32)])
+        scalars.append(jnp.broadcast_to(both, (2 * bands, LANES)))
+    scalars = jnp.concatenate(scalars, axis=1).astype(BF16)
+
+    def collect(p, carry):
+        found = lax.dot_general(acted_s[p], select_s[p], tn, preferred_element_type=F32)
+        cosines, sines = phase_s[p, :width_third], phase_s[p, width_third:]
+        reals, imags = [], []
+        for n in range(bands):
+            at = n * width_third
+            real = found[at : at + width_third]
+            imag = found[wide + at : wide + at + width_third]
+            reals.append(jnp.sum(real * cosines + imag * sines, axis=0, keepdims=True))
+            imags.append(jnp.sum(imag * cosines - real * sines, axis=0, keepdims=True))
+        real, imag = jnp.concatenate(reals), jnp.concatenate(imags)
+        centre = centre_s[p]
+        cosine, sine = centre[0:1], centre[1:2]
+        result = jnp.concatenate([real * cosine + imag * sine, imag * cosine - real * sine])
+        sent_ref[p, :, :count] = result.astype(BF16)
+        sent_ref[p, :, count:] = scalars
+        return carry
+
+    lax.fori_loop(0, devices, collect, 0)
+
+
+def on_grid(waves, potential, rest_density, kinetic, occupation, bands, width_second):
+    devices, _, count = waves.shape
+    width_first, rows, width_third = potential.shape
+    slab = width_first // devices
+    wide = bands * width_third
+    tables = wave_tables(devices, rows, width_first, width_second, width_third)
+    vmem = pl.BlockSpec(memory_space=pltpu.VMEM)
+    smem = pl.BlockSpec(memory_space=pltpu.SMEM)
+    return pl.pallas_call(
+        functools.partial(grid_kernel, bands),
+        out_shape=(
+            jax.ShapeDtypeStruct((devices, 2 * bands, count + 2 * LANES), BF16),
+            jax.ShapeDtypeStruct(rest_density.shape, F32),
+            jax.ShapeDtypeStruct(rest_density.shape, BF16),
+        ),
+        in_specs=[vmem] * 8 + [smem],
+        out_specs=(vmem, vmem, vmem),
+        scratch_shapes=[
+            pltpu.VMEM((devices, 2 * width_third, count), F32),
+            pltpu.VMEM((devices, rows * slab, count), BF16),
+            pltpu.VMEM((devices, 2, count), F32),
+            pltpu.VMEM((2 * wide, count), BF16),
+            pltpu.VMEM((rows, 2 * width_first, wide), BF16),
+            pltpu.VMEM((devices, rows * slab, 2 * wide), BF16),
+            pltpu.VMEM((width_first, rows, width_third), F32),
+            pltpu.VMEM((bands, 8, width_third), F32),
+            pltpu.VMEM((bands, count), F32),
+        ],
+        compiler_params=pltpu.CompilerParams(vmem_limit_bytes=56 * 1024 * 1024),
+    )(waves, *[jnp.asarray(t) for t in tables], potential, rest_density, kinetic[None], occupation)
+
+
+def inner_kernel(bands, mine_ref, theirs_ref, trial_ref, partner_ref, kinetic_ref, all_ref, sent_ref, rest_ref):
+    count = kinetic_ref.shape[1]
+    first = lax.axis_index("band") == 0
+    nt = (((1,), (1,)), ((), ()))
+
+    def order(one, two):
+        return jnp.concatenate([jnp.where(first, one, two), jnp.where(first, two, one)])
+
+    kinetic = kinetic_ref[...]
+    damping = 1.0 / (1.0 + kinetic)
+    mine, theirs = mine_ref[...], theirs_ref[...]
+    pairs = order(mine[:bands] + 0.0, theirs[:bands]), order(mine[bands:], theirs[bands:])
+    sums = (pairs[0] + pairs[1])[:, count:]
+    ratio = sums[:, 0:1] / (sums[:, LANES : LANES + 1] + EPSILON)
+    halves, dampeds, softs = [], [], []
+    for part in range(2):
+        trial = order(trial_ref[part].astype(F32), partner_ref[part].astype(F32))
+        action = kinetic * trial + pairs[part][:, :count]
+        halves.append(action.astype(BF16))
+        dampeds.append((action * damping).astype(BF16))
+        softs.append((trial * damping).astype(BF16))
+    rows = jnp.concatenate(halves + dampeds + softs)
+    one = lax.dot_general(rows, all_ref[0], nt, preferred_element_type=F32)
+    two = lax.dot_general(rows, all_ref[1], nt, preferred_element_type=F32)
+    block = 2 * bands
+
+    def inner(at):
+        real = one[at : at + block] + two[at + block : at + 2 * block]
+        imag = one[at + block : at + 2 * block] - two[at : at + block]
+        return real, imag
+
+    correlation = inner(0)
+    damped = inner(2 * block)
+    soft = inner(4 * block)
+    coefficients = [d - ratio * s for d, s in zip(damped, soft)]
+    sent_ref[...] = jnp.concatenate([*correlation, *coefficients]).astype(BF16)
+    own_ratio = jnp.where(first, ratio[:bands], ratio[bands:])
+    for part in range(2):
+        d, s = dampeds[part].astype(F32), softs[part].astype(F32)
+        d = jnp.where(first, d[:bands], d[bands:])
+        s = jnp.where(first, s[:bands], s[bands:])
+        rest_ref[part * bands : (part + 1) * bands] = d - own_ratio * s
+
+
+def project_kernel(bands, sums_ref, arrived_ref, all_ref, rest_ref, correlation_ref, own_ref, sent_ref):
+    block = 2 * bands
+    first = lax.axis_index("band") == 0
+    total = sums_ref[...].astype(F32) + arrived_ref[...].astype(F32)
+    correlation_ref[...] = total[: 2 * block]
+    coefficients = total[2 * block :].astype(BF16)
+    one = jnp.dot(coefficients, all_ref[0], preferred_element_type=F32)
+    two = jnp.dot(coefficients, all_ref[1], preferred_element_type=F32)
+    real = one[:block] - two[block:]
+    imag = one[block:] + two[:block]
+    for part, value in enumerate((real, imag)):
+        low, high = value[:bands], value[bands:]
+        rows = slice(part * bands, (part + 1) * bands)
+        own_ref[rows] = rest_ref[rows] - jnp.where(first, low, high)
+        sent_ref[rows] = jnp.where(first, high, low)
+
+
+def swap(values, axis, bit):
+    size = lax.axis_size(axis)
+    return lax.ppermute(values, axis, [(i, i ^ bit) for i in range(size)])
+
+
+def in_waves(trial_block, all_bands, potential, rest_density, wave_cells, kinetic, occupation):
+    devices = lax.axis_size("pw")
+    _, rows, width_third = potential.shape
+    width_second = rows * devices
+    _, bands, count = trial_block.shape
+    partner = swap(trial_block, "band", 1)
+    first = wave_cells // (width_second * width_third)
+    second = wave_cells // width_third % width_second
+    third = wave_cells % width_third
+    place = jnp.stack([first, second, third]).astype(BF16)
+    packet = jnp.concatenate([trial_block.reshape(2 * bands, count), place])
+    packet = jnp.pad(packet, ((0, -packet.shape[0] % 16), (0, 0)))
+    packets = jnp.broadcast_to(packet[None], (devices, *packet.shape))
+    waves = lax.all_to_all(packets, "pw", split_axis=0, concat_axis=0, tiled=True)
+    partial, density_own, density_other = on_grid(
+        waves, potential, rest_density, kinetic, occupation, bands, width_second
+    )
+    arrived = lax.all_to_all(partial, "pw", split_axis=0, concat_axis=0, tiled=True)
+    mine = jnp.sum(arrived.astype(F32), axis=0)
+    theirs = swap(mine, "band", 1)
+    density = density_own + swap(density_other, "band", 1).astype(F32)
+    vmem = pl.BlockSpec(memory_space=pltpu.VMEM)
+    states = all_bands.shape[1]
+    block = 2 * bands
+    params = pltpu.CompilerParams(vmem_limit_bytes=32 * 1024 * 1024)
+    sums, rest = pl.pallas_call(
+        functools.partial(inner_kernel, bands),
+        out_shape=(
+            jax.ShapeDtypeStruct((4 * block, states), BF16),
+            jax.ShapeDtypeStruct((block, count), F32),
+        ),
+        in_specs=[vmem] * 6,
+        out_specs=(vmem, vmem),
+        compiler_params=params,
+    )(mine, theirs, trial_block, partner, kinetic[None], all_bands)
+    bit = 1
+    while 2 * bit < devices:
+        sums = sums + swap(sums, "pw", bit)
+        bit *= 2
+    correlation, own, sent = pl.pallas_call(
+        functools.partial(project_kernel, bands),
+        out_shape=(
+            jax.ShapeDtypeStruct((2 * block, states), F32),
+            jax.ShapeDtypeStruct((block, count), F32),
+            jax.ShapeDtypeStruct((block, count), F32),
+        ),
+        in_specs=[vmem] * 4,
+        out_specs=(vmem, vmem, vmem),
+        compiler_params=params,
+    )(sums, swap(sums, "pw", bit), all_bands, rest)
+    correction = (own - swap(sent, "band", 1)).reshape(2, bands, count)
+    correlation = correlation.reshape(2, block, states).transpose(0, 2, 1)
+    return (correction, correlation, density)
+
+
+def fits(trial_block, potential, mesh):
+    devices = mesh.shape["pw"]
+    width_first, width_second, width_third = potential.shape[0] // mesh.shape["ens"], *potential.shape[1:]
+    slab, rows = width_first // devices, width_second // devices
+    bands = trial_block.shape[1] // mesh.shape["band"]
+    return (
+        mesh.shape["band"] == 2
+        and devices >= 2
+        and devices & (devices - 1) == 0
+        and slab % 16 == 0
+        and rows % 16 == 0
+        and width_first % LANES == 0
+        and width_second == LANES
+        and width_third == LANES
+        and bands == 4
+        and trial_block.shape[2] // devices % LANES == 0
+    )
 
 
 def tables(length):
@@ -140,10 +517,12 @@
         P("pw"),
         P(("ens", "band")),
     )
-    return jax.shard_map(
-        on_device,
-        mesh=mesh,
-        in_specs=placed,
-        out_specs=(P("ens", "band", "pw"), P("ens", "band", None), P(("ens", "band"), "pw", None)),
-        check_vma=False,
-    )
+    results = (P("ens", "band", "pw"), P("ens", "band", None), P(("ens", "band"), "pw", None))
+
+    def program(*arguments):
+        body = in_waves if fits(arguments[0], arguments[2], mesh) else on_device
+        return jax.shard_map(
+            body, mesh=mesh, in_specs=placed, out_specs=results, check_vma=False
+        )(*arguments)
+
+    return program

time: 1060 us -> 73.8 us (0.07); the launches traced: 1040 us -> 73.3 us
  local copies, waits for them, and re-layouts: 435 us -> 4.74 us
  waiting for transfers between devices: 404 us -> 28.4 us
  matrix products: 97.4 us -> 0 us
  blocking collectives: 63.9 us -> 0 us
  Pallas kernels: 0 us -> 25.6 us
  between operations: 16.8 us -> 0.75 us
  other arithmetic: 14.2 us -> 1.79 us
    all_to_all x2, waiting for transfers between devices: 320 us -> 13.9 us  [the longest x1 7.2 us: in_waves(): lax.all_to_all(partial, 'pw', split_axis=0, concat_axis=0, tiled=True)]
    reshape x2, local copies, waits for them, and re-layouts: 220 us -> 1.4 us  [the longest x1 0.78 us: in_waves(): packet = jnp.concatenate([trial_block.reshape(2 * bands, count), place])]
    dot_general x23 -> x0, matrix products: 97.4 us -> none  [the longest x6 80.8 us: transform(): return jnp.einsum(formula, table, fields, precision=HIGHEST)]
    psum x2 -> x0, waiting for transfers between devices: 83.1 us -> none  [the longest x1 66.3 us: on_device(): lax.psum((correlation, numerator, denominator), 'pw')]
    broadcast_in_dim x1 -> x2, local copies, waits for them, and re-layouts: 81.1 us -> 1.96 us  [the longest x1 1.27 us: on_grid(): kinetic[None]]
    scatter x1 -> x0, local copies, waits for them, and re-layouts: 70.4 us -> none  [on_device(): filled = filled.at[:, :, wave_cells].set(trial_float)]
    psum x2 -> x0, blocking collectives: 52.9 us -> none  [the longest x1 33.4 us: on_device(): coefficients = lax.psum(local_terms, 'pw')]
    transpose x3 -> x0, local copies, waits for them, and re-layouts: 30.3 us -> none  [transform(): return jnp.einsum(formula, table, fields, precision=HIGHEST)]
  transfers between devices with their start and end apart: 4 -> 9, of which waited for: 4 -> 7; matrix products, arithmetic and copies ran while one was open for 2% -> 3% of each run, Pallas kernels for 0% -> 3%
where the time goes in v1:
time: 73.8 us; the launch traced here: 73.3 us
  waiting for transfers between devices  28.4 us (38%)
  Pallas kernels  25.6 us (35%)
  starting transfers between devices  12.1 us (16%)
  local copies, waits for them, and re-layouts  4.74 us (6%)
  other arithmetic  1.79 us (2%)
  between operations  0.75 us (1%)
    pallas_call x1, Pallas kernels, on_grid(): pl.pallas_call(functools.partial(grid_kernel, bands), out_shape=(jax.Shap...  23.5 us
    ppermute x7, waiting for transfers between devices, swap(): return lax.ppermute(values, axis, [(i, i ^ bit) for i in range(size)])  14.5 us
    all_to_all x1, starting transfers between devices, in_waves(): lax.all_to_all(packets, 'pw', split_axis=0, concat_axis=0, tiled=True)  7.25 us
    all_to_all x1, waiting for transfers between devices, in_waves(): lax.all_to_all(partial, 'pw', split_axis=0, concat_axis=0, tiled=True)  7.2 us
    all_to_all x1, waiting for transfers between devices, in_waves(): lax.all_to_all(packets, 'pw', split_axis=0, concat_axis=0, tiled=True)  6.69 us
    all_to_all x1, starting transfers between devices, in_waves(): lax.all_to_all(partial, 'pw', split_axis=0, concat_axis=0, tiled=True)  3.37 us
  transfers between devices with their start and end apart: 9, of which 7 were waited for; matrix products, arithmetic and copies ran while one was open for 3% of the time, Pallas kernels for 3%

profile of v1, /device:TPU:0, one launch (start us, length us, event | category | flops | bytes accessed | tf_op | source)
XLA Modules:
  0.0 73.3 jit_solution(11291046206815253045)
XLA Ops:
  0.6 0.0 copy-start.1
  0.6 0.0 copy-start
  0.7 0.9 %fusion.8 = (bf16[768]{0:T(1024)(128)(2,1)S(1)}, bf16[768]{0:T(1024)(128)(2,1)S(1)}, bf16[768]{0:T(1024)(128)(2,1)S(1)}) fusion(s32[768]{0:T(1024)} %param.15), kind=kLoop, calls=%fused_computation.22 | loop fusion | flops 33024 | bytes 7680 | tf_op jit(solution)/shard_map/convert.5 | solution.py:524
  1.5 0.8 %reshape.16 = bf16[8,768]{1,0:T(8,128)(2,1)S(1)} reshape(bf16[2,4,768]{2,1,0:T(4,128)(2,1)} %trial_ref.1) | data formatting | bytes 24576 | tf_op jit(solution)/shard_map/reshape | solution.py:325
  2.4 0.7 broadcast_in_dim.4
  3.0 7.3 %all-to-all-start = ((bf16[8,16,768]{2,1,0:T(8,128)(2,1)}), bf16[8,16,768]{2,1,0:T(8,128)(2,1)S(1)}, u32[]{:S(2)}, u32[]{:S(2)}) async-start(bf16[8,16,768]{2,1,0:T(8,128)(2,1)} %broadcast_in_dim.4), calls=%async_computation | async-start | bytes 393216 | tf_op jit(solution)/shard_map/all_to_all | solution.py:328
  10.3 1.3 %broadcast_in_dim.5.kinetic_ref = f32[1,768]{1,0:T(1,128)} reshape(f32[768]{0:T(1024)} %param.16) | data formatting | bytes 6144 | tf_op jit(solution)/shard_map/broadcast_in_dim | solution.py:246
  11.6 6.7 %all-to-all-done.waves_ref = bf16[8,16,768]{2,1,0:T(8,128)(2,1)S(1)} async-done(((bf16[8,16,768]{2,1,0:T(8,128)(2,1)}), bf16[8,16,768]{2,1,0:T(8,128)(2,1)S(1)}, u32[]{:S(2)}, u32[]{:S(2)}) %all-to-all-start) | async-done | bytes 196640 | tf_op jit(solution)/shard_map/all_to_all | solution.py:328
  18.2 0.0 copy-start.3
  18.3 0.7 copy-done.3
  18.9 23.5 %shard_map.130 = (bf16[8,8,1024]{2,1,0:T(8,128)(2,1)}, f32[64,16,128]{2,1,0:T(8,128)}, bf16[64,16,128]{2,1,0:T(8,128)(2,1)}) custom-call(bf16[8,16,768]{2,1,0:T(8,128)(2,1)} %copy-done.3, bf16[8,32,128]{2,1,0:T(8,128)(2,1)} %constant.57.clone.second_ref, bf16[256,256]{1,0:T(8,128)(2,1)} %constant.58.clone.third_ref, ...), custom_call_target="tpu_custom_call" | custom-call | tf_op jit(solution)/shard_map/pallas_call | solution.py:225
  42.4 3.4 %all-to-all-start.1 = ((bf16[8,8,1024]{2,1,0:T(8,128)(2,1)}), bf16[8,8,1024]{2,1,0:T(8,128)(2,1)S(1)}, u32[]{:S(2)}, u32[]{:S(2)}) async-start(bf16[8,8,1024]{2,1,0:T(8,128)(2,1)} %get-tuple-element.11), calls=%async_computation.1 | async-start | bytes 262144 | tf_op jit(solution)/shard_map/all_to_all | solution.py:332
  45.8 0.1 collective-permute-start.6
  45.9 7.2 %all-to-all-done.1 = bf16[8,8,1024]{2,1,0:T(8,128)(2,1)S(1)} async-done(((bf16[8,8,1024]{2,1,0:T(8,128)(2,1)}), bf16[8,8,1024]{2,1,0:T(8,128)(2,1)S(1)}, u32[]{:S(2)}, u32[]{:S(2)}) %all-to-all-start.1) | async-done | bytes 131104 | tf_op jit(solution)/shard_map/all_to_all | solution.py:332
  53.1 0.1 collective-permute-start
  53.2 0.0 copy-done.1
  53.2 0.5 collective-permute-start.1
  53.7 0.8 %collective-permute-done.1.partner_ref = bf16[2,4,768]{2,1,0:T(4,128)(2,1)S(1)} collective-permute-done((bf16[2,4,768]{2,1,0:T(4,128)(2,1)S(1)}, bf16[2,4,768]{2,1,0:T(4,128)(2,1)S(1)}, u32[]{:S(2)}, u32[]{:S(2)}) %collective-permute-start.1) | collective-permute-done | bytes 12320 | tf_op jit(solution)/shard_map/ppermute | solution.py:312
  54.5 0.0 collective-permute-done.theirs_ref
  54.5 0.0 copy-done
  54.5 0.0 copy-start.2
  54.5 0.7 copy-done.2
  55.2 0.0 copy-start.4
  55.2 1.0 %shard_map.131 = (bf16[32,1024]{1,0:T(8,128)(2,1)S(1)}, f32[8,768]{1,0:T(8,128)S(1)}) custom-call(f32[8,1024]{1,0:T(8,128)S(1)} %convert_reduce_fusion.mine_ref, f32[8,1024]{1,0:T(8,128)S(1)} %collective-permute-done.theirs_ref, bf16[2,4,768]{2,1,0:T(4,128)(2,1)S(1)} %copy-done.1, bf16[2,4,768]{2,1,0:T(4,128)(2,1)S(1)} %collective-permute-done.1.partner_ref, ...), custom_call_target="tpu_custom_call" | custom-call | tf_op jit(solution)/shard_map/pallas_call | solution.py:340
  56.3 0.3 collective-permute-start.2
  56.6 4.1 %collective-permute-done.2 = bf16[32,1024]{1,0:T(8,128)(2,1)S(1)} collective-permute-done((bf16[32,1024]{1,0:T(8,128)(2,1)S(1)}, bf16[32,1024]{1,0:T(8,128)(2,1)S(1)}, u32[]{:S(2)}, u32[]{:S(2)}) %collective-permute-start.2) | collective-permute-done | bytes 65568 | tf_op jit(solution)/shard_map/ppermute | solution.py:312
  60.7 0.1 collective-permute-start.3
  60.8 4.3 %collective-permute-done.3 = bf16[32,1024]{1,0:T(8,128)(2,1)S(1)} collective-permute-done((bf16[32,1024]{1,0:T(8,128)(2,1)S(1)}, bf16[32,1024]{1,0:T(8,128)(2,1)S(1)}, u32[]{:S(2)}, u32[]{:S(2)}) %collective-permute-start.3) | collective-permute-done | bytes 65568 | tf_op jit(solution)/shard_map/ppermute | solution.py:312
  65.1 0.5 collective-permute-start.4
  65.5 4.9 %collective-permute-done.4.arrived_ref = bf16[32,1024]{1,0:T(8,128)(2,1)S(1)} collective-permute-done((bf16[32,1024]{1,0:T(8,128)(2,1)S(1)}, bf16[32,1024]{1,0:T(8,128)(2,1)S(1)}, u32[]{:S(2)}, u32[]{:S(2)}) %collective-permute-start.4) | collective-permute-done | bytes 65568 | tf_op jit(solution)/shard_map/ppermute | solution.py:312
  70.4 1.0 %shard_map.132 = (f32[16,1024]{1,0:T(8,128)}, f32[8,768]{1,0:T(8,128)S(1)}, f32[8,768]{1,0:T(8,128)S(1)}) custom-call(bf16[32,1024]{1,0:T(8,128)(2,1)S(1)} %add.26.sums_ref, bf16[32,1024]{1,0:T(8,128)(2,1)S(1)} %collective-permute-done.4.arrived_ref, bf16[2,1024,768]{2,1,0:T(8,128)(2,1)S(1)} %copy-done, f32[8,768]{1,0:T(8,128)S(1)} %get-tuple-element.13.rest_ref), custom_call_target="tpu_custom_call" | custom-call | tf_op jit(solution)/shard_map/pallas_call | solution.py:354
  71.5 0.0 collective-permute-start.5
  71.5 0.0 collective-permute-done.6
  71.5 0.0 copy-done.4
  71.5 0.8 %convert_add_fusion = f32[64,16,128]{2,1,0:T(8,128)} fusion(f32[64,16,128]{2,1,0:T(8,128)S(1)} %copy-done.4, bf16[64,16,128]{2,1,0:T(8,128)(2,1)S(1)} %collective-permute-done.6), kind=kLoop, calls=%fused_computation | loop fusion | flops 262144 | bytes 1310720 | tf_op jit(solution)/shard_map/add | solution.py:335
  72.4 0.3 collective-permute-done.5
  72.7 0.6 reshape.17
  (8 shorter events, 0.1 us)
Async XLA Ops:
  0.6 52.6 %copy-start.1 = (bf16[2,4,768]{2,1,0:T(4,128)(2,1)S(1)}, bf16[2,4,768]{2,1,0:T(4,128)(2,1)}, u32[]{:S(2)}) copy-start(bf16[2,4,768]{2,1,0:T(4,128)(2,1)} %trial_ref.1) | copy-start | bytes 36868
  0.6 53.9 %copy-start = (bf16[2,1024,768]{2,1,0:T(8,128)(2,1)S(1)}, bf16[2,1024,768]{2,1,0:T(8,128)(2,1)}, u32[]{:S(2)}) copy-start(bf16[2,1024,768]{2,1,0:T(8,128)(2,1)} %all_ref.3) | copy-start | bytes 9437188
  3.0 15.2 %all-to-all-start = ((bf16[8,16,768]{2,1,0:T(8,128)(2,1)}), bf16[8,16,768]{2,1,0:T(8,128)(2,1)S(1)}, u32[]{:S(2)}, u32[]{:S(2)}) async-start(bf16[8,16,768]{2,1,0:T(8,128)(2,1)} %broadcast_in_dim.4), calls=%async_computation | async-start | bytes 393216 | tf_op jit(solution)/shard_map/all_to_all | solution.py:328
  18.2 0.7 copy-start.3
  42.4 10.7 %all-to-all-start.1 = ((bf16[8,8,1024]{2,1,0:T(8,128)(2,1)}), bf16[8,8,1024]{2,1,0:T(8,128)(2,1)S(1)}, u32[]{:S(2)}, u32[]{:S(2)}) async-start(bf16[8,8,1024]{2,1,0:T(8,128)(2,1)} %get-tuple-element.11), calls=%async_computation.1 | async-start | bytes 262144 | tf_op jit(solution)/shard_map/all_to_all | solution.py:332
  45.8 25.7 %collective-permute-start.6 = (bf16[64,16,128]{2,1,0:T(8,128)(2,1)}, bf16[64,16,128]{2,1,0:T(8,128)(2,1)S(1)}, u32[]{:S(2)}, u32[]{:S(2)}) collective-permute-start(bf16[64,16,128]{2,1,0:T(8,128)(2,1)} %get-tuple-element.18), channel_id=1, source_target_pairs={{0,1},{1,0},{2,3},{3,2},{4,5},{5,4},{6,7},{7,6},{8,9},{9,8},{10,11... | collective-permute-start | bytes 786440 | tf_op jit(solution)/shard_map/ppermute | solution.py:312
  53.1 1.4 %collective-permute-start = (f32[8,1024]{1,0:T(8,128)S(1)}, f32[8,1024]{1,0:T(8,128)S(1)}, u32[]{:S(2)}, u32[]{:S(2)}) collective-permute-start(f32[8,1024]{1,0:T(8,128)S(1)} %convert_reduce_fusion.mine_ref), channel_id=1, source_target_pairs={{0,1},{1,0},{2,3},{3,2},{4,5},{5,4},{6,7},{7,6},{8,9},{9,8},{10,11... | collective-permute-start | bytes 98312 | tf_op jit(solution)/shard_map/ppermute | solution.py:312
  53.2 1.3 %collective-permute-start.1 = (bf16[2,4,768]{2,1,0:T(4,128)(2,1)S(1)}, bf16[2,4,768]{2,1,0:T(4,128)(2,1)S(1)}, u32[]{:S(2)}, u32[]{:S(2)}) collective-permute-start(bf16[2,4,768]{2,1,0:T(4,128)(2,1)S(1)} %copy-done.1), channel_id=1, source_target_pairs={{0,1},{1,0},{2,3},{3,2},{4,5},{5,4},{6,7},{7,6},{8,9},{9,8},{10,11... | collective-permute-start | bytes 36872 | tf_op jit(solution)/shard_map/ppermute | solution.py:312
  54.5 0.7 copy-start.2
  55.2 16.3 %copy-start.4 = (f32[64,16,128]{2,1,0:T(8,128)S(1)}, f32[64,16,128]{2,1,0:T(8,128)}, u32[]{:S(2)}) copy-start(f32[64,16,128]{2,1,0:T(8,128)} %get-tuple-element.17) | copy-start | bytes 1572868
  56.3 4.4 %collective-permute-start.2 = (bf16[32,1024]{1,0:T(8,128)(2,1)S(1)}, bf16[32,1024]{1,0:T(8,128)(2,1)S(1)}, u32[]{:S(2)}, u32[]{:S(2)}) collective-permute-start(bf16[32,1024]{1,0:T(8,128)(2,1)S(1)} %get-tuple-element.12), channel_id=1, source_target_pairs={{0,2},{2,0},{4,6},{6,4},{8,10},{10,8},{12,14},{14,12},{1,3},{3,1},... | collective-permute-start | bytes 196616 | tf_op jit(solution)/shard_map/ppermute | solution.py:312
  60.7 4.3 %collective-permute-start.3 = (bf16[32,1024]{1,0:T(8,128)(2,1)S(1)}, bf16[32,1024]{1,0:T(8,128)(2,1)S(1)}, u32[]{:S(2)}, u32[]{:S(2)}) collective-permute-start(bf16[32,1024]{1,0:T(8,128)(2,1)S(1)} %add.25), channel_id=1, source_target_pairs={{0,4},{2,6},{4,0},{6,2},{8,12},{10,14},{12,8},{14,10},{1,5},{3,7},... | collective-permute-start | bytes 196616 | tf_op jit(solution)/shard_map/ppermute | solution.py:312
  65.1 5.4 %collective-permute-start.4 = (bf16[32,1024]{1,0:T(8,128)(2,1)S(1)}, bf16[32,1024]{1,0:T(8,128)(2,1)S(1)}, u32[]{:S(2)}, u32[]{:S(2)}) collective-permute-start(bf16[32,1024]{1,0:T(8,128)(2,1)S(1)} %add.26.sums_ref), channel_id=1, source_target_pairs={{0,8},{2,10},{4,12},{6,14},{8,0},{10,2},{12,4},{14,6},{1,9},{3,11}... | collective-permute-start | bytes 196616 | tf_op jit(solution)/shard_map/ppermute | solution.py:312
  71.5 1.2 %collective-permute-start.5 = (f32[8,768]{1,0:T(8,128)S(1)}, f32[8,768]{1,0:T(8,128)S(1)}, u32[]{:S(2)}, u32[]{:S(2)}) collective-permute-start(f32[8,768]{1,0:T(8,128)S(1)} %get-tuple-element.15), channel_id=1, source_target_pairs={{0,1},{1,0},{2,3},{3,2},{4,5},{5,4},{6,7},{7,6},{8,9},{9,8},{10,11... | collective-permute-start | bytes 73736 | tf_op jit(solution)/shard_map/ppermute | solution.py:312

commit v2 on v1

--- a/solution.py
+++ b/solution.py
@@ -52,6 +52,19 @@
     return second_table, third_table, back, fore
 
 
+def pack_kernel(bands, devices, width_second, width_third, trial_ref, cells_ref, packet_ref):
+    cells = cells_ref[...].reshape(1, cells_ref.shape[0])
+    first = lax.div(cells, width_second * width_third)
+    second = lax.rem(lax.div(cells, width_third), width_second)
+    third = lax.rem(cells, width_third)
+    unused = jnp.zeros((packet_ref.shape[1] - 2 * bands - 3, cells.shape[1]), jnp.int32)
+    place = jnp.concatenate([first, second, third, unused]).astype(F32)
+    trial = [trial_ref[part].astype(F32) for part in range(2)]
+    packet = jnp.concatenate([*trial, place]).astype(BF16)
+    for p in range(devices):
+        packet_ref[p] = packet
+
+
 def grid_kernel(
     bands,
     waves_ref,
@@ -60,36 +73,34 @@
     back_ref,
     fore_ref,
     potential_ref,
-    rest_ref,
     kinetic_ref,
     occupation_ref,
+    partner_ref,
     sent_ref,
     own_ref,
     other_ref,
     phase_s,
     select_s,
-    centre_s,
-    coef_s,
     slab_s,
     acted_s,
-    density_s,
-    energy_s,
-    square_s,
 ):
     devices, _, count = waves_ref.shape
-    width_first, rows, width_third = potential_ref.shape
+    rows, width_first, width_third = potential_ref.shape
     slab = width_first // devices
     half = rows // 2
-    wide = bands * width_third
+    share = width_first // 2
     me = lax.axis_index("pw")
-    side = lax.axis_index("band")
+    low_side = lax.axis_index("band") == 0
     nt = (((1,), (1,)), ((), ()))
     tn = (((0,), (0,)), ((), ()))
     near = second_ref[me]
-    square_s[...] = jnp.zeros_like(square_s)
-    energy_s[...] = jnp.zeros_like(energy_s)
-
-    def spread(p, carry):
+    weights = [occupation_ref[n].astype(F32) for n in range(bands)]
+    lanes = [slice(n * width_third, (n + 1) * width_third) for n in range(bands)]
+    square = jnp.zeros((bands, count), F32)
+    energies = [jnp.zeros((8, width_third), F32) for _ in range(bands)]
+    centres = []
+
+    for p in range(devices):
         waves = waves_ref[p].astype(F32)
         place = waves[2 * bands : 2 * bands + 8].astype(jnp.int32)
         first, second, third = place[0:1], place[1:2], place[2:3]
@@ -100,9 +111,9 @@
         phase = jnp.dot(third_ref[...], jnp.concatenate([pick, pick]), preferred_element_type=F32)
         phase_s[p] = phase
         centre = turn[rows : rows + 2] + turn[rows + 2 : rows + 4]
-        centre_s[p] = centre
+        centres.append(centre)
         real, imag = waves[:bands], waves[bands : 2 * bands]
-        square_s[...] += real * real + imag * imag
+        square = square + real * real + imag * imag
         turned_real = real * centre[0:1] - imag * centre[1:2]
         turned_imag = real * centre[1:2] + imag * centre[0:1]
         inside = lax.broadcasted_iota(jnp.int32, (slab, count), 0) == first
@@ -113,78 +124,77 @@
         cosines, sines = phase[:width_third], phase[width_third:]
         for n in range(bands):
             a, b = turned_real[n : n + 1], turned_imag[n : n + 1]
-            at = n * width_third
-            coef_s[at : at + width_third, :] = (a * cosines - b * sines).astype(BF16)
-            coef_s[wide + at : wide + at + width_third, :] = (a * sines + b * cosines).astype(BF16)
-        planes = lax.dot_general(select_s[p], coef_s[...], nt, preferred_element_type=F32)
-        for k in range(half):
-            even = planes[k * slab : (k + 1) * slab]
-            odd = planes[(half + k) * slab : (half + k + 1) * slab]
-            even_real, even_imag = even[:, :wide], even[:, wide:]
-            odd_real, odd_imag = odd[:, :wide], odd[:, wide:]
-            real_rows = pl.ds(pl.multiple_of(p * slab, slab), slab)
-            imag_rows = pl.ds(pl.multiple_of(width_first + p * slab, slab), slab)
-            slab_s[half + k, real_rows, :] = (even_real - odd_imag).astype(BF16)
-            slab_s[half + k, imag_rows, :] = (even_imag + odd_real).astype(BF16)
-            slab_s[half - 1 - k, real_rows, :] = (even_real + odd_imag).astype(BF16)
-            slab_s[half - 1 - k, imag_rows, :] = (even_imag - odd_real).astype(BF16)
-        return carry
-
-    lax.fori_loop(0, devices, spread, 0)
-
-    weights = [occupation_ref[n].astype(F32) for n in range(bands)]
-
-    def one_row(row):
-        spatial = jnp.dot(back_ref[...], slab_s[row], preferred_element_type=F32)
-        local = potential_ref[:, row, :]
-        density = jnp.zeros((width_first, width_third), F32)
-        moved_real, moved_imag = [], []
-        for n in range(bands):
-            real = spatial[:width_first, n * width_third : (n + 1) * width_third]
-            imag = spatial[width_first:, n * width_third : (n + 1) * width_third]
-            power = real * real + imag * imag
-            density = density + weights[n] * power
-            energy = (power * local).reshape(width_first // 8, 8, width_third)
-            energy_s[n] += jnp.sum(energy, axis=0)
-            moved_real.append((real * local).astype(BF16))
-            moved_imag.append((imag * local).astype(BF16))
-        density_s[:, row, :] = density
-        moved = jnp.concatenate(
-            [jnp.concatenate(moved_real, axis=1), jnp.concatenate(moved_imag, axis=1)]
-        )
-        return jnp.dot(fore_ref[...], moved, preferred_element_type=F32)
-
-    def pair(k, carry):
-        plus = one_row(half + k)
-        minus = one_row(half - 1 - k)
-        total = (plus + minus).astype(BF16)
-        gap = plus - minus
-        gap_real = gap[width_first:].astype(BF16)
-        gap_imag = (-gap[:width_first]).astype(BF16)
-        for p in range(devices):
-            even_rows = pl.ds(pl.multiple_of(k * slab, slab), slab)
-            odd_rows = pl.ds(pl.multiple_of((half + k) * slab, slab), slab)
-            mine = slice(p * slab, (p + 1) * slab)
-            acted_s[p, even_rows, :wide] = total[mine]
-            acted_s[p, even_rows, wide:] = total[width_first + p * slab : width_first + (p + 1) * slab]
-            acted_s[p, odd_rows, :wide] = gap_real[mine]
-            acted_s[p, odd_rows, wide:] = gap_imag[mine]
-        return carry
-
-    lax.fori_loop(0, half, pair, 0)
-
-    share = width_first // 2
-    own_ref[...] = density_s[pl.ds(side * share, share)] + rest_ref[...]
-    other_ref[...] = density_s[pl.ds((1 - side) * share, share)].astype(BF16)
+            turned = jnp.concatenate([a * cosines - b * sines, a * sines + b * cosines]).astype(BF16)
+            planes = lax.dot_general(select_s[p], turned, nt, preferred_element_type=F32)
+            even, odd = planes[: half * slab], planes[half * slab :]
+            even_real, even_imag = even[:, :width_third], even[:, width_third:]
+            odd_real, odd_imag = odd[:, :width_third], odd[:, width_third:]
+            plus_real = (even_real - odd_imag).astype(BF16)
+            plus_imag = (even_imag + odd_real).astype(BF16)
+            minus_real = (even_real + odd_imag).astype(BF16)
+            minus_imag = (even_imag - odd_real).astype(BF16)
+            real_rows = slice(p * slab, (p + 1) * slab)
+            imag_rows = slice(width_first + p * slab, width_first + (p + 1) * slab)
+            for k in range(half):
+                part = slice(k * slab, (k + 1) * slab)
+                slab_s[half + k, real_rows, lanes[n]] = plus_real[part]
+                slab_s[half + k, imag_rows, lanes[n]] = plus_imag[part]
+                slab_s[half - 1 - k, real_rows, lanes[n]] = minus_real[part]
+                slab_s[half - 1 - k, imag_rows, lanes[n]] = minus_imag[part]
+
+    group = 2
+    for k in range(half):
+        densities = [0.0, 0.0]
+        for start in range(0, bands, group):
+            members = range(start, start + group)
+            at = slice(start * width_third, (start + group) * width_third)
+            results = []
+            for sign, row in enumerate((half + k, half - 1 - k)):
+                spatial = jnp.dot(back_ref[...], slab_s[row, :, at], preferred_element_type=F32)
+                local = potential_ref[row]
+                moved_real, moved_imag = [], []
+                for i, n in enumerate(members):
+                    real = spatial[:width_first, lanes[i]]
+                    imag = spatial[width_first:, lanes[i]]
+                    power = real * real + imag * imag
+                    densities[sign] = densities[sign] + weights[n] * power
+                    energy = (power * local).reshape(width_first // 8, 8, width_third)
+                    energies[n] = energies[n] + jnp.sum(energy, axis=0)
+                    moved_real.append((real * local).astype(BF16))
+                    moved_imag.append((imag * local).astype(BF16))
+                moved = jnp.concatenate(
+                    [jnp.concatenate(moved_real, axis=1), jnp.concatenate(moved_imag, axis=1)]
+                )
+                results.append(jnp.dot(fore_ref[...], moved, preferred_element_type=F32))
+            plus, minus = results
+            total = (plus + minus).astype(BF16)
+            gap = plus - minus
+            gap_real = gap[width_first:].astype(BF16)
+            gap_imag = (-gap[:width_first]).astype(BF16)
+            for p in range(devices):
+                mine = slice(p * slab, (p + 1) * slab)
+                mine_imag = slice(width_first + p * slab, width_first + (p + 1) * slab)
+                even_rows = slice(k * slab, (k + 1) * slab)
+                odd_rows = slice((half + k) * slab, (half + k + 1) * slab)
+                for i, n in enumerate(members):
+                    to_real = slice(2 * n * width_third, (2 * n + 1) * width_third)
+                    to_imag = slice((2 * n + 1) * width_third, (2 * n + 2) * width_third)
+                    acted_s[p, even_rows, to_real] = total[mine, lanes[i]]
+                    acted_s[p, even_rows, to_imag] = total[mine_imag, lanes[i]]
+                    acted_s[p, odd_rows, to_real] = gap_real[mine, lanes[i]]
+                    acted_s[p, odd_rows, to_imag] = gap_imag[mine, lanes[i]]
+        for sign, row in enumerate((half + k, half - 1 - k)):
+            low, high = densities[sign][:share], densities[sign][share:]
+            own_ref[row] = jnp.where(low_side, low, high)
+            other_ref[row] = jnp.where(low_side, high, low).astype(BF16)
 
     waves = waves_ref[me].astype(F32)
     real, imag = waves[:bands], waves[bands : 2 * bands]
-    moving = jnp.sum((real * real + imag * imag) * kinetic_ref[...], axis=1, keepdims=True)
-    energy = jnp.concatenate(
-        [jnp.sum(energy_s[n], axis=(0, 1), keepdims=True) for n in range(bands)]
-    )
+    kinetic = kinetic_ref[...].reshape(1, count)
+    moving = jnp.sum((real * real + imag * imag) * kinetic, axis=1, keepdims=True)
+    energy = jnp.concatenate([jnp.sum(e, axis=(0, 1), keepdims=True) for e in energies])
     numerator = moving + energy
-    denominator = jnp.sum(square_s[...], axis=1, keepdims=True) * (1.0 / devices)
+    denominator = jnp.sum(square, axis=1, keepdims=True) * (1.0 / devices)
     scalars = []
     for value in (numerator, denominator):
         high = value.astype(BF16)
@@ -193,71 +203,67 @@
         scalars.append(jnp.broadcast_to(both, (2 * bands, LANES)))
     scalars = jnp.concatenate(scalars, axis=1).astype(BF16)
 
-    def collect(p, carry):
-        found = lax.dot_general(acted_s[p], select_s[p], tn, preferred_element_type=F32)
+    for p in range(devices):
         cosines, sines = phase_s[p, :width_third], phase_s[p, width_third:]
         reals, imags = [], []
         for n in range(bands):
-            at = n * width_third
-            real = found[at : at + width_third]
-            imag = found[wide + at : wide + at + width_third]
-            reals.append(jnp.sum(real * cosines + imag * sines, axis=0, keepdims=True))
-            imags.append(jnp.sum(imag * cosines - real * sines, axis=0, keepdims=True))
+            at = slice(2 * n * width_third, 2 * (n + 1) * width_third)
+            found = lax.dot_general(acted_s[p, :, at], select_s[p], tn, preferred_element_type=F32)
+            real, imag = found[:width_third], found[width_third:]
+            reals.append(
+                jnp.sum(real * cosines, axis=0, keepdims=True)
+                + jnp.sum(imag * sines, axis=0, keepdims=True)
+            )
+            imags.append(
+                jnp.sum(imag * cosines, axis=0, keepdims=True)
+                - jnp.sum(real * sines, axis=0, keepdims=True)
+            )
         real, imag = jnp.concatenate(reals), jnp.concatenate(imags)
-        centre = centre_s[p]
-        cosine, sine = centre[0:1], centre[1:2]
+        cosine, sine = centres[p][0:1], centres[p][1:2]
         result = jnp.concatenate([real * cosine + imag * sine, imag * cosine - real * sine])
         sent_ref[p, :, :count] = result.astype(BF16)
         sent_ref[p, :, count:] = scalars
-        return carry
-
-    lax.fori_loop(0, devices, collect, 0)
-
-
-def on_grid(waves, potential, rest_density, kinetic, occupation, bands, width_second):
+
+
+def on_grid(waves, potential, kinetic, occupation, partner, bands, width_second):
     devices, _, count = waves.shape
-    width_first, rows, width_third = potential.shape
+    rows, width_first, width_third = potential.shape
     slab = width_first // devices
-    wide = bands * width_third
     tables = wave_tables(devices, rows, width_first, width_second, width_third)
     vmem = pl.BlockSpec(memory_space=pltpu.VMEM)
     smem = pl.BlockSpec(memory_space=pltpu.SMEM)
+    planes = (rows, width_first // 2, width_third)
     return pl.pallas_call(
         functools.partial(grid_kernel, bands),
         out_shape=(
             jax.ShapeDtypeStruct((devices, 2 * bands, count + 2 * LANES), BF16),
-            jax.ShapeDtypeStruct(rest_density.shape, F32),
-            jax.ShapeDtypeStruct(rest_density.shape, BF16),
+            jax.ShapeDtypeStruct(planes, F32),
+            jax.ShapeDtypeStruct(planes, BF16),
         ),
-        in_specs=[vmem] * 8 + [smem],
+        in_specs=[vmem] * 7 + [smem, pl.BlockSpec(memory_space=pl.ANY)],
         out_specs=(vmem, vmem, vmem),
         scratch_shapes=[
             pltpu.VMEM((devices, 2 * width_third, count), F32),
             pltpu.VMEM((devices, rows * slab, count), BF16),
-            pltpu.VMEM((devices, 2, count), F32),
-            pltpu.VMEM((2 * wide, count), BF16),
-            pltpu.VMEM((rows, 2 * width_first, wide), BF16),
-            pltpu.VMEM((devices, rows * slab, 2 * wide), BF16),
-            pltpu.VMEM((width_first, rows, width_third), F32),
-            pltpu.VMEM((bands, 8, width_third), F32),
-            pltpu.VMEM((bands, count), F32),
+            pltpu.VMEM((rows, 2 * width_first, bands * width_third), BF16),
+            pltpu.VMEM((devices, rows * slab, 2 * bands * width_third), BF16),
         ],
-        compiler_params=pltpu.CompilerParams(vmem_limit_bytes=56 * 1024 * 1024),
-    )(waves, *[jnp.asarray(t) for t in tables], potential, rest_density, kinetic[None], occupation)
-
-
-def inner_kernel(bands, mine_ref, theirs_ref, trial_ref, partner_ref, kinetic_ref, all_ref, sent_ref, rest_ref):
-    count = kinetic_ref.shape[1]
+        compiler_params=pltpu.CompilerParams(vmem_limit_bytes=40 * 1024 * 1024),
+    )(waves, *[jnp.asarray(t) for t in tables], potential, kinetic, occupation, partner)
+
+
+def inner_kernel(bands, mine_ref, theirs_ref, trial_ref, partner_ref, kinetic_ref, all_ref, density_ref, sent_ref, rest_ref):
+    count = kinetic_ref.shape[0]
     first = lax.axis_index("band") == 0
     nt = (((1,), (1,)), ((), ()))
 
     def order(one, two):
         return jnp.concatenate([jnp.where(first, one, two), jnp.where(first, two, one)])
 
-    kinetic = kinetic_ref[...]
+    kinetic = kinetic_ref[...].reshape(1, count)
     damping = 1.0 / (1.0 + kinetic)
     mine, theirs = mine_ref[...], theirs_ref[...]
-    pairs = order(mine[:bands] + 0.0, theirs[:bands]), order(mine[bands:], theirs[bands:])
+    pairs = order(mine[:bands], theirs[:bands]), order(mine[bands:], theirs[bands:])
     sums = (pairs[0] + pairs[1])[:, count:]
     ratio = sums[:, 0:1] / (sums[:, LANES : LANES + 1] + EPSILON)
     halves, dampeds, softs = [], [], []
@@ -302,9 +308,9 @@
     imag = one[block:] + two[:block]
     for part, value in enumerate((real, imag)):
         low, high = value[:bands], value[bands:]
-        rows = slice(part * bands, (part + 1) * bands)
-        own_ref[rows] = rest_ref[rows] - jnp.where(first, low, high)
-        sent_ref[rows] = jnp.where(first, high, low)
+        rest = rest_ref[part * bands : (part + 1) * bands]
+        own_ref[part] = rest - jnp.where(first, low, high)
+        sent_ref[part] = jnp.where(first, high, low)
 
 
 def swap(values, axis, bit):
@@ -317,36 +323,37 @@
     _, rows, width_third = potential.shape
     width_second = rows * devices
     _, bands, count = trial_block.shape
+    states = all_bands.shape[1]
+    block = 2 * bands
+    vmem = pl.BlockSpec(memory_space=pltpu.VMEM)
+    params = pltpu.CompilerParams(vmem_limit_bytes=16 * 1024 * 1024)
     partner = swap(trial_block, "band", 1)
-    first = wave_cells // (width_second * width_third)
-    second = wave_cells // width_third % width_second
-    third = wave_cells % width_third
-    place = jnp.stack([first, second, third]).astype(BF16)
-    packet = jnp.concatenate([trial_block.reshape(2 * bands, count), place])
-    packet = jnp.pad(packet, ((0, -packet.shape[0] % 16), (0, 0)))
-    packets = jnp.broadcast_to(packet[None], (devices, *packet.shape))
+    packets = pl.pallas_call(
+        functools.partial(pack_kernel, bands, devices, width_second, width_third),
+        out_shape=jax.ShapeDtypeStruct((devices, 16, count), BF16),
+        in_specs=[vmem] * 2,
+        out_specs=vmem,
+        compiler_params=params,
+    )(trial_block, wave_cells)
     waves = lax.all_to_all(packets, "pw", split_axis=0, concat_axis=0, tiled=True)
     partial, density_own, density_other = on_grid(
-        waves, potential, rest_density, kinetic, occupation, bands, width_second
+        waves, potential.transpose(1, 0, 2), kinetic, occupation, partner, bands, width_second
     )
     arrived = lax.all_to_all(partial, "pw", split_axis=0, concat_axis=0, tiled=True)
+    block_density = density_own + swap(density_other, "band", 1).astype(F32)
+    density = rest_density + block_density.transpose(1, 0, 2)
     mine = jnp.sum(arrived.astype(F32), axis=0)
     theirs = swap(mine, "band", 1)
-    density = density_own + swap(density_other, "band", 1).astype(F32)
-    vmem = pl.BlockSpec(memory_space=pltpu.VMEM)
-    states = all_bands.shape[1]
-    block = 2 * bands
-    params = pltpu.CompilerParams(vmem_limit_bytes=32 * 1024 * 1024)
     sums, rest = pl.pallas_call(
         functools.partial(inner_kernel, bands),
         out_shape=(
             jax.ShapeDtypeStruct((4 * block, states), BF16),
             jax.ShapeDtypeStruct((block, count), F32),
         ),
-        in_specs=[vmem] * 6,
+        in_specs=[vmem] * 6 + [pl.BlockSpec(memory_space=pl.ANY)],
         out_specs=(vmem, vmem),
         compiler_params=params,
-    )(mine, theirs, trial_block, partner, kinetic[None], all_bands)
+    )(mine, theirs, trial_block, partner, kinetic, all_bands, density)
     bit = 1
     while 2 * bit < devices:
         sums = sums + swap(sums, "pw", bit)
@@ -355,14 +362,14 @@
         functools.partial(project_kernel, bands),
         out_shape=(
             jax.ShapeDtypeStruct((2 * block, states), F32),
-            jax.ShapeDtypeStruct((block, count), F32),
-            jax.ShapeDtypeStruct((block, count), F32),
+            jax.ShapeDtypeStruct((2, bands, count), F32),
+            jax.ShapeDtypeStruct((2, bands, count), F32),
         ),
         in_specs=[vmem] * 4,
         out_specs=(vmem, vmem, vmem),
         compiler_params=params,
     )(sums, swap(sums, "pw", bit), all_bands, rest)
-    correction = (own - swap(sent, "band", 1)).reshape(2, bands, count)
+    correction = own - swap(sent, "band", 1)
     correlation = correlation.reshape(2, block, states).transpose(0, 2, 1)
     return (correction, correlation, density)
 

time: 73.8 us -> 72.1 us (0.977)
  local copies, waits for them, and re-layouts: 4.74 us -> 13.6 us
  Pallas kernels: 25.6 us -> 17.9 us
  waiting for transfers between devices: 28.4 us -> 25.2 us
    unnamed x10 -> x31, local copies, waits for them, and re-layouts: 1.37 us -> 11.7 us
    pallas_call x1, Pallas kernels: 23.5 us -> 15.1 us  [on_grid(): pl.pallas_call(functools.partial(grid_kernel, bands), out_shape=(jax.Shap...]
    broadcast_in_dim x2 -> x0, local copies, waits for them, and re-layouts: 1.96 us -> none  [the longest x1 1.27 us: on_grid(): kinetic[None]]
    pallas_call x0 -> x1, local copies, waits for them, and re-layouts: none -> 1.83 us  [on_grid(): pl.pallas_call(functools.partial(grid_kernel, bands), out_shape=(jax.Shap...]
    all_to_all x1, waiting for transfers between devices: 7.2 us -> 5.45 us  [in_waves(): lax.all_to_all(partial, 'pw', split_axis=0, concat_axis=0, tiled=True)]
    all_to_all x1, waiting for transfers between devices: 6.69 us -> 5.13 us  [in_waves(): lax.all_to_all(packets, 'pw', split_axis=0, concat_axis=0, tiled=True)]
    reshape x2 -> x0, local copies, waits for them, and re-layouts: 1.4 us -> none  [the longest x1 0.78 us: in_waves(): packet = jnp.concatenate([trial_block.reshape(2 * bands, count), place])]
    another operation x1 -> x0, other arithmetic: 0.86 us -> none  [program(): jax.shard_map(body, mesh=mesh, in_specs=placed, out_specs=results, check_...]
  transfers between devices with their start and end apart: 9 -> 9, of which waited for: 7 -> 6; matrix products, arithmetic and copies ran while one was open for 3% -> 9% of each run, Pallas kernels for 3% -> 0%
where the time goes in v2:
time: 72.1 us; the launch traced here: 71.4 us
  waiting for transfers between devices  25.2 us (35%)
  Pallas kernels  17.9 us (25%)
  local copies, waits for them, and re-layouts  13.6 us (19%)
  starting transfers between devices  11.7 us (16%)
  other arithmetic  2.26 us (3%)
  between operations  0.76 us (1%)
    pallas_call x1, Pallas kernels, on_grid(): pl.pallas_call(functools.partial(grid_kernel, bands), out_shape=(jax.Shap...  15.1 us
    ppermute x7, waiting for transfers between devices, swap(): return lax.ppermute(values, axis, [(i, i ^ bit) for i in range(size)])  14.6 us
    unnamed x31, local copies, waits for them, and re-layouts  11.7 us
    all_to_all x1, starting transfers between devices, in_waves(): lax.all_to_all(packets, 'pw', split_axis=0, concat_axis=0, tiled=True)  7.38 us
    all_to_all x1, waiting for transfers between devices, in_waves(): lax.all_to_all(partial, 'pw', split_axis=0, concat_axis=0, tiled=True)  5.45 us
    all_to_all x1, waiting for transfers between devices, in_waves(): lax.all_to_all(packets, 'pw', split_axis=0, concat_axis=0, tiled=True)  5.13 us
    all_to_all x1, starting transfers between devices, in_waves(): lax.all_to_all(partial, 'pw', split_axis=0, concat_axis=0, tiled=True)  3.37 us
    pallas_call x1, local copies, waits for them, and re-layouts, on_grid(): pl.pallas_call(functools.partial(grid_kernel, bands), out_shape=(jax.Shap...  1.83 us
  transfers between devices with their start and end apart: 9, of which 6 were waited for; matrix products, arithmetic and copies ran while one was open for 9% of the time, Pallas kernels for 0%

profile of v2, /device:TPU:0, one launch (start us, length us, event | category | flops | bytes accessed | tf_op | source)
XLA Modules:
  0.0 71.4 jit_solution(12080355077312249263)
XLA Ops:
  0.6 0.0 copy-start.9
  0.6 0.7 copy-done.9
  1.3 0.0 copy-start.13
  1.3 0.7 copy-done.13
  2.0 0.7 shard_map.130
  2.7 0.0 copy-start.10
  2.7 0.0 copy-start.12
  2.7 7.4 %all-to-all-start = ((bf16[8,16,768]{2,1,0:T(8,128)(2,1)}), bf16[8,16,768]{2,1,0:T(8,128)(2,1)S(1)}, u32[]{:S(2)}, u32[]{:S(2)}) async-start(bf16[8,16,768]{2,1,0:T(8,128)(2,1)} %shard_map.130), calls=%async_computation | async-start | bytes 393216 | tf_op jit(solution)/shard_map/all_to_all | solution.py:338
  10.1 0.0 copy-start
  10.1 0.1 collective-permute-start
  10.2 2.7 %copy.21 = f32[128,16,128]{2,0,1:T(8,128)} copy(f32[128,16,128]{2,1,0:T(8,128)} %param.13) | data formatting | bytes 2097152 | tf_op args[2]
  12.9 0.0 collective-permute-done.partner_ref
  12.9 5.1 %all-to-all-done.waves_ref = bf16[8,16,768]{2,1,0:T(8,128)(2,1)S(1)} async-done(((bf16[8,16,768]{2,1,0:T(8,128)(2,1)}), bf16[8,16,768]{2,1,0:T(8,128)(2,1)S(1)}, u32[]{:S(2)}, u32[]{:S(2)}) %all-to-all-start) | async-done | bytes 196640 | tf_op jit(solution)/shard_map/all_to_all | solution.py:338
  18.1 0.0 copy-start.1
  18.1 1.2 %copy-done.1 = f32[128,16,128]{2,0,1:T(8,128)S(1)} copy-done((f32[128,16,128]{2,0,1:T(8,128)S(1)}, f32[128,16,128]{2,0,1:T(8,128)}, u32[]{:S(2)}) %copy-start.1) | copy-done | bytes 1048600
  19.3 0.9 %copy-done.5 = bf16[256,256]{1,0:T(8,128)(2,1)S(1)} copy-done((bf16[256,256]{1,0:T(8,128)(2,1)S(1)}, bf16[256,256]{1,0:T(8,128)(2,1)}, u32[]{:S(2)}) %copy-start.5) | copy-done | bytes 131096
  20.2 0.9 %copy-done.6 = bf16[256,256]{1,0:T(8,128)(2,1)S(1)} copy-done((bf16[256,256]{1,0:T(8,128)(2,1)S(1)}, bf16[256,256]{1,0:T(8,128)(2,1)}, u32[]{:S(2)}) %copy-start.6) | copy-done | bytes 131096
  21.1 0.9 %copy-done.7 = bf16[256,256]{1,0:T(8,128)(2,1)S(1)} copy-done((bf16[256,256]{1,0:T(8,128)(2,1)S(1)}, bf16[256,256]{1,0:T(8,128)(2,1)}, u32[]{:S(2)}) %copy-start.7) | copy-done | bytes 131096
  22.0 0.8 %copy-done.8 = bf16[8,32,128]{2,1,0:T(8,128)(2,1)S(1)} copy-done((bf16[8,32,128]{2,1,0:T(8,128)(2,1)S(1)}, bf16[8,32,128]{2,1,0:T(8,128)(2,1)}, u32[]{:S(2)}) %copy-start.8) | copy-done | bytes 65560
  22.9 0.7 copy-done.11
  23.5 0.7 copy-done.14
  24.2 15.1 %shard_map.131 = (bf16[8,8,1024]{2,1,0:T(8,128)(2,1)}, f32[16,64,128]{2,1,0:T(8,128)S(1)}, bf16[16,64,128]{2,1,0:T(8,128)(2,1)S(1)}) custom-call(bf16[8,16,768]{2,1,0:T(8,128)(2,1)S(1)} %all-to-all-done.waves_ref, bf16[8,32,128]{2,1,0:T(8,128)(2,1)S(1)} %copy-done.8, bf16[256,256]{1,0:T(8,128)(2,1)S(1)} %copy-done.7, bf16[256,256]{1,0:T(8,128)(2,1)S(1)} %copy-done.6, ...), custom_call_target="tpu_custom_call" | custom-call | tf_op jit(solution)/shard_map/pallas_call | solution.py:236
  39.3 0.8 %copy-done.3 = f32[16,64,128]{2,1,0:T(8,128)} copy-done((f32[16,64,128]{2,1,0:T(8,128)}, f32[16,64,128]{2,1,0:T(8,128)S(1)}, u32[]{:S(2)}) %copy-start.3) | copy-done | bytes 524312
  40.1 0.7 copy-done.4
  40.8 3.4 %all-to-all-start.1 = ((bf16[8,8,1024]{2,1,0:T(8,128)(2,1)}), bf16[8,8,1024]{2,1,0:T(8,128)(2,1)S(1)}, u32[]{:S(2)}, u32[]{:S(2)}) async-start(bf16[8,8,1024]{2,1,0:T(8,128)(2,1)} %get-tuple-element.11), calls=%async_computation.1 | async-start | bytes 262144 | tf_op jit(solution)/shard_map/all_to_all | solution.py:342
  44.2 1.8 %copy.15 = bf16[16,64,128]{2,0,1:T(8,128)(2,1)} copy(bf16[16,64,128]{2,1,0:T(8,128)(2,1)} %copy-done.4) | data formatting | bytes 524288 | tf_op jit(solution)/shard_map/pallas_call | solution.py:236
  46.0 0.0 collective-permute-start.2
  46.0 5.5 %all-to-all-done.1 = bf16[8,8,1024]{2,1,0:T(8,128)(2,1)S(1)} async-done(((bf16[8,8,1024]{2,1,0:T(8,128)(2,1)}), bf16[8,8,1024]{2,1,0:T(8,128)(2,1)S(1)}, u32[]{:S(2)}, u32[]{:S(2)}) %all-to-all-start.1) | async-done | bytes 131104 | tf_op jit(solution)/shard_map/all_to_all | solution.py:342
  51.5 0.1 collective-permute-start.1
  51.6 0.0 collective-permute-done.2
  51.6 1.6 %bitcast_add_fusion.density_ref = f32[64,16,128]{2,1,0:T(8,128)S(1)} fusion(f32[64,16,128]{2,1,0:T(8,128)} %param.14, f32[16,64,128]{2,1,0:T(8,128)} %copy-done.3, bf16[16,64,128]{2,0,1:T(8,128)(2,1)} %collective-permute-done.2), kind=kLoop, calls=%fused_computation.1 | loop fusion | flops 393216 | bytes 1835008 | tf_op jit(solution)/shard_map/add | solution.py:344
  53.2 0.0 copy-start.2
  53.2 0.0 collective-permute-done.1.theirs_ref
  53.2 0.0 copy-done.10
  53.2 0.0 copy-done.12
  53.2 0.0 copy-done
  53.2 1.0 %shard_map.132 = (bf16[32,1024]{1,0:T(8,128)(2,1)S(1)}, f32[8,768]{1,0:T(8,128)S(1)}) custom-call(f32[8,1024]{1,0:T(8,128)S(1)} %convert_reduce_fusion.mine_ref, f32[8,1024]{1,0:T(8,128)S(1)} %collective-permute-done.1.theirs_ref, bf16[2,4,768]{2,1,0:T(4,128)(2,1)S(1)} %copy-done.10, bf16[2,4,768]{2,1,0:T(4,128)(2,1)S(1)} %collective-permute-done.partner_ref, ...), custom_call_target="tpu_custom_call" | custom-call | tf_op jit(solution)/shard_map/pallas_call | solution.py:347
  54.3 0.3 collective-permute-start.3
  54.6 4.3 %collective-permute-done.3 = bf16[32,1024]{1,0:T(8,128)(2,1)S(1)} collective-permute-done((bf16[32,1024]{1,0:T(8,128)(2,1)S(1)}, bf16[32,1024]{1,0:T(8,128)(2,1)S(1)}, u32[]{:S(2)}, u32[]{:S(2)}) %collective-permute-start.3) | collective-permute-done | bytes 65568 | tf_op jit(solution)/shard_map/ppermute | solution.py:318
  58.9 0.1 collective-permute-start.4
  58.9 4.3 %collective-permute-done.4 = bf16[32,1024]{1,0:T(8,128)(2,1)S(1)} collective-permute-done((bf16[32,1024]{1,0:T(8,128)(2,1)S(1)}, bf16[32,1024]{1,0:T(8,128)(2,1)S(1)}, u32[]{:S(2)}, u32[]{:S(2)}) %collective-permute-start.4) | collective-permute-done | bytes 65568 | tf_op jit(solution)/shard_map/ppermute | solution.py:318
  63.2 0.5 collective-permute-start.5
  63.7 4.9 %collective-permute-done.5.arrived_ref = bf16[32,1024]{1,0:T(8,128)(2,1)S(1)} collective-permute-done((bf16[32,1024]{1,0:T(8,128)(2,1)S(1)}, bf16[32,1024]{1,0:T(8,128)(2,1)S(1)}, u32[]{:S(2)}, u32[]{:S(2)}) %collective-permute-start.5) | collective-permute-done | bytes 65568 | tf_op jit(solution)/shard_map/ppermute | solution.py:318
  68.6 1.0 %shard_map.133 = (f32[16,1024]{1,0:T(8,128)}, f32[2,4,768]{2,1,0:T(4,128)S(1)}, f32[2,4,768]{2,1,0:T(4,128)S(1)}) custom-call(bf16[32,1024]{1,0:T(8,128)(2,1)S(1)} %add.15.sums_ref, bf16[32,1024]{1,0:T(8,128)(2,1)S(1)} %collective-permute-done.5.arrived_ref, bf16[2,1024,768]{2,1,0:T(8,128)(2,1)S(1)} %copy-done, f32[8,768]{1,0:T(8,128)S(1)} %get-tuple-element.15.rest_ref), custom_call_target="tpu_custom_call" | custom-call | tf_op jit(solution)/shard_map/pallas_call | solution.py:361
  69.6 0.0 copy-done.2
  69.6 0.0 collective-permute-start.6
  69.6 1.2 %collective-permute-done.6 = f32[2,4,768]{2,1,0:T(4,128)S(1)} collective-permute-done((f32[2,4,768]{2,1,0:T(4,128)S(1)}, f32[2,4,768]{2,1,0:T(4,128)S(1)}, u32[]{:S(2)}, u32[]{:S(2)}) %collective-permute-start.6) | collective-permute-done | bytes 24608 | tf_op jit(solution)/shard_map/ppermute | solution.py:318
  70.8 0.6 sub.3
  (11 shorter events, 0.1 us)
Async XLA Ops:
  0.6 0.7 copy-start.9
  1.3 0.7 copy-start.13
  2.7 50.5 %copy-start.10 = (bf16[2,4,768]{2,1,0:T(4,128)(2,1)S(1)}, bf16[2,4,768]{2,1,0:T(4,128)(2,1)}, u32[]{:S(2)}) copy-start(bf16[2,4,768]{2,1,0:T(4,128)(2,1)} %trial_ref.3) | copy-start | bytes 36868
  2.7 50.5 %copy-start.12 = (f32[768]{0:T(1024)S(1)}, f32[768]{0:T(1024)}, u32[]{:S(2)}) copy-start(f32[768]{0:T(1024)} %kinetic_ref.3) | copy-start | bytes 9220
  2.7 15.3 %all-to-all-start = ((bf16[8,16,768]{2,1,0:T(8,128)(2,1)}), bf16[8,16,768]{2,1,0:T(8,128)(2,1)S(1)}, u32[]{:S(2)}, u32[]{:S(2)}) async-start(bf16[8,16,768]{2,1,0:T(8,128)(2,1)} %shard_map.130), calls=%async_computation | async-start | bytes 393216 | tf_op jit(solution)/shard_map/all_to_all | solution.py:338
  10.1 43.1 %copy-start = (bf16[2,1024,768]{2,1,0:T(8,128)(2,1)S(1)}, bf16[2,1024,768]{2,1,0:T(8,128)(2,1)}, u32[]{:S(2)}) copy-start(bf16[2,1024,768]{2,1,0:T(8,128)(2,1)} %all_ref.3) | copy-start | bytes 9437188
  10.1 2.8 %collective-permute-start = (bf16[2,4,768]{2,1,0:T(4,128)(2,1)}, bf16[2,4,768]{2,1,0:T(4,128)(2,1)S(1)}, u32[]{:S(2)}, u32[]{:S(2)}) collective-permute-start(bf16[2,4,768]{2,1,0:T(4,128)(2,1)} %trial_ref.3), channel_id=1, source_target_pairs={{0,1},{1,0},{2,3},{3,2},{4,5},{5,4},{6,7},{7,6},{8,9},{9,8},{10,11... | collective-permute-start | bytes 36872 | tf_op jit(solution)/shard_map/ppermute | solution.py:318
  18.1 1.2 %copy-start.1 = (f32[128,16,128]{2,0,1:T(8,128)S(1)}, f32[128,16,128]{2,0,1:T(8,128)}, u32[]{:S(2)}) copy-start(f32[128,16,128]{2,0,1:T(8,128)} %copy.21) | copy-start | bytes 3145732
  19.3 0.9 %copy-start.5 = (bf16[256,256]{1,0:T(8,128)(2,1)S(1)}, bf16[256,256]{1,0:T(8,128)(2,1)}, u32[]{:S(2)}) copy-start(bf16[256,256]{1,0:T(8,128)(2,1)} %constant.13.clone.fore_ref) | copy-start | bytes 393220
  20.2 0.9 %copy-start.6 = (bf16[256,256]{1,0:T(8,128)(2,1)S(1)}, bf16[256,256]{1,0:T(8,128)(2,1)}, u32[]{:S(2)}) copy-start(bf16[256,256]{1,0:T(8,128)(2,1)} %constant.12.clone.back_ref) | copy-start | bytes 393220
  21.1 0.9 %copy-start.7 = (bf16[256,256]{1,0:T(8,128)(2,1)S(1)}, bf16[256,256]{1,0:T(8,128)(2,1)}, u32[]{:S(2)}) copy-start(bf16[256,256]{1,0:T(8,128)(2,1)} %constant.11.clone.third_ref) | copy-start | bytes 393220
  22.0 0.8 %copy-start.8 = (bf16[8,32,128]{2,1,0:T(8,128)(2,1)S(1)}, bf16[8,32,128]{2,1,0:T(8,128)(2,1)}, u32[]{:S(2)}) copy-start(bf16[8,32,128]{2,1,0:T(8,128)(2,1)} %constant.10.clone.second_ref) | copy-start | bytes 196612
  22.8 0.7 copy-start.11
  23.5 0.7 copy-start.14
  39.3 0.8 %copy-start.3 = (f32[16,64,128]{2,1,0:T(8,128)}, f32[16,64,128]{2,1,0:T(8,128)S(1)}, u32[]{:S(2)}) copy-start(f32[16,64,128]{2,1,0:T(8,128)S(1)} %get-tuple-element.12) | copy-start | bytes 1572868
  40.1 0.7 copy-start.4
  40.8 10.7 %all-to-all-start.1 = ((bf16[8,8,1024]{2,1,0:T(8,128)(2,1)}), bf16[8,8,1024]{2,1,0:T(8,128)(2,1)S(1)}, u32[]{:S(2)}, u32[]{:S(2)}) async-start(bf16[8,8,1024]{2,1,0:T(8,128)(2,1)} %get-tuple-element.11), calls=%async_computation.1 | async-start | bytes 262144 | tf_op jit(solution)/shard_map/all_to_all | solution.py:342
  46.0 5.6 %collective-permute-start.2 = (bf16[16,64,128]{2,0,1:T(8,128)(2,1)}, bf16[16,64,128]{2,0,1:T(8,128)(2,1)}, u32[]{:S(2)}, u32[]{:S(2)}) collective-permute-start(bf16[16,64,128]{2,0,1:T(8,128)(2,1)} %copy.15), channel_id=1, source_target_pairs={{0,1},{1,0},{2,3},{3,2},{4,5},{5,4},{6,7},{7,6},{8,9},{9,8},{10,11... | collective-permute-start | bytes 786440 | tf_op jit(solution)/shard_map/ppermute | solution.py:318
  51.5 1.7 %collective-permute-start.1 = (f32[8,1024]{1,0:T(8,128)S(1)}, f32[8,1024]{1,0:T(8,128)S(1)}, u32[]{:S(2)}, u32[]{:S(2)}) collective-permute-start(f32[8,1024]{1,0:T(8,128)S(1)} %convert_reduce_fusion.mine_ref), channel_id=1, source_target_pairs={{0,1},{1,0},{2,3},{3,2},{4,5},{5,4},{6,7},{7,6},{8,9},{9,8},{10,11... | collective-permute-start | bytes 98312 | tf_op jit(solution)/shard_map/ppermute | solution.py:318
  53.2 16.4 %copy-start.2 = (f32[64,16,128]{2,1,0:T(8,128)}, f32[64,16,128]{2,1,0:T(8,128)S(1)}, u32[]{:S(2)}) copy-start(f32[64,16,128]{2,1,0:T(8,128)S(1)} %bitcast_add_fusion.density_ref) | copy-start | bytes 1572868
  54.3 4.5 %collective-permute-start.3 = (bf16[32,1024]{1,0:T(8,128)(2,1)S(1)}, bf16[32,1024]{1,0:T(8,128)(2,1)S(1)}, u32[]{:S(2)}, u32[]{:S(2)}) collective-permute-start(bf16[32,1024]{1,0:T(8,128)(2,1)S(1)} %get-tuple-element.14), channel_id=1, source_target_pairs={{0,2},{2,0},{4,6},{6,4},{8,10},{10,8},{12,14},{14,12},{1,3},{3,1},... | collective-permute-start | bytes 196616 | tf_op jit(solution)/shard_map/ppermute | solution.py:318
  58.9 4.3 %collective-permute-start.4 = (bf16[32,1024]{1,0:T(8,128)(2,1)S(1)}, bf16[32,1024]{1,0:T(8,128)(2,1)S(1)}, u32[]{:S(2)}, u32[]{:S(2)}) collective-permute-start(bf16[32,1024]{1,0:T(8,128)(2,1)S(1)} %add.14), channel_id=1, source_target_pairs={{0,4},{2,6},{4,0},{6,2},{8,12},{10,14},{12,8},{14,10},{1,5},{3,7},... | collective-permute-start | bytes 196616 | tf_op jit(solution)/shard_map/ppermute | solution.py:318
  63.2 5.4 %collective-permute-start.5 = (bf16[32,1024]{1,0:T(8,128)(2,1)S(1)}, bf16[32,1024]{1,0:T(8,128)(2,1)S(1)}, u32[]{:S(2)}, u32[]{:S(2)}) collective-permute-start(bf16[32,1024]{1,0:T(8,128)(2,1)S(1)} %add.15.sums_ref), channel_id=1, source_target_pairs={{0,8},{2,10},{4,12},{6,14},{8,0},{10,2},{12,4},{14,6},{1,9},{3,11}... | collective-permute-start | bytes 196616 | tf_op jit(solution)/shard_map/ppermute | solution.py:318
  69.6 1.2 %collective-permute-start.6 = (f32[2,4,768]{2,1,0:T(4,128)S(1)}, f32[2,4,768]{2,1,0:T(4,128)S(1)}, u32[]{:S(2)}, u32[]{:S(2)}) collective-permute-start(f32[2,4,768]{2,1,0:T(4,128)S(1)} %get-tuple-element.17), channel_id=1, source_target_pairs={{0,1},{1,0},{2,3},{3,2},{4,5},{5,4},{6,7},{7,6},{8,9},{9,8},{10,11... | collective-permute-start | bytes 73736 | tf_op jit(solution)/shard_map/ppermute | solution.py:318

commit v3 on v2

--- a/solution.py
+++ b/solution.py
@@ -72,19 +72,24 @@
     third_ref,
     back_ref,
     fore_ref,
-    potential_ref,
+    potential_in,
     kinetic_ref,
     occupation_ref,
-    partner_ref,
     sent_ref,
-    own_ref,
-    other_ref,
+    own_out,
+    other_out,
     phase_s,
     select_s,
     slab_s,
     acted_s,
+    potential_ref,
+    own_ref,
+    other_ref,
+    done,
 ):
     devices, _, count = waves_ref.shape
+    fetch = pltpu.make_async_copy(potential_in, potential_ref, done.at[2])
+    fetch.start()
     rows, width_first, width_third = potential_ref.shape
     slab = width_first // devices
     half = rows // 2
@@ -142,6 +147,7 @@
                 slab_s[half - 1 - k, real_rows, lanes[n]] = minus_real[part]
                 slab_s[half - 1 - k, imag_rows, lanes[n]] = minus_imag[part]
 
+    fetch.wait()
     group = 2
     for k in range(half):
         densities = [0.0, 0.0]
@@ -188,6 +194,13 @@
             own_ref[row] = jnp.where(low_side, low, high)
             other_ref[row] = jnp.where(low_side, high, low).astype(BF16)
 
+    stores = [
+        pltpu.make_async_copy(own_ref, own_out, done.at[0]),
+        pltpu.make_async_copy(other_ref, other_out, done.at[1]),
+    ]
+    for store in stores:
+        store.start()
+
     waves = waves_ref[me].astype(F32)
     real, imag = waves[:bands], waves[bands : 2 * bands]
     kinetic = kinetic_ref[...].reshape(1, count)
@@ -224,14 +237,18 @@
         sent_ref[p, :, :count] = result.astype(BF16)
         sent_ref[p, :, count:] = scalars
 
-
-def on_grid(waves, potential, kinetic, occupation, partner, bands, width_second):
+    for store in stores:
+        store.wait()
+
+
+def on_grid(waves, potential, kinetic, occupation, bands, width_second):
     devices, _, count = waves.shape
     rows, width_first, width_third = potential.shape
     slab = width_first // devices
     tables = wave_tables(devices, rows, width_first, width_second, width_third)
     vmem = pl.BlockSpec(memory_space=pltpu.VMEM)
     smem = pl.BlockSpec(memory_space=pltpu.SMEM)
+    anywhere = pl.BlockSpec(memory_space=pl.ANY)
     planes = (rows, width_first // 2, width_third)
     return pl.pallas_call(
         functools.partial(grid_kernel, bands),
@@ -240,43 +257,61 @@
             jax.ShapeDtypeStruct(planes, F32),
             jax.ShapeDtypeStruct(planes, BF16),
         ),
-        in_specs=[vmem] * 7 + [smem, pl.BlockSpec(memory_space=pl.ANY)],
-        out_specs=(vmem, vmem, vmem),
+        in_specs=[vmem] * 5 + [anywhere, vmem, smem],
+        out_specs=(vmem, anywhere, anywhere),
         scratch_shapes=[
             pltpu.VMEM((devices, 2 * width_third, count), F32),
             pltpu.VMEM((devices, rows * slab, count), BF16),
             pltpu.VMEM((rows, 2 * width_first, bands * width_third), BF16),
             pltpu.VMEM((devices, rows * slab, 2 * bands * width_third), BF16),
+            pltpu.VMEM(potential.shape, F32),
+            pltpu.VMEM(planes, F32),
+            pltpu.VMEM(planes, BF16),
+            pltpu.SemaphoreType.DMA((3,)),
         ],
-        compiler_params=pltpu.CompilerParams(vmem_limit_bytes=40 * 1024 * 1024),
-    )(waves, *[jnp.asarray(t) for t in tables], potential, kinetic, occupation, partner)
-
-
-def inner_kernel(bands, mine_ref, theirs_ref, trial_ref, partner_ref, kinetic_ref, all_ref, density_ref, sent_ref, rest_ref):
+        compiler_params=pltpu.CompilerParams(vmem_limit_bytes=56 * 1024 * 1024),
+    )(waves, *[jnp.asarray(t) for t in tables], potential, kinetic, occupation)
+
+
+def action_kernel(bands, arrived_ref, trial_ref, kinetic_ref, rows_ref, rest_ref):
+    devices = arrived_ref.shape[0]
     count = kinetic_ref.shape[0]
+    block = 2 * bands
+    total = sum(arrived_ref[p].astype(F32) for p in range(devices))
+    applied = total[:, :count]
+    scalars = total[:bands, count:] + total[bands:, count:]
+    ratio = scalars[:, 0:1] / (scalars[:, LANES : LANES + 1] + EPSILON)
+    kinetic = kinetic_ref[...].reshape(1, count)
+    damping = 1.0 / (1.0 + kinetic)
+    trial = jnp.concatenate([trial_ref[part].astype(F32) for part in range(2)])
+    action = kinetic * trial + applied
+    damped = (action * damping).astype(BF16).astype(F32)
+    soft = (trial * damping).astype(BF16).astype(F32)
+    both = jnp.concatenate([ratio, ratio])
+    rest_ref[...] = damped - both * soft
+    high = ratio.astype(BF16).astype(F32)
+    pair = jnp.broadcast_to(jnp.concatenate([high, ratio - high]), (block, LANES))
+    unused = jnp.zeros((block, count), F32)
+    rows = jnp.concatenate([action, damped, soft, unused])
+    tail = jnp.concatenate([pair, pair, pair, pair])
+    rows_ref[...] = jnp.concatenate([rows, tail], axis=1).astype(BF16)
+
+
+def inner_kernel(bands, mine_ref, theirs_ref, all_ref, received_ref, sent_ref, passed_ref):
+    count = all_ref.shape[2]
+    block = 2 * bands
     first = lax.axis_index("band") == 0
     nt = (((1,), (1,)), ((), ()))
-
-    def order(one, two):
-        return jnp.concatenate([jnp.where(first, one, two), jnp.where(first, two, one)])
-
-    kinetic = kinetic_ref[...].reshape(1, count)
-    damping = 1.0 / (1.0 + kinetic)
-    mine, theirs = mine_ref[...], theirs_ref[...]
-    pairs = order(mine[:bands], theirs[:bands]), order(mine[bands:], theirs[bands:])
-    sums = (pairs[0] + pairs[1])[:, count:]
-    ratio = sums[:, 0:1] / (sums[:, LANES : LANES + 1] + EPSILON)
-    halves, dampeds, softs = [], [], []
-    for part in range(2):
-        trial = order(trial_ref[part].astype(F32), partner_ref[part].astype(F32))
-        action = kinetic * trial + pairs[part][:, :count]
-        halves.append(action.astype(BF16))
-        dampeds.append((action * damping).astype(BF16))
-        softs.append((trial * damping).astype(BF16))
-    rows = jnp.concatenate(halves + dampeds + softs)
+    mine, theirs = mine_ref[...].astype(F32), theirs_ref[...].astype(F32)
+    low, high = jnp.where(first, mine, theirs), jnp.where(first, theirs, mine)
+    pieces = []
+    for at in range(0, 3 * block, bands):
+        pieces += [low[at : at + bands], high[at : at + bands]]
+    pair = pieces[0][:, count:] + pieces[2][:, count:], pieces[1][:, count:] + pieces[3][:, count:]
+    ratio = jnp.concatenate(pair)[:, 0:1]
+    rows = jnp.concatenate(pieces)[:, :count].astype(BF16)
     one = lax.dot_general(rows, all_ref[0], nt, preferred_element_type=F32)
     two = lax.dot_general(rows, all_ref[1], nt, preferred_element_type=F32)
-    block = 2 * bands
 
     def inner(at):
         real = one[at : at + block] + two[at + block : at + 2 * block]
@@ -288,18 +323,13 @@
     soft = inner(4 * block)
     coefficients = [d - ratio * s for d, s in zip(damped, soft)]
     sent_ref[...] = jnp.concatenate([*correlation, *coefficients]).astype(BF16)
-    own_ratio = jnp.where(first, ratio[:bands], ratio[bands:])
-    for part in range(2):
-        d, s = dampeds[part].astype(F32), softs[part].astype(F32)
-        d = jnp.where(first, d[:bands], d[bands:])
-        s = jnp.where(first, s[:bands], s[bands:])
-        rest_ref[part * bands : (part + 1) * bands] = d - own_ratio * s
-
-
-def project_kernel(bands, sums_ref, arrived_ref, all_ref, rest_ref, correlation_ref, own_ref, sent_ref):
+
+
+def project_kernel(bands, parts, *refs):
+    terms, (all_ref, rest_ref, _, correlation_ref, own_ref, sent_ref) = refs[:parts], refs[parts:]
     block = 2 * bands
     first = lax.axis_index("band") == 0
-    total = sums_ref[...].astype(F32) + arrived_ref[...].astype(F32)
+    total = sum(term[...].astype(F32) for term in terms)
     correlation_ref[...] = total[: 2 * block]
     coefficients = total[2 * block :].astype(BF16)
     one = jnp.dot(coefficients, all_ref[0], preferred_element_type=F32)
@@ -326,49 +356,57 @@
     states = all_bands.shape[1]
     block = 2 * bands
     vmem = pl.BlockSpec(memory_space=pltpu.VMEM)
+    anywhere = pl.BlockSpec(memory_space=pl.ANY)
     params = pltpu.CompilerParams(vmem_limit_bytes=16 * 1024 * 1024)
-    partner = swap(trial_block, "band", 1)
     packets = pl.pallas_call(
         functools.partial(pack_kernel, bands, devices, width_second, width_third),
         out_shape=jax.ShapeDtypeStruct((devices, 16, count), BF16),
         in_specs=[vmem] * 2,
         out_specs=vmem,
-        compiler_params=params,
+        compiler_params=pltpu.CompilerParams(vmem_limit_bytes=56 * 1024 * 1024),
     )(trial_block, wave_cells)
     waves = lax.all_to_all(packets, "pw", split_axis=0, concat_axis=0, tiled=True)
     partial, density_own, density_other = on_grid(
-        waves, potential.transpose(1, 0, 2), kinetic, occupation, partner, bands, width_second
+        waves, potential.transpose(1, 0, 2), kinetic, occupation, bands, width_second
     )
     arrived = lax.all_to_all(partial, "pw", split_axis=0, concat_axis=0, tiled=True)
-    block_density = density_own + swap(density_other, "band", 1).astype(F32)
-    density = rest_density + block_density.transpose(1, 0, 2)
-    mine = jnp.sum(arrived.astype(F32), axis=0)
+    received = swap(density_other, "band", 1)
+    mine, rest = pl.pallas_call(
+        functools.partial(action_kernel, bands),
+        out_shape=(
+            jax.ShapeDtypeStruct((4 * block, count + LANES), BF16),
+            jax.ShapeDtypeStruct((block, count), F32),
+        ),
+        in_specs=[vmem] * 3,
+        out_specs=(vmem, vmem),
+        compiler_params=params,
+    )(arrived, trial_block, kinetic)
     theirs = swap(mine, "band", 1)
-    sums, rest = pl.pallas_call(
+    sums, received = pl.pallas_call(
         functools.partial(inner_kernel, bands),
         out_shape=(
             jax.ShapeDtypeStruct((4 * block, states), BF16),
-            jax.ShapeDtypeStruct((block, count), F32),
+            jax.ShapeDtypeStruct(received.shape, received.dtype),
         ),
-        in_specs=[vmem] * 6 + [pl.BlockSpec(memory_space=pl.ANY)],
-        out_specs=(vmem, vmem),
+        in_specs=[vmem] * 3 + [anywhere],
+        out_specs=(vmem, anywhere),
+        input_output_aliases={3: 1},
         compiler_params=params,
-    )(mine, theirs, trial_block, partner, kinetic, all_bands, density)
-    bit = 1
-    while 2 * bit < devices:
-        sums = sums + swap(sums, "pw", bit)
-        bit *= 2
+    )(mine, theirs, all_bands, received)
+    density = rest_density + (density_own + received.astype(F32)).transpose(1, 0, 2)
+    near = sums + swap(sums, "pw", 1)
+    terms = [near] + [swap(near, "pw", step) for step in range(2, devices, 2)]
     correlation, own, sent = pl.pallas_call(
-        functools.partial(project_kernel, bands),
+        functools.partial(project_kernel, bands, len(terms)),
         out_shape=(
             jax.ShapeDtypeStruct((2 * block, states), F32),
             jax.ShapeDtypeStruct((2, bands, count), F32),
             jax.ShapeDtypeStruct((2, bands, count), F32),
         ),
-        in_specs=[vmem] * 4,
+        in_specs=[vmem] * (len(terms) + 2) + [anywhere],
         out_specs=(vmem, vmem, vmem),
         compiler_params=params,
-    )(sums, swap(sums, "pw", bit), all_bands, rest)
+    )(*terms, all_bands, rest, density)
     correction = own - swap(sent, "band", 1)
     correlation = correlation.reshape(2, block, states).transpose(0, 2, 1)
     return (correction, correlation, density)

time: 72.1 us -> 62.4 us (0.87)
  local copies, waits for them, and re-layouts: 13.6 us -> 3.26 us
  starting transfers between devices: 11.7 us -> 15.5 us
  waiting for transfers between devices: 25.2 us -> 21.9 us
  Pallas kernels: 17.9 us -> 19.6 us
  other arithmetic: 2.26 us -> 1.1 us
    unnamed x31 -> x15, local copies, waits for them, and re-layouts: 11.7 us -> 3.26 us
    ppermute x7, waiting for transfers between devices: 14.6 us -> 9.28 us  [swap(): return lax.ppermute(values, axis, [(i, i ^ bit) for i in range(size)])]
    ppermute x7, starting transfers between devices: 0.94 us -> 4.83 us  [swap(): return lax.ppermute(values, axis, [(i, i ^ bit) for i in range(size)])]
    pallas_call x1 -> x0, local copies, waits for them, and re-layouts: 1.83 us -> none  [on_grid(): pl.pallas_call(functools.partial(grid_kernel, bands), out_shape=(jax.Shap...]
    all_to_all x1, waiting for transfers between devices: 5.45 us -> 7.2 us  [in_waves(): lax.all_to_all(partial, 'pw', split_axis=0, concat_axis=0, tiled=True)]
    add x3 -> x2, other arithmetic: 1.63 us -> 0.49 us  [the longest x1 0.47 us: in_waves(): rest_density + (density_own + received.astype(F32)).transpose(1, 0, 2)]
    pallas_call x1, Pallas kernels: 0.7 us -> 1.56 us  [in_waves(): pl.pallas_call(functools.partial(pack_kernel, bands, devices, width_secon...]
    pallas_call x1, Pallas kernels: 15.1 us -> 15.9 us  [on_grid(): pl.pallas_call(functools.partial(grid_kernel, bands), out_shape=(jax.Shap...]
  transfers between devices with their start and end apart: 9 -> 9, of which waited for: 6 -> 7; matrix products, arithmetic and copies ran while one was open for 9% -> 5% of each run, Pallas kernels for 0% -> 0%
where the time goes in v3:
time: 62.4 us; the launch traced here: 62.1 us
  waiting for transfers between devices  21.9 us (35%)
  Pallas kernels  19.6 us (31%)
  starting transfers between devices  15.5 us (25%)
  local copies, waits for them, and re-layouts  3.26 us (5%)
  other arithmetic  1.1 us (2%)
  between operations  0.74 us (1%)
    pallas_call x1, Pallas kernels, on_grid(): pl.pallas_call(functools.partial(grid_kernel, bands), out_shape=(jax.Shap...  15.9 us
    ppermute x7, waiting for transfers between devices, swap(): return lax.ppermute(values, axis, [(i, i ^ bit) for i in range(size)])  9.28 us
    all_to_all x1, starting transfers between devices, in_waves(): lax.all_to_all(packets, 'pw', split_axis=0, concat_axis=0, tiled=True)  7.25 us
    all_to_all x1, waiting for transfers between devices, in_waves(): lax.all_to_all(partial, 'pw', split_axis=0, concat_axis=0, tiled=True)  7.2 us
    all_to_all x1, waiting for transfers between devices, in_waves(): lax.all_to_all(packets, 'pw', split_axis=0, concat_axis=0, tiled=True)  5.4 us
    ppermute x7, starting transfers between devices, swap(): return lax.ppermute(values, axis, [(i, i ^ bit) for i in range(size)])  4.83 us
    all_to_all x1, starting transfers between devices, in_waves(): lax.all_to_all(partial, 'pw', split_axis=0, concat_axis=0, tiled=True)  3.38 us
    unnamed x15, local copies, waits for them, and re-layouts  3.26 us
  transfers between devices with their start and end apart: 9, of which 7 were waited for; matrix products, arithmetic and copies ran while one was open for 5% of the time, Pallas kernels for 0%

profile of v3, /device:TPU:0, one launch (start us, length us, event | category | flops | bytes accessed | tf_op | source)
XLA Modules:
  0.0 62.1 jit_solution(3799356206907345377)
XLA Ops:
  0.6 0.0 copy-start.2
  0.6 0.0 copy-start.3
  0.7 0.0 copy-start
  0.7 1.6 %shard_map.130 = bf16[8,16,768]{2,1,0:T(8,128)(2,1)} custom-call(bf16[2,4,768]{2,1,0:T(4,128)(2,1)} %trial_ref.3, s32[768]{0:T(1024)} %cells_ref.1), custom_call_target="tpu_custom_call" | custom-call | tf_op jit(solution)/shard_map/pallas_call | solution.py:361
  2.2 7.3 %all-to-all-start = ((bf16[8,16,768]{2,1,0:T(8,128)(2,1)}), bf16[8,16,768]{2,1,0:T(8,128)(2,1)S(1)}, u32[]{:S(2)}, u32[]{:S(2)}) async-start(bf16[8,16,768]{2,1,0:T(8,128)(2,1)} %shard_map.130), calls=%async_computation | async-start | bytes 393216 | tf_op jit(solution)/shard_map/all_to_all | solution.py:368
  9.5 2.5 %copy.23 = f32[128,16,128]{2,0,1:T(8,128)} copy(f32[128,16,128]{2,1,0:T(8,128)} %param.13) | data formatting | bytes 2097152 | tf_op args[2]
  12.0 5.4 %all-to-all-done.waves_ref = bf16[8,16,768]{2,1,0:T(8,128)(2,1)S(1)} async-done(((bf16[8,16,768]{2,1,0:T(8,128)(2,1)}), bf16[8,16,768]{2,1,0:T(8,128)(2,1)S(1)}, u32[]{:S(2)}, u32[]{:S(2)}) %all-to-all-start) | async-done | bytes 196640 | tf_op jit(solution)/shard_map/all_to_all | solution.py:368
  17.4 0.0 copy-start.4
  17.4 0.7 %copy-done.4 = bf16[8,16,768]{2,1,0:T(8,128)(2,1)} copy-done((bf16[8,16,768]{2,1,0:T(8,128)(2,1)}, bf16[8,16,768]{2,1,0:T(8,128)(2,1)S(1)}, u32[]{:S(2)}) %copy-start.4) | copy-done | bytes 196632
  18.1 15.9 %shard_map.131 = (bf16[8,8,1024]{2,1,0:T(8,128)(2,1)}, f32[16,64,128]{2,1,0:T(8,128)}, bf16[16,64,128]{2,1,0:T(8,128)(2,1)}) custom-call(bf16[8,16,768]{2,1,0:T(8,128)(2,1)} %copy-done.4, bf16[8,32,128]{2,1,0:T(8,128)(2,1)} %constant.8.clone.second_ref, bf16[256,256]{1,0:T(8,128)(2,1)} %constant.9.clone.third_ref, bf16[256,256]{1,0:T(8,128)(2,1)} %constant.10.clone.back_ref, ...), custom_call_target="tpu_custom_call" | custom-call | tf_op jit(solution)/shard_map/pallas_call | solution.py:253
  34.0 3.4 %all-to-all-start.1 = ((bf16[8,8,1024]{2,1,0:T(8,128)(2,1)}), bf16[8,8,1024]{2,1,0:T(8,128)(2,1)S(1)}, u32[]{:S(2)}, u32[]{:S(2)}) async-start(bf16[8,8,1024]{2,1,0:T(8,128)(2,1)} %get-tuple-element.13), calls=%async_computation.1 | async-start | bytes 262144 | tf_op jit(solution)/shard_map/all_to_all | solution.py:372
  37.4 0.1 collective-permute-start.1
  37.5 7.2 %all-to-all-done.1.arrived_ref = bf16[8,8,1024]{2,1,0:T(8,128)(2,1)S(1)} async-done(((bf16[8,8,1024]{2,1,0:T(8,128)(2,1)}), bf16[8,8,1024]{2,1,0:T(8,128)(2,1)S(1)}, u32[]{:S(2)}, u32[]{:S(2)}) %all-to-all-start.1) | async-done | bytes 131104 | tf_op jit(solution)/shard_map/all_to_all | solution.py:372
  44.7 0.0 copy-done.2
  44.7 0.0 copy-done.3
  44.7 0.0 copy-start.5
  44.7 0.0 copy-start.6
  44.7 0.1 shard_map.132
  44.8 0.0 collective-permute-start
  44.8 0.0 collective-permute-done.1.received_ref
  44.8 1.2 %collective-permute-done.theirs_ref = bf16[32,896]{1,0:T(8,128)(2,1)S(1)} collective-permute-done((bf16[32,896]{1,0:T(8,128)(2,1)S(1)}, bf16[32,896]{1,0:T(8,128)(2,1)S(1)}, u32[]{:S(2)}, u32[]{:S(2)}) %collective-permute-start) | collective-permute-done | bytes 57376 | tf_op jit(solution)/shard_map/ppermute | solution.py:348
  46.1 0.0 copy-done
  46.1 1.0 %shard_map.133 = (bf16[32,1024]{1,0:T(8,128)(2,1)S(1)}, bf16[16,64,128]{2,1,0:T(8,128)(2,1)S(1)}) custom-call(bf16[32,896]{1,0:T(8,128)(2,1)S(1)} %get-tuple-element.14.mine_ref, bf16[32,896]{1,0:T(8,128)(2,1)S(1)} %collective-permute-done.theirs_ref, bf16[2,1024,768]{2,1,0:T(8,128)(2,1)S(1)} %copy-done, ...), custom_call_target="tpu_custom_call", output_to_operand_aliasing={{1}: (3, {})} | custom-call | tf_op jit(solution)/shard_map/pallas_call | solution.py:385
  47.1 0.3 collective-permute-start.2
  47.4 4.0 %collective-permute-done.2 = bf16[32,1024]{1,0:T(8,128)(2,1)S(1)} collective-permute-done((bf16[32,1024]{1,0:T(8,128)(2,1)S(1)}, bf16[32,1024]{1,0:T(8,128)(2,1)S(1)}, u32[]{:S(2)}, u32[]{:S(2)}) %collective-permute-start.2) | collective-permute-done | bytes 65568 | tf_op jit(solution)/shard_map/ppermute | solution.py:348
  51.5 0.6 %collective-permute-start.5 = (bf16[32,1024]{1,0:T(8,128)(2,1)S(1)}, bf16[32,1024]{1,0:T(8,128)(2,1)S(1)}, u32[]{:S(2)}, u32[]{:S(2)}) collective-permute-start(bf16[32,1024]{1,0:T(8,128)(2,1)S(1)} %add.9.refs_0_), channel_id=1, source_target_pairs={{0,12},{2,14},{4,8},{6,10},{8,4},{10,6},{12,0},{14,2},{1,13},{3,15... | collective-permute-start | bytes 196616 | tf_op jit(solution)/shard_map/ppermute | solution.py:348
  52.1 0.8 %collective-permute-start.4 = (bf16[32,1024]{1,0:T(8,128)(2,1)S(1)}, bf16[32,1024]{1,0:T(8,128)(2,1)S(1)}, u32[]{:S(2)}, u32[]{:S(2)}) collective-permute-start(bf16[32,1024]{1,0:T(8,128)(2,1)S(1)} %add.9.refs_0_), channel_id=1, source_target_pairs={{0,8},{2,10},{4,12},{6,14},{8,0},{10,2},{12,4},{14,6},{1,9},{3,11}... | collective-permute-start | bytes 196616 | tf_op jit(solution)/shard_map/ppermute | solution.py:348
  52.8 3.1 %collective-permute-start.3 = (bf16[32,1024]{1,0:T(8,128)(2,1)S(1)}, bf16[32,1024]{1,0:T(8,128)(2,1)S(1)}, u32[]{:S(2)}, u32[]{:S(2)}) collective-permute-start(bf16[32,1024]{1,0:T(8,128)(2,1)S(1)} %add.9.refs_0_), channel_id=1, source_target_pairs={{0,4},{2,6},{4,0},{6,2},{8,12},{10,14},{12,8},{14,10},{1,5},{3,7},... | collective-permute-start | bytes 196616 | tf_op jit(solution)/shard_map/ppermute | solution.py:348
  55.9 0.0 copy-done.5
  55.9 0.0 copy-done.6
  55.9 0.5 bitcast_add_fusion.refs_6_
  56.4 0.0 copy-start.1
  56.4 1.5 %collective-permute-done.5.refs_3_ = bf16[32,1024]{1,0:T(8,128)(2,1)S(1)} collective-permute-done((bf16[32,1024]{1,0:T(8,128)(2,1)S(1)}, bf16[32,1024]{1,0:T(8,128)(2,1)S(1)}, u32[]{:S(2)}, u32[]{:S(2)}) %collective-permute-start.5) | collective-permute-done | bytes 65568 | tf_op jit(solution)/shard_map/ppermute | solution.py:348
  57.9 1.3 %collective-permute-done.4.refs_2_ = bf16[32,1024]{1,0:T(8,128)(2,1)S(1)} collective-permute-done((bf16[32,1024]{1,0:T(8,128)(2,1)S(1)}, bf16[32,1024]{1,0:T(8,128)(2,1)S(1)}, u32[]{:S(2)}, u32[]{:S(2)}) %collective-permute-start.4) | collective-permute-done | bytes 65568 | tf_op jit(solution)/shard_map/ppermute | solution.py:348
  59.2 0.0 collective-permute-done.3.refs_1_
  59.2 1.1 %shard_map.134 = (f32[16,1024]{1,0:T(8,128)}, f32[2,4,768]{2,1,0:T(4,128)S(1)}, f32[2,4,768]{2,1,0:T(4,128)S(1)}) custom-call(bf16[32,1024]{1,0:T(8,128)(2,1)S(1)} %add.9.refs_0_, bf16[32,1024]{1,0:T(8,128)(2,1)S(1)} %collective-permute-done.3.refs_1_, bf16[32,1024]{1,0:T(8,128)(2,1)S(1)} %collective-permute-done.4.refs_2_, ...), custom_call_target="tpu_custom_call" | custom-call | tf_op jit(solution)/shard_map/pallas_call | solution.py:399
  60.3 0.0 collective-permute-start.6
  60.3 1.2 %collective-permute-done.6 = f32[2,4,768]{2,1,0:T(4,128)S(1)} collective-permute-done((f32[2,4,768]{2,1,0:T(4,128)S(1)}, f32[2,4,768]{2,1,0:T(4,128)S(1)}, u32[]{:S(2)}, u32[]{:S(2)}) %collective-permute-start.6) | collective-permute-done | bytes 24608 | tf_op jit(solution)/shard_map/ppermute | solution.py:348
  61.5 0.6 sub.3
  62.1 0.0 copy-done.1
  (1 shorter events, 0.0 us)
Async XLA Ops:
  0.6 44.1 %copy-start.2 = (bf16[2,4,768]{2,1,0:T(4,128)(2,1)S(1)}, bf16[2,4,768]{2,1,0:T(4,128)(2,1)}, u32[]{:S(2)}) copy-start(bf16[2,4,768]{2,1,0:T(4,128)(2,1)} %trial_ref.3) | copy-start | bytes 36868
  0.6 44.1 %copy-start.3 = (f32[768]{0:T(1024)S(1)}, f32[768]{0:T(1024)}, u32[]{:S(2)}) copy-start(f32[768]{0:T(1024)} %kinetic_ref.3) | copy-start | bytes 9220
  0.7 45.4 %copy-start = (bf16[2,1024,768]{2,1,0:T(8,128)(2,1)S(1)}, bf16[2,1024,768]{2,1,0:T(8,128)(2,1)}, u32[]{:S(2)}) copy-start(bf16[2,1024,768]{2,1,0:T(8,128)(2,1)} %refs_4_.1) | copy-start | bytes 9437188
  2.2 15.2 %all-to-all-start = ((bf16[8,16,768]{2,1,0:T(8,128)(2,1)}), bf16[8,16,768]{2,1,0:T(8,128)(2,1)S(1)}, u32[]{:S(2)}, u32[]{:S(2)}) async-start(bf16[8,16,768]{2,1,0:T(8,128)(2,1)} %shard_map.130), calls=%async_computation | async-start | bytes 393216 | tf_op jit(solution)/shard_map/all_to_all | solution.py:368
  17.4 0.7 %copy-start.4 = (bf16[8,16,768]{2,1,0:T(8,128)(2,1)}, bf16[8,16,768]{2,1,0:T(8,128)(2,1)S(1)}, u32[]{:S(2)}) copy-start(bf16[8,16,768]{2,1,0:T(8,128)(2,1)S(1)} %all-to-all-done.waves_ref) | copy-start | bytes 589828
  34.0 10.7 %all-to-all-start.1 = ((bf16[8,8,1024]{2,1,0:T(8,128)(2,1)}), bf16[8,8,1024]{2,1,0:T(8,128)(2,1)S(1)}, u32[]{:S(2)}, u32[]{:S(2)}) async-start(bf16[8,8,1024]{2,1,0:T(8,128)(2,1)} %get-tuple-element.13), calls=%async_computation.1 | async-start | bytes 262144 | tf_op jit(solution)/shard_map/all_to_all | solution.py:372
  37.4 7.4 %collective-permute-start.1 = (bf16[16,64,128]{2,1,0:T(8,128)(2,1)}, bf16[16,64,128]{2,1,0:T(8,128)(2,1)S(1)}, u32[]{:S(2)}, u32[]{:S(2)}) collective-permute-start(bf16[16,64,128]{2,1,0:T(8,128)(2,1)} %get-tuple-element.15), channel_id=1, source_target_pairs={{0,1},{1,0},{2,3},{3,2},{4,5},{5,4},{6,7},{7,6},{8,9},{9,8},{10,11... | collective-permute-start | bytes 786440 | tf_op jit(solution)/shard_map/ppermute | solution.py:348
  44.7 11.2 %copy-start.5 = (f32[64,16,128]{2,1,0:T(8,128)S(1)}, f32[64,16,128]{2,1,0:T(8,128)}, u32[]{:S(2)}) copy-start(f32[64,16,128]{2,1,0:T(8,128)} %param.14) | copy-start | bytes 1572868
  44.7 11.2 %copy-start.6 = (f32[16,64,128]{2,1,0:T(8,128)S(1)}, f32[16,64,128]{2,1,0:T(8,128)}, u32[]{:S(2)}) copy-start(f32[16,64,128]{2,1,0:T(8,128)} %get-tuple-element.18) | copy-start | bytes 1572868
  44.8 1.3 %collective-permute-start = (bf16[32,896]{1,0:T(8,128)(2,1)S(1)}, bf16[32,896]{1,0:T(8,128)(2,1)S(1)}, u32[]{:S(2)}, u32[]{:S(2)}) collective-permute-start(bf16[32,896]{1,0:T(8,128)(2,1)S(1)} %get-tuple-element.14.mine_ref), channel_id=1, source_target_pairs={{0,1},{1,0},{2,3},{3,2},{4,5},{5,4},{6,7},{7,6},{8,9},{9,8},{10,11... | collective-permute-start | bytes 172040 | tf_op jit(solution)/shard_map/ppermute | solution.py:348
  47.1 4.3 %collective-permute-start.2 = (bf16[32,1024]{1,0:T(8,128)(2,1)S(1)}, bf16[32,1024]{1,0:T(8,128)(2,1)S(1)}, u32[]{:S(2)}, u32[]{:S(2)}) collective-permute-start(bf16[32,1024]{1,0:T(8,128)(2,1)S(1)} %get-tuple-element.16), channel_id=1, source_target_pairs={{0,2},{2,0},{4,6},{6,4},{8,10},{10,8},{12,14},{14,12},{1,3},{3,1},... | collective-permute-start | bytes 196616 | tf_op jit(solution)/shard_map/ppermute | solution.py:348
  51.5 6.5 %collective-permute-start.5 = (bf16[32,1024]{1,0:T(8,128)(2,1)S(1)}, bf16[32,1024]{1,0:T(8,128)(2,1)S(1)}, u32[]{:S(2)}, u32[]{:S(2)}) collective-permute-start(bf16[32,1024]{1,0:T(8,128)(2,1)S(1)} %add.9.refs_0_), channel_id=1, source_target_pairs={{0,12},{2,14},{4,8},{6,10},{8,4},{10,6},{12,0},{14,2},{1,13},{3,15... | collective-permute-start | bytes 196616 | tf_op jit(solution)/shard_map/ppermute | solution.py:348
  52.1 7.1 %collective-permute-start.4 = (bf16[32,1024]{1,0:T(8,128)(2,1)S(1)}, bf16[32,1024]{1,0:T(8,128)(2,1)S(1)}, u32[]{:S(2)}, u32[]{:S(2)}) collective-permute-start(bf16[32,1024]{1,0:T(8,128)(2,1)S(1)} %add.9.refs_0_), channel_id=1, source_target_pairs={{0,8},{2,10},{4,12},{6,14},{8,0},{10,2},{12,4},{14,6},{1,9},{3,11}... | collective-permute-start | bytes 196616 | tf_op jit(solution)/shard_map/ppermute | solution.py:348
  52.8 6.4 %collective-permute-start.3 = (bf16[32,1024]{1,0:T(8,128)(2,1)S(1)}, bf16[32,1024]{1,0:T(8,128)(2,1)S(1)}, u32[]{:S(2)}, u32[]{:S(2)}) collective-permute-start(bf16[32,1024]{1,0:T(8,128)(2,1)S(1)} %add.9.refs_0_), channel_id=1, source_target_pairs={{0,4},{2,6},{4,0},{6,2},{8,12},{10,14},{12,8},{14,10},{1,5},{3,7},... | collective-permute-start | bytes 196616 | tf_op jit(solution)/shard_map/ppermute | solution.py:348
  56.4 5.7 %copy-start.1 = (f32[64,16,128]{2,1,0:T(8,128)}, f32[64,16,128]{2,1,0:T(8,128)S(1)}, u32[]{:S(2)}) copy-start(f32[64,16,128]{2,1,0:T(8,128)S(1)} %bitcast_add_fusion.refs_6_) | copy-start | bytes 1572868
  60.3 1.2 %collective-permute-start.6 = (f32[2,4,768]{2,1,0:T(4,128)S(1)}, f32[2,4,768]{2,1,0:T(4,128)S(1)}, u32[]{:S(2)}, u32[]{:S(2)}) collective-permute-start(f32[2,4,768]{2,1,0:T(4,128)S(1)} %get-tuple-element.21), channel_id=1, source_target_pairs={{0,1},{1,0},{2,3},{3,2},{4,5},{5,4},{6,7},{7,6},{8,9},{9,8},{10,11... | collective-permute-start | bytes 73736 | tf_op jit(solution)/shard_map/ppermute | solution.py:348

commit v4 on v3

--- a/solution.py
+++ b/solution.py
@@ -39,7 +39,7 @@
     missing = -second_table.shape[1] % 16
     second_table = np.pad(second_table, ((0, 0), (0, missing), (0, 0)))
     third = np.arange(width_third)
-    angles = (np.outer(third, third) % width_third) * (2 * math.pi / width_third)
+    angles = np.outer(third[: width_third // 2], third) % width_third * (2 * math.pi / width_third)
     factor = 1.0 / math.sqrt(width_second * width_third)
     values = np.concatenate([np.cos(angles), np.sin(angles)]) * factor
     third_table = np.concatenate(split_pair(values), axis=1)
@@ -99,10 +99,18 @@
     nt = (((1,), (1,)), ((), ()))
     tn = (((0,), (0,)), ((), ()))
     near = second_ref[me]
-    weights = [occupation_ref[n].astype(F32) for n in range(bands)]
-    lanes = [slice(n * width_third, (n + 1) * width_third) for n in range(bands)]
+    fold = width_third // 2
+    full = rows * slab
+    groups = bands // 2
+    low_lanes = lax.broadcasted_iota(jnp.int32, (1, width_third), 1) < fold
     square = jnp.zeros((bands, count), F32)
-    energies = [jnp.zeros((8, width_third), F32) for _ in range(bands)]
+    energies = [jnp.zeros((8, width_third), F32) for _ in range(groups)]
+    weights = [
+        jnp.where(
+            low_lanes, occupation_ref[2 * g].astype(F32), occupation_ref[2 * g + 1].astype(F32)
+        )
+        for g in range(groups)
+    ]
     centres = []
 
     for p in range(devices):
@@ -122,50 +130,66 @@
         turned_real = real * centre[0:1] - imag * centre[1:2]
         turned_imag = real * centre[1:2] + imag * centre[0:1]
         inside = lax.broadcasted_iota(jnp.int32, (slab, count), 0) == first
+        sign = jnp.where(lax.rem(third, 2) == 0, 1.0, -1.0)
+        near_turn, far_turn = turn[:rows], turn[:rows] * sign
         for k in range(rows):
-            select_s[p, k * slab : (k + 1) * slab, :] = jnp.where(
-                inside, turn[k : k + 1], 0.0
-            ).astype(BF16)
-        cosines, sines = phase[:width_third], phase[width_third:]
-        for n in range(bands):
-            a, b = turned_real[n : n + 1], turned_imag[n : n + 1]
-            turned = jnp.concatenate([a * cosines - b * sines, a * sines + b * cosines]).astype(BF16)
+            at = slice(k * slab, (k + 1) * slab)
+            select_s[p, at, :] = jnp.where(inside, near_turn[k : k + 1], 0.0).astype(BF16)
+            at = slice(full + k * slab, full + (k + 1) * slab)
+            select_s[p, at, :] = jnp.where(inside, far_turn[k : k + 1], 0.0).astype(BF16)
+        cosines, sines = phase[:fold], phase[fold:]
+        for g in range(groups):
+            reals, imags = [], []
+            for n in (2 * g, 2 * g + 1):
+                a, b = turned_real[n : n + 1], turned_imag[n : n + 1]
+                reals.append(a * cosines - b * sines)
+                imags.append(a * sines + b * cosines)
+            turned = jnp.concatenate(reals + imags).astype(BF16)
             planes = lax.dot_general(select_s[p], turned, nt, preferred_element_type=F32)
-            even, odd = planes[: half * slab], planes[half * slab :]
-            even_real, even_imag = even[:, :width_third], even[:, width_third:]
-            odd_real, odd_imag = odd[:, :width_third], odd[:, width_third:]
-            plus_real = (even_real - odd_imag).astype(BF16)
-            plus_imag = (even_imag + odd_real).astype(BF16)
-            minus_real = (even_real + odd_imag).astype(BF16)
-            minus_imag = (even_imag - odd_real).astype(BF16)
-            real_rows = slice(p * slab, (p + 1) * slab)
-            imag_rows = slice(width_first + p * slab, width_first + (p + 1) * slab)
-            for k in range(half):
-                part = slice(k * slab, (k + 1) * slab)
-                slab_s[half + k, real_rows, lanes[n]] = plus_real[part]
-                slab_s[half + k, imag_rows, lanes[n]] = plus_imag[part]
-                slab_s[half - 1 - k, real_rows, lanes[n]] = minus_real[part]
-                slab_s[half - 1 - k, imag_rows, lanes[n]] = minus_imag[part]
+            for h in range(2):
+                even = planes[h * full : h * full + full // 2]
+                odd = planes[h * full + full // 2 : (h + 1) * full]
+                even_real, even_imag = even[:, :width_third], even[:, width_third:]
+                odd_real, odd_imag = odd[:, :width_third], odd[:, width_third:]
+                plus_real = (even_real - odd_imag).astype(BF16)
+                plus_imag = (even_imag + odd_real).astype(BF16)
+                minus_real = (even_real + odd_imag).astype(BF16)
+                minus_imag = (even_imag - odd_real).astype(BF16)
+                real_rows = slice(p * slab, (p + 1) * slab)
+                imag_rows = slice(width_first + p * slab, width_first + (p + 1) * slab)
+                to = slice((2 * g + h) * width_third, (2 * g + h + 1) * width_third)
+                for k in range(half):
+                    part = slice(k * slab, (k + 1) * slab)
+                    slab_s[half + k, real_rows, to] = plus_real[part]
+                    slab_s[half + k, imag_rows, to] = plus_imag[part]
+                    slab_s[half - 1 - k, real_rows, to] = minus_real[part]
+                    slab_s[half - 1 - k, imag_rows, to] = minus_imag[part]
 
     fetch.wait()
-    group = 2
+    blocks = [slice(h * width_third, (h + 1) * width_third) for h in range(2)]
     for k in range(half):
-        densities = [0.0, 0.0]
-        for start in range(0, bands, group):
-            members = range(start, start + group)
-            at = slice(start * width_third, (start + group) * width_third)
+        densities = [[0.0, 0.0], [0.0, 0.0]]
+        locals_ = []
+        for row in (half + k, half - 1 - k):
+            values = potential_ref[row]
+            other = pltpu.roll(values, fold, 1)
+            locals_.append(
+                (jnp.where(low_lanes, values, other), jnp.where(low_lanes, other, values))
+            )
+        for g in range(groups):
+            at = slice(2 * g * width_third, (2 * g + 2) * width_third)
             results = []
-            for sign, row in enumerate((half + k, half - 1 - k)):
+            for side, row in enumerate((half + k, half - 1 - k)):
                 spatial = jnp.dot(back_ref[...], slab_s[row, :, at], preferred_element_type=F32)
-                local = potential_ref[row]
                 moved_real, moved_imag = [], []
-                for i, n in enumerate(members):
-                    real = spatial[:width_first, lanes[i]]
-                    imag = spatial[width_first:, lanes[i]]
+                for h in range(2):
+                    local = locals_[side][h]
+                    real = spatial[:width_first, blocks[h]]
+                    imag = spatial[width_first:, blocks[h]]
                     power = real * real + imag * imag
-                    densities[sign] = densities[sign] + weights[n] * power
+                    densities[side][h] = densities[side][h] + weights[g] * power
                     energy = (power * local).reshape(width_first // 8, 8, width_third)
-                    energies[n] = energies[n] + jnp.sum(energy, axis=0)
+                    energies[g] = energies[g] + jnp.sum(energy, axis=0)
                     moved_real.append((real * local).astype(BF16))
                     moved_imag.append((imag * local).astype(BF16))
                 moved = jnp.concatenate(
@@ -177,20 +201,23 @@
             gap = plus - minus
             gap_real = gap[width_first:].astype(BF16)
             gap_imag = (-gap[:width_first]).astype(BF16)
+            to_real = slice(2 * g * width_third, (2 * g + 1) * width_third)
+            to_imag = slice((2 * g + 1) * width_third, (2 * g + 2) * width_third)
             for p in range(devices):
                 mine = slice(p * slab, (p + 1) * slab)
                 mine_imag = slice(width_first + p * slab, width_first + (p + 1) * slab)
-                even_rows = slice(k * slab, (k + 1) * slab)
-                odd_rows = slice((half + k) * slab, (half + k + 1) * slab)
-                for i, n in enumerate(members):
-                    to_real = slice(2 * n * width_third, (2 * n + 1) * width_third)
-                    to_imag = slice((2 * n + 1) * width_third, (2 * n + 2) * width_third)
-                    acted_s[p, even_rows, to_real] = total[mine, lanes[i]]
-                    acted_s[p, even_rows, to_imag] = total[mine_imag, lanes[i]]
-                    acted_s[p, odd_rows, to_real] = gap_real[mine, lanes[i]]
-                    acted_s[p, odd_rows, to_imag] = gap_imag[mine, lanes[i]]
-        for sign, row in enumerate((half + k, half - 1 - k)):
-            low, high = densities[sign][:share], densities[sign][share:]
+                for h in range(2):
+                    even_rows = slice(h * full + k * slab, h * full + (k + 1) * slab)
+                    start = h * full + full // 2 + k * slab
+                    odd_rows = slice(start, start + slab)
+                    acted_s[p, even_rows, to_real] = total[mine, blocks[h]]
+                    acted_s[p, even_rows, to_imag] = total[mine_imag, blocks[h]]
+                    acted_s[p, odd_rows, to_real] = gap_real[mine, blocks[h]]
+                    acted_s[p, odd_rows, to_imag] = gap_imag[mine, blocks[h]]
+        for side, row in enumerate((half + k, half - 1 - k)):
+            folded = [d + pltpu.roll(d, fold, 1) for d in densities[side]]
+            density = jnp.where(low_lanes, *folded)
+            low, high = density[:share], density[share:]
             own_ref[row] = jnp.where(low_side, low, high)
             other_ref[row] = jnp.where(low_side, high, low).astype(BF16)
 
@@ -205,7 +232,11 @@
     real, imag = waves[:bands], waves[bands : 2 * bands]
     kinetic = kinetic_ref[...].reshape(1, count)
     moving = jnp.sum((real * real + imag * imag) * kinetic, axis=1, keepdims=True)
-    energy = jnp.concatenate([jnp.sum(e, axis=(0, 1), keepdims=True) for e in energies])
+    energy = []
+    for values in energies:
+        for part in (jnp.where(low_lanes, values, 0.0), jnp.where(low_lanes, 0.0, values)):
+            energy.append(jnp.sum(part, axis=(0, 1), keepdims=True))
+    energy = jnp.concatenate(energy)
     numerator = moving + energy
     denominator = jnp.sum(square, axis=1, keepdims=True) * (1.0 / devices)
     scalars = []
@@ -217,20 +248,22 @@
     scalars = jnp.concatenate(scalars, axis=1).astype(BF16)
 
     for p in range(devices):
-        cosines, sines = phase_s[p, :width_third], phase_s[p, width_third:]
+        cosines, sines = phase_s[p, :fold], phase_s[p, fold:]
         reals, imags = [], []
-        for n in range(bands):
-            at = slice(2 * n * width_third, 2 * (n + 1) * width_third)
+        for g in range(groups):
+            at = slice(2 * g * width_third, 2 * (g + 1) * width_third)
             found = lax.dot_general(acted_s[p, :, at], select_s[p], tn, preferred_element_type=F32)
-            real, imag = found[:width_third], found[width_third:]
-            reals.append(
-                jnp.sum(real * cosines, axis=0, keepdims=True)
-                + jnp.sum(imag * sines, axis=0, keepdims=True)
-            )
-            imags.append(
-                jnp.sum(imag * cosines, axis=0, keepdims=True)
-                - jnp.sum(real * sines, axis=0, keepdims=True)
-            )
+            for i in range(2):
+                real = found[i * fold : (i + 1) * fold]
+                imag = found[width_third + i * fold : width_third + (i + 1) * fold]
+                reals.append(
+                    jnp.sum(real * cosines, axis=0, keepdims=True)
+                    + jnp.sum(imag * sines, axis=0, keepdims=True)
+                )
+                imags.append(
+                    jnp.sum(imag * cosines, axis=0, keepdims=True)
+                    - jnp.sum(real * sines, axis=0, keepdims=True)
+                )
         real, imag = jnp.concatenate(reals), jnp.concatenate(imags)
         cosine, sine = centres[p][0:1], centres[p][1:2]
         result = jnp.concatenate([real * cosine + imag * sine, imag * cosine - real * sine])
@@ -260,10 +293,10 @@
         in_specs=[vmem] * 5 + [anywhere, vmem, smem],
         out_specs=(vmem, anywhere, anywhere),
         scratch_shapes=[
-            pltpu.VMEM((devices, 2 * width_third, count), F32),
-            pltpu.VMEM((devices, rows * slab, count), BF16),
+            pltpu.VMEM((devices, width_third, count), F32),
+            pltpu.VMEM((devices, 2 * rows * slab, count), BF16),
             pltpu.VMEM((rows, 2 * width_first, bands * width_third), BF16),
-            pltpu.VMEM((devices, rows * slab, 2 * bands * width_third), BF16),
+            pltpu.VMEM((devices, 2 * rows * slab, bands * width_third), BF16),
             pltpu.VMEM(potential.shape, F32),
             pltpu.VMEM(planes, F32),
             pltpu.VMEM(planes, BF16),

time: 62.4 us -> 60.9 us (0.976)
  Pallas kernels: 19.6 us -> 18.1 us
    pallas_call x1, Pallas kernels: 15.9 us -> 14.4 us  [on_grid(): pl.pallas_call(functools.partial(grid_kernel, bands), out_shape=(jax.Shap...]
where the time goes in v4:
time: 60.9 us; the launch traced here: 60.6 us
  waiting for transfers between devices  21.9 us (36%)
  Pallas kernels  18.1 us (30%)
  starting transfers between devices  15.5 us (25%)
  local copies, waits for them, and re-layouts  3.26 us (5%)
  other arithmetic  1.1 us (2%)
  between operations  0.74 us (1%)
    pallas_call x1, Pallas kernels, on_grid(): pl.pallas_call(functools.partial(grid_kernel, bands), out_shape=(jax.Shap...  14.4 us
    ppermute x7, waiting for transfers between devices, swap(): return lax.ppermute(values, axis, [(i, i ^ bit) for i in range(size)])  9.28 us
    all_to_all x1, starting transfers between devices, in_waves(): lax.all_to_all(packets, 'pw', split_axis=0, concat_axis=0, tiled=True)  7.25 us
    all_to_all x1, waiting for transfers between devices, in_waves(): lax.all_to_all(partial, 'pw', split_axis=0, concat_axis=0, tiled=True)  7.2 us
    all_to_all x1, waiting for transfers between devices, in_waves(): lax.all_to_all(packets, 'pw', split_axis=0, concat_axis=0, tiled=True)  5.4 us
    ppermute x7, starting transfers between devices, swap(): return lax.ppermute(values, axis, [(i, i ^ bit) for i in range(size)])  4.82 us
    all_to_all x1, starting transfers between devices, in_waves(): lax.all_to_all(partial, 'pw', split_axis=0, concat_axis=0, tiled=True)  3.38 us
    unnamed x15, local copies, waits for them, and re-layouts  3.26 us
  transfers between devices with their start and end apart: 9, of which 7 were waited for; matrix products, arithmetic and copies ran while one was open for 5% of the time, Pallas kernels for 0%

profile of v4, /device:TPU:0, one launch (start us, length us, event | category | flops | bytes accessed | tf_op | source)
XLA Modules:
  0.0 60.6 jit_solution(10543849712216769925)
XLA Ops:
  0.6 0.0 copy-start.2
  0.6 0.0 copy-start.3
  0.7 0.0 copy-start
  0.7 1.6 %shard_map.130 = bf16[8,16,768]{2,1,0:T(8,128)(2,1)} custom-call(bf16[2,4,768]{2,1,0:T(4,128)(2,1)} %trial_ref.3, s32[768]{0:T(1024)} %cells_ref.1), custom_call_target="tpu_custom_call" | custom-call | tf_op jit(solution)/shard_map/pallas_call | solution.py:394
  2.2 7.3 %all-to-all-start = ((bf16[8,16,768]{2,1,0:T(8,128)(2,1)}), bf16[8,16,768]{2,1,0:T(8,128)(2,1)S(1)}, u32[]{:S(2)}, u32[]{:S(2)}) async-start(bf16[8,16,768]{2,1,0:T(8,128)(2,1)} %shard_map.130), calls=%async_computation | async-start | bytes 393216 | tf_op jit(solution)/shard_map/all_to_all | solution.py:401
  9.5 2.5 %copy.23 = f32[128,16,128]{2,0,1:T(8,128)} copy(f32[128,16,128]{2,1,0:T(8,128)} %param.13) | data formatting | bytes 2097152 | tf_op args[2]
  12.0 5.4 %all-to-all-done.waves_ref = bf16[8,16,768]{2,1,0:T(8,128)(2,1)S(1)} async-done(((bf16[8,16,768]{2,1,0:T(8,128)(2,1)}), bf16[8,16,768]{2,1,0:T(8,128)(2,1)S(1)}, u32[]{:S(2)}, u32[]{:S(2)}) %all-to-all-start) | async-done | bytes 196640 | tf_op jit(solution)/shard_map/all_to_all | solution.py:401
  17.4 0.0 copy-start.4
  17.4 0.7 %copy-done.4 = bf16[8,16,768]{2,1,0:T(8,128)(2,1)} copy-done((bf16[8,16,768]{2,1,0:T(8,128)(2,1)}, bf16[8,16,768]{2,1,0:T(8,128)(2,1)S(1)}, u32[]{:S(2)}) %copy-start.4) | copy-done | bytes 196632
  18.1 14.4 %shard_map.131 = (bf16[8,8,1024]{2,1,0:T(8,128)(2,1)}, f32[16,64,128]{2,1,0:T(8,128)}, bf16[16,64,128]{2,1,0:T(8,128)(2,1)}) custom-call(bf16[8,16,768]{2,1,0:T(8,128)(2,1)} %copy-done.4, bf16[8,32,128]{2,1,0:T(8,128)(2,1)} %constant.8.clone.second_ref, bf16[128,256]{1,0:T(8,128)(2,1)} %constant.9.clone.third_ref, bf16[256,256]{1,0:T(8,128)(2,1)} %constant.10.clone.back_ref, ...), custom_call_target="tpu_custom_call" | custom-call | tf_op jit(solution)/shard_map/pallas_call | solution.py:286
  32.5 3.4 %all-to-all-start.1 = ((bf16[8,8,1024]{2,1,0:T(8,128)(2,1)}), bf16[8,8,1024]{2,1,0:T(8,128)(2,1)S(1)}, u32[]{:S(2)}, u32[]{:S(2)}) async-start(bf16[8,8,1024]{2,1,0:T(8,128)(2,1)} %get-tuple-element.13), calls=%async_computation.1 | async-start | bytes 262144 | tf_op jit(solution)/shard_map/all_to_all | solution.py:405
  35.9 0.1 collective-permute-start.1
  36.0 7.2 %all-to-all-done.1.arrived_ref = bf16[8,8,1024]{2,1,0:T(8,128)(2,1)S(1)} async-done(((bf16[8,8,1024]{2,1,0:T(8,128)(2,1)}), bf16[8,8,1024]{2,1,0:T(8,128)(2,1)S(1)}, u32[]{:S(2)}, u32[]{:S(2)}) %all-to-all-start.1) | async-done | bytes 131104 | tf_op jit(solution)/shard_map/all_to_all | solution.py:405
  43.2 0.0 copy-done.2
  43.2 0.0 copy-done.3
  43.2 0.0 copy-start.5
  43.2 0.0 copy-start.6
  43.2 0.1 shard_map.132
  43.3 0.0 collective-permute-start
  43.3 0.0 collective-permute-done.1.received_ref
  43.3 1.2 %collective-permute-done.theirs_ref = bf16[32,896]{1,0:T(8,128)(2,1)S(1)} collective-permute-done((bf16[32,896]{1,0:T(8,128)(2,1)S(1)}, bf16[32,896]{1,0:T(8,128)(2,1)S(1)}, u32[]{:S(2)}, u32[]{:S(2)}) %collective-permute-start) | collective-permute-done | bytes 57376 | tf_op jit(solution)/shard_map/ppermute | solution.py:381
  44.5 0.0 copy-done
  44.5 1.0 %shard_map.133 = (bf16[32,1024]{1,0:T(8,128)(2,1)S(1)}, bf16[16,64,128]{2,1,0:T(8,128)(2,1)S(1)}) custom-call(bf16[32,896]{1,0:T(8,128)(2,1)S(1)} %get-tuple-element.14.mine_ref, bf16[32,896]{1,0:T(8,128)(2,1)S(1)} %collective-permute-done.theirs_ref, bf16[2,1024,768]{2,1,0:T(8,128)(2,1)S(1)} %copy-done, ...), custom_call_target="tpu_custom_call", output_to_operand_aliasing={{1}: (3, {})} | custom-call | tf_op jit(solution)/shard_map/pallas_call | solution.py:418
  45.6 0.3 collective-permute-start.2
  45.9 4.1 %collective-permute-done.2 = bf16[32,1024]{1,0:T(8,128)(2,1)S(1)} collective-permute-done((bf16[32,1024]{1,0:T(8,128)(2,1)S(1)}, bf16[32,1024]{1,0:T(8,128)(2,1)S(1)}, u32[]{:S(2)}, u32[]{:S(2)}) %collective-permute-start.2) | collective-permute-done | bytes 65568 | tf_op jit(solution)/shard_map/ppermute | solution.py:381
  49.9 0.6 %collective-permute-start.5 = (bf16[32,1024]{1,0:T(8,128)(2,1)S(1)}, bf16[32,1024]{1,0:T(8,128)(2,1)S(1)}, u32[]{:S(2)}, u32[]{:S(2)}) collective-permute-start(bf16[32,1024]{1,0:T(8,128)(2,1)S(1)} %add.9.refs_0_), channel_id=1, source_target_pairs={{0,12},{2,14},{4,8},{6,10},{8,4},{10,6},{12,0},{14,2},{1,13},{3,15... | collective-permute-start | bytes 196616 | tf_op jit(solution)/shard_map/ppermute | solution.py:381
  50.5 0.8 %collective-permute-start.4 = (bf16[32,1024]{1,0:T(8,128)(2,1)S(1)}, bf16[32,1024]{1,0:T(8,128)(2,1)S(1)}, u32[]{:S(2)}, u32[]{:S(2)}) collective-permute-start(bf16[32,1024]{1,0:T(8,128)(2,1)S(1)} %add.9.refs_0_), channel_id=1, source_target_pairs={{0,8},{2,10},{4,12},{6,14},{8,0},{10,2},{12,4},{14,6},{1,9},{3,11}... | collective-permute-start | bytes 196616 | tf_op jit(solution)/shard_map/ppermute | solution.py:381
  51.3 3.1 %collective-permute-start.3 = (bf16[32,1024]{1,0:T(8,128)(2,1)S(1)}, bf16[32,1024]{1,0:T(8,128)(2,1)S(1)}, u32[]{:S(2)}, u32[]{:S(2)}) collective-permute-start(bf16[32,1024]{1,0:T(8,128)(2,1)S(1)} %add.9.refs_0_), channel_id=1, source_target_pairs={{0,4},{2,6},{4,0},{6,2},{8,12},{10,14},{12,8},{14,10},{1,5},{3,7},... | collective-permute-start | bytes 196616 | tf_op jit(solution)/shard_map/ppermute | solution.py:381
  54.4 0.0 copy-done.5
  54.4 0.0 copy-done.6
  54.4 0.5 bitcast_add_fusion.refs_6_
  54.9 0.0 copy-start.1
  54.9 1.5 %collective-permute-done.5.refs_3_ = bf16[32,1024]{1,0:T(8,128)(2,1)S(1)} collective-permute-done((bf16[32,1024]{1,0:T(8,128)(2,1)S(1)}, bf16[32,1024]{1,0:T(8,128)(2,1)S(1)}, u32[]{:S(2)}, u32[]{:S(2)}) %collective-permute-start.5) | collective-permute-done | bytes 65568 | tf_op jit(solution)/shard_map/ppermute | solution.py:381
  56.4 1.3 %collective-permute-done.4.refs_2_ = bf16[32,1024]{1,0:T(8,128)(2,1)S(1)} collective-permute-done((bf16[32,1024]{1,0:T(8,128)(2,1)S(1)}, bf16[32,1024]{1,0:T(8,128)(2,1)S(1)}, u32[]{:S(2)}, u32[]{:S(2)}) %collective-permute-start.4) | collective-permute-done | bytes 65568 | tf_op jit(solution)/shard_map/ppermute | solution.py:381
  57.7 0.0 collective-permute-done.3.refs_1_
  57.7 1.1 %shard_map.134 = (f32[16,1024]{1,0:T(8,128)}, f32[2,4,768]{2,1,0:T(4,128)S(1)}, f32[2,4,768]{2,1,0:T(4,128)S(1)}) custom-call(bf16[32,1024]{1,0:T(8,128)(2,1)S(1)} %add.9.refs_0_, bf16[32,1024]{1,0:T(8,128)(2,1)S(1)} %collective-permute-done.3.refs_1_, bf16[32,1024]{1,0:T(8,128)(2,1)S(1)} %collective-permute-done.4.refs_2_, ...), custom_call_target="tpu_custom_call" | custom-call | tf_op jit(solution)/shard_map/pallas_call | solution.py:432
  58.7 0.0 collective-permute-start.6
  58.7 1.2 %collective-permute-done.6 = f32[2,4,768]{2,1,0:T(4,128)S(1)} collective-permute-done((f32[2,4,768]{2,1,0:T(4,128)S(1)}, f32[2,4,768]{2,1,0:T(4,128)S(1)}, u32[]{:S(2)}, u32[]{:S(2)}) %collective-permute-start.6) | collective-permute-done | bytes 24608 | tf_op jit(solution)/shard_map/ppermute | solution.py:381
  59.9 0.6 %sub.3 = f32[2,4,768]{2,1,0:T(4,128)} subtract(f32[2,4,768]{2,1,0:T(4,128)S(1)} %get-tuple-element.20, f32[2,4,768]{2,1,0:T(4,128)S(1)} %collective-permute-done.6) | non-fusion elementwise | flops 6144 | bytes 73728 | tf_op jit(solution)/shard_map/sub | solution.py:443
  60.6 0.0 copy-done.1
  (1 shorter events, 0.0 us)
Async XLA Ops:
  0.6 42.5 %copy-start.2 = (bf16[2,4,768]{2,1,0:T(4,128)(2,1)S(1)}, bf16[2,4,768]{2,1,0:T(4,128)(2,1)}, u32[]{:S(2)}) copy-start(bf16[2,4,768]{2,1,0:T(4,128)(2,1)} %trial_ref.3) | copy-start | bytes 36868
  0.6 42.5 %copy-start.3 = (f32[768]{0:T(1024)S(1)}, f32[768]{0:T(1024)}, u32[]{:S(2)}) copy-start(f32[768]{0:T(1024)} %kinetic_ref.3) | copy-start | bytes 9220
  0.7 43.9 %copy-start = (bf16[2,1024,768]{2,1,0:T(8,128)(2,1)S(1)}, bf16[2,1024,768]{2,1,0:T(8,128)(2,1)}, u32[]{:S(2)}) copy-start(bf16[2,1024,768]{2,1,0:T(8,128)(2,1)} %refs_4_.1) | copy-start | bytes 9437188
  2.2 15.2 %all-to-all-start = ((bf16[8,16,768]{2,1,0:T(8,128)(2,1)}), bf16[8,16,768]{2,1,0:T(8,128)(2,1)S(1)}, u32[]{:S(2)}, u32[]{:S(2)}) async-start(bf16[8,16,768]{2,1,0:T(8,128)(2,1)} %shard_map.130), calls=%async_computation | async-start | bytes 393216 | tf_op jit(solution)/shard_map/all_to_all | solution.py:401
  17.4 0.7 %copy-start.4 = (bf16[8,16,768]{2,1,0:T(8,128)(2,1)}, bf16[8,16,768]{2,1,0:T(8,128)(2,1)S(1)}, u32[]{:S(2)}) copy-start(bf16[8,16,768]{2,1,0:T(8,128)(2,1)S(1)} %all-to-all-done.waves_ref) | copy-start | bytes 589828
  32.5 10.7 %all-to-all-start.1 = ((bf16[8,8,1024]{2,1,0:T(8,128)(2,1)}), bf16[8,8,1024]{2,1,0:T(8,128)(2,1)S(1)}, u32[]{:S(2)}, u32[]{:S(2)}) async-start(bf16[8,8,1024]{2,1,0:T(8,128)(2,1)} %get-tuple-element.13), calls=%async_computation.1 | async-start | bytes 262144 | tf_op jit(solution)/shard_map/all_to_all | solution.py:405
  35.9 7.4 %collective-permute-start.1 = (bf16[16,64,128]{2,1,0:T(8,128)(2,1)}, bf16[16,64,128]{2,1,0:T(8,128)(2,1)S(1)}, u32[]{:S(2)}, u32[]{:S(2)}) collective-permute-start(bf16[16,64,128]{2,1,0:T(8,128)(2,1)} %get-tuple-element.15), channel_id=1, source_target_pairs={{0,1},{1,0},{2,3},{3,2},{4,5},{5,4},{6,7},{7,6},{8,9},{9,8},{10,11... | collective-permute-start | bytes 786440 | tf_op jit(solution)/shard_map/ppermute | solution.py:381
  43.2 11.2 %copy-start.5 = (f32[64,16,128]{2,1,0:T(8,128)S(1)}, f32[64,16,128]{2,1,0:T(8,128)}, u32[]{:S(2)}) copy-start(f32[64,16,128]{2,1,0:T(8,128)} %param.14) | copy-start | bytes 1572868
  43.2 11.2 %copy-start.6 = (f32[16,64,128]{2,1,0:T(8,128)S(1)}, f32[16,64,128]{2,1,0:T(8,128)}, u32[]{:S(2)}) copy-start(f32[16,64,128]{2,1,0:T(8,128)} %get-tuple-element.18) | copy-start | bytes 1572868
  43.3 1.3 %collective-permute-start = (bf16[32,896]{1,0:T(8,128)(2,1)S(1)}, bf16[32,896]{1,0:T(8,128)(2,1)S(1)}, u32[]{:S(2)}, u32[]{:S(2)}) collective-permute-start(bf16[32,896]{1,0:T(8,128)(2,1)S(1)} %get-tuple-element.14.mine_ref), channel_id=1, source_target_pairs={{0,1},{1,0},{2,3},{3,2},{4,5},{5,4},{6,7},{7,6},{8,9},{9,8},{10,11... | collective-permute-start | bytes 172040 | tf_op jit(solution)/shard_map/ppermute | solution.py:381
  45.6 4.3 %collective-permute-start.2 = (bf16[32,1024]{1,0:T(8,128)(2,1)S(1)}, bf16[32,1024]{1,0:T(8,128)(2,1)S(1)}, u32[]{:S(2)}, u32[]{:S(2)}) collective-permute-start(bf16[32,1024]{1,0:T(8,128)(2,1)S(1)} %get-tuple-element.16), channel_id=1, source_target_pairs={{0,2},{2,0},{4,6},{6,4},{8,10},{10,8},{12,14},{14,12},{1,3},{3,1},... | collective-permute-start | bytes 196616 | tf_op jit(solution)/shard_map/ppermute | solution.py:381
  49.9 6.5 %collective-permute-start.5 = (bf16[32,1024]{1,0:T(8,128)(2,1)S(1)}, bf16[32,1024]{1,0:T(8,128)(2,1)S(1)}, u32[]{:S(2)}, u32[]{:S(2)}) collective-permute-start(bf16[32,1024]{1,0:T(8,128)(2,1)S(1)} %add.9.refs_0_), channel_id=1, source_target_pairs={{0,12},{2,14},{4,8},{6,10},{8,4},{10,6},{12,0},{14,2},{1,13},{3,15... | collective-permute-start | bytes 196616 | tf_op jit(solution)/shard_map/ppermute | solution.py:381
  50.5 7.1 %collective-permute-start.4 = (bf16[32,1024]{1,0:T(8,128)(2,1)S(1)}, bf16[32,1024]{1,0:T(8,128)(2,1)S(1)}, u32[]{:S(2)}, u32[]{:S(2)}) collective-permute-start(bf16[32,1024]{1,0:T(8,128)(2,1)S(1)} %add.9.refs_0_), channel_id=1, source_target_pairs={{0,8},{2,10},{4,12},{6,14},{8,0},{10,2},{12,4},{14,6},{1,9},{3,11}... | collective-permute-start | bytes 196616 | tf_op jit(solution)/shard_map/ppermute | solution.py:381
  51.3 6.4 %collective-permute-start.3 = (bf16[32,1024]{1,0:T(8,128)(2,1)S(1)}, bf16[32,1024]{1,0:T(8,128)(2,1)S(1)}, u32[]{:S(2)}, u32[]{:S(2)}) collective-permute-start(bf16[32,1024]{1,0:T(8,128)(2,1)S(1)} %add.9.refs_0_), channel_id=1, source_target_pairs={{0,4},{2,6},{4,0},{6,2},{8,12},{10,14},{12,8},{14,10},{1,5},{3,7},... | collective-permute-start | bytes 196616 | tf_op jit(solution)/shard_map/ppermute | solution.py:381
  54.9 5.7 %copy-start.1 = (f32[64,16,128]{2,1,0:T(8,128)}, f32[64,16,128]{2,1,0:T(8,128)S(1)}, u32[]{:S(2)}) copy-start(f32[64,16,128]{2,1,0:T(8,128)S(1)} %bitcast_add_fusion.refs_6_) | copy-start | bytes 1572868
  58.7 1.2 %collective-permute-start.6 = (f32[2,4,768]{2,1,0:T(4,128)S(1)}, f32[2,4,768]{2,1,0:T(4,128)S(1)}, u32[]{:S(2)}, u32[]{:S(2)}) collective-permute-start(f32[2,4,768]{2,1,0:T(4,128)S(1)} %get-tuple-element.21), channel_id=1, source_target_pairs={{0,1},{1,0},{2,3},{3,2},{4,5},{5,4},{6,7},{7,6},{8,9},{9,8},{10,11... | collective-permute-start | bytes 73736 | tf_op jit(solution)/shard_map/ppermute | solution.py:381

commit v5 on v4

--- a/solution.py
+++ b/solution.py
@@ -82,6 +82,7 @@
     select_s,
     slab_s,
     acted_s,
+    coef_s,
     potential_ref,
     own_ref,
     other_ref,
@@ -103,7 +104,6 @@
     full = rows * slab
     groups = bands // 2
     low_lanes = lax.broadcasted_iota(jnp.int32, (1, width_third), 1) < fold
-    square = jnp.zeros((bands, count), F32)
     energies = [jnp.zeros((8, width_third), F32) for _ in range(groups)]
     weights = [
         jnp.where(
@@ -113,7 +113,9 @@
     ]
     centres = []
 
-    for p in range(devices):
+    squares = []
+
+    def place(p):
         waves = waves_ref[p].astype(F32)
         place = waves[2 * bands : 2 * bands + 8].astype(jnp.int32)
         first, second, third = place[0:1], place[1:2], place[2:3]
@@ -121,12 +123,13 @@
         pick = jnp.where(line == second, 1.0, 0.0).astype(BF16)
         turn = jnp.dot(near, pick, preferred_element_type=F32)
         pick = jnp.where(line == third, 1.0, 0.0).astype(BF16)
-        phase = jnp.dot(third_ref[...], jnp.concatenate([pick, pick]), preferred_element_type=F32)
-        phase_s[p] = phase
+        phase_s[p] = jnp.dot(
+            third_ref[...], jnp.concatenate([pick, pick]), preferred_element_type=F32
+        )
         centre = turn[rows : rows + 2] + turn[rows + 2 : rows + 4]
         centres.append(centre)
         real, imag = waves[:bands], waves[bands : 2 * bands]
-        square = square + real * real + imag * imag
+        squares.append(real * real + imag * imag)
         turned_real = real * centre[0:1] - imag * centre[1:2]
         turned_imag = real * centre[1:2] + imag * centre[0:1]
         inside = lax.broadcasted_iota(jnp.int32, (slab, count), 0) == first
@@ -137,33 +140,52 @@
             select_s[p, at, :] = jnp.where(inside, near_turn[k : k + 1], 0.0).astype(BF16)
             at = slice(full + k * slab, full + (k + 1) * slab)
             select_s[p, at, :] = jnp.where(inside, far_turn[k : k + 1], 0.0).astype(BF16)
-        cosines, sines = phase[:fold], phase[fold:]
-        for g in range(groups):
-            reals, imags = [], []
-            for n in (2 * g, 2 * g + 1):
-                a, b = turned_real[n : n + 1], turned_imag[n : n + 1]
-                reals.append(a * cosines - b * sines)
-                imags.append(a * sines + b * cosines)
-            turned = jnp.concatenate(reals + imags).astype(BF16)
-            planes = lax.dot_general(select_s[p], turned, nt, preferred_element_type=F32)
-            for h in range(2):
-                even = planes[h * full : h * full + full // 2]
-                odd = planes[h * full + full // 2 : (h + 1) * full]
-                even_real, even_imag = even[:, :width_third], even[:, width_third:]
-                odd_real, odd_imag = odd[:, :width_third], odd[:, width_third:]
-                plus_real = (even_real - odd_imag).astype(BF16)
-                plus_imag = (even_imag + odd_real).astype(BF16)
-                minus_real = (even_real + odd_imag).astype(BF16)
-                minus_imag = (even_imag - odd_real).astype(BF16)
-                real_rows = slice(p * slab, (p + 1) * slab)
-                imag_rows = slice(width_first + p * slab, width_first + (p + 1) * slab)
-                to = slice((2 * g + h) * width_third, (2 * g + h + 1) * width_third)
-                for k in range(half):
-                    part = slice(k * slab, (k + 1) * slab)
-                    slab_s[half + k, real_rows, to] = plus_real[part]
-                    slab_s[half + k, imag_rows, to] = plus_imag[part]
-                    slab_s[half - 1 - k, real_rows, to] = minus_real[part]
-                    slab_s[half - 1 - k, imag_rows, to] = minus_imag[part]
+        return turned_real, turned_imag
+
+    def weigh(p, g, turned):
+        turned_real, turned_imag = turned
+        cosines, sines = phase_s[p, :fold], phase_s[p, fold:]
+        slot = (p * groups + g) % 2
+        for i, n in enumerate((2 * g, 2 * g + 1)):
+            a, b = turned_real[n : n + 1], turned_imag[n : n + 1]
+            real_rows = slice(i * fold, (i + 1) * fold)
+            imag_rows = slice(width_third + i * fold, width_third + (i + 1) * fold)
+            coef_s[slot, real_rows, :] = (a * cosines - b * sines).astype(BF16)
+            coef_s[slot, imag_rows, :] = (a * sines + b * cosines).astype(BF16)
+
+    def spread(p, g):
+        planes = lax.dot_general(
+            select_s[p], coef_s[(p * groups + g) % 2], nt, preferred_element_type=F32
+        )
+        for h in range(2):
+            even = planes[h * full : h * full + full // 2]
+            odd = planes[h * full + full // 2 : (h + 1) * full]
+            even_real, even_imag = even[:, :width_third], even[:, width_third:]
+            odd_real, odd_imag = odd[:, :width_third], odd[:, width_third:]
+            plus_real = (even_real - odd_imag).astype(BF16)
+            plus_imag = (even_imag + odd_real).astype(BF16)
+            minus_real = (even_real + odd_imag).astype(BF16)
+            minus_imag = (even_imag - odd_real).astype(BF16)
+            real_rows = slice(p * slab, (p + 1) * slab)
+            imag_rows = slice(width_first + p * slab, width_first + (p + 1) * slab)
+            to = slice((2 * g + h) * width_third, (2 * g + h + 1) * width_third)
+            for k in range(half):
+                part = slice(k * slab, (k + 1) * slab)
+                slab_s[half + k, real_rows, to] = plus_real[part]
+                slab_s[half + k, imag_rows, to] = plus_imag[part]
+                slab_s[half - 1 - k, real_rows, to] = minus_real[part]
+                slab_s[half - 1 - k, imag_rows, to] = minus_imag[part]
+
+    steps = [(p, g) for p in range(devices) for g in range(groups)]
+    turned = {0: place(0)}
+    weigh(0, 0, turned[0])
+    for i, (p, g) in enumerate(steps):
+        if g == 0 and p + 1 < devices:
+            turned[p + 1] = place(p + 1)
+        if i + 1 < len(steps):
+            weigh(*steps[i + 1], turned[steps[i + 1][0]])
+        spread(p, g)
+    square = sum(squares)
 
     fetch.wait()
     blocks = [slice(h * width_third, (h + 1) * width_third) for h in range(2)]
@@ -297,6 +319,7 @@
             pltpu.VMEM((devices, 2 * rows * slab, count), BF16),
             pltpu.VMEM((rows, 2 * width_first, bands * width_third), BF16),
             pltpu.VMEM((devices, 2 * rows * slab, bands * width_third), BF16),
+            pltpu.VMEM((2, 2 * width_third, count), BF16),
             pltpu.VMEM(potential.shape, F32),
             pltpu.VMEM(planes, F32),
             pltpu.VMEM(planes, BF16),

time: 60.9 us -> 60 us (0.985)
  Pallas kernels: 18.1 us -> 17.2 us
    pallas_call x1, Pallas kernels: 14.4 us -> 13.4 us  [on_grid(): pl.pallas_call(functools.partial(grid_kernel, bands), out_shape=(jax.Shap...]
where the time goes in v5:
time: 60 us; the launch traced here: 59.6 us
  waiting for transfers between devices  21.9 us (36%)
  Pallas kernels  17.2 us (29%)
  starting transfers between devices  15.5 us (26%)
  local copies, waits for them, and re-layouts  3.26 us (5%)
  other arithmetic  1.1 us (2%)
  between operations  0.74 us (1%)
    pallas_call x1, Pallas kernels, on_grid(): pl.pallas_call(functools.partial(grid_kernel, bands), out_shape=(jax.Shap...  13.4 us
    ppermute x7, waiting for transfers between devices, swap(): return lax.ppermute(values, axis, [(i, i ^ bit) for i in range(size)])  9.28 us
    all_to_all x1, starting transfers between devices, in_waves(): lax.all_to_all(packets, 'pw', split_axis=0, concat_axis=0, tiled=True)  7.25 us
    all_to_all x1, waiting for transfers between devices, in_waves(): lax.all_to_all(partial, 'pw', split_axis=0, concat_axis=0, tiled=True)  7.2 us
    all_to_all x1, waiting for transfers between devices, in_waves(): lax.all_to_all(packets, 'pw', split_axis=0, concat_axis=0, tiled=True)  5.4 us
    ppermute x7, starting transfers between devices, swap(): return lax.ppermute(values, axis, [(i, i ^ bit) for i in range(size)])  4.82 us
    all_to_all x1, starting transfers between devices, in_waves(): lax.all_to_all(partial, 'pw', split_axis=0, concat_axis=0, tiled=True)  3.38 us
    unnamed x15, local copies, waits for them, and re-layouts  3.26 us
  transfers between devices with their start and end apart: 9, of which 7 were waited for; matrix products, arithmetic and copies ran while one was open for 5% of the time, Pallas kernels for 0%

profile of v5, /device:TPU:0, one launch (start us, length us, event | category | flops | bytes accessed | tf_op | source)
XLA Modules:
  0.0 59.6 jit_solution(10941897460789107757)
XLA Ops:
  0.6 0.0 copy-start.2
  0.6 0.0 copy-start.3
  0.7 0.0 copy-start
  0.7 1.6 %shard_map.130 = bf16[8,16,768]{2,1,0:T(8,128)(2,1)} custom-call(bf16[2,4,768]{2,1,0:T(4,128)(2,1)} %trial_ref.3, s32[768]{0:T(1024)} %cells_ref.1), custom_call_target="tpu_custom_call" | custom-call | tf_op jit(solution)/shard_map/pallas_call | solution.py:417
  2.2 7.3 %all-to-all-start = ((bf16[8,16,768]{2,1,0:T(8,128)(2,1)}), bf16[8,16,768]{2,1,0:T(8,128)(2,1)S(1)}, u32[]{:S(2)}, u32[]{:S(2)}) async-start(bf16[8,16,768]{2,1,0:T(8,128)(2,1)} %shard_map.130), calls=%async_computation | async-start | bytes 393216 | tf_op jit(solution)/shard_map/all_to_all | solution.py:424
  9.5 2.5 %copy.23 = f32[128,16,128]{2,0,1:T(8,128)} copy(f32[128,16,128]{2,1,0:T(8,128)} %param.13) | data formatting | bytes 2097152 | tf_op args[2]
  12.0 5.4 %all-to-all-done.waves_ref = bf16[8,16,768]{2,1,0:T(8,128)(2,1)S(1)} async-done(((bf16[8,16,768]{2,1,0:T(8,128)(2,1)}), bf16[8,16,768]{2,1,0:T(8,128)(2,1)S(1)}, u32[]{:S(2)}, u32[]{:S(2)}) %all-to-all-start) | async-done | bytes 196640 | tf_op jit(solution)/shard_map/all_to_all | solution.py:424
  17.4 0.0 copy-start.4
  17.4 0.7 %copy-done.4 = bf16[8,16,768]{2,1,0:T(8,128)(2,1)} copy-done((bf16[8,16,768]{2,1,0:T(8,128)(2,1)}, bf16[8,16,768]{2,1,0:T(8,128)(2,1)S(1)}, u32[]{:S(2)}) %copy-start.4) | copy-done | bytes 196632
  18.1 13.4 %shard_map.131 = (bf16[8,8,1024]{2,1,0:T(8,128)(2,1)}, f32[16,64,128]{2,1,0:T(8,128)}, bf16[16,64,128]{2,1,0:T(8,128)(2,1)}) custom-call(bf16[8,16,768]{2,1,0:T(8,128)(2,1)} %copy-done.4, bf16[8,32,128]{2,1,0:T(8,128)(2,1)} %constant.8.clone.second_ref, bf16[128,256]{1,0:T(8,128)(2,1)} %constant.9.clone.third_ref, bf16[256,256]{1,0:T(8,128)(2,1)} %constant.10.clone.back_ref, ...), custom_call_target="tpu_custom_call" | custom-call | tf_op jit(solution)/shard_map/pallas_call | solution.py:308
  31.5 3.4 %all-to-all-start.1 = ((bf16[8,8,1024]{2,1,0:T(8,128)(2,1)}), bf16[8,8,1024]{2,1,0:T(8,128)(2,1)S(1)}, u32[]{:S(2)}, u32[]{:S(2)}) async-start(bf16[8,8,1024]{2,1,0:T(8,128)(2,1)} %get-tuple-element.13), calls=%async_computation.1 | async-start | bytes 262144 | tf_op jit(solution)/shard_map/all_to_all | solution.py:428
  34.9 0.1 collective-permute-start.1
  35.0 7.2 %all-to-all-done.1.arrived_ref = bf16[8,8,1024]{2,1,0:T(8,128)(2,1)S(1)} async-done(((bf16[8,8,1024]{2,1,0:T(8,128)(2,1)}), bf16[8,8,1024]{2,1,0:T(8,128)(2,1)S(1)}, u32[]{:S(2)}, u32[]{:S(2)}) %all-to-all-start.1) | async-done | bytes 131104 | tf_op jit(solution)/shard_map/all_to_all | solution.py:428
  42.2 0.0 copy-done.2
  42.2 0.0 copy-done.3
  42.2 0.0 copy-start.5
  42.2 0.0 copy-start.6
  42.2 0.1 shard_map.132
  42.3 0.0 collective-permute-start
  42.4 0.0 collective-permute-done.1.received_ref
  42.4 1.2 %collective-permute-done.theirs_ref = bf16[32,896]{1,0:T(8,128)(2,1)S(1)} collective-permute-done((bf16[32,896]{1,0:T(8,128)(2,1)S(1)}, bf16[32,896]{1,0:T(8,128)(2,1)S(1)}, u32[]{:S(2)}, u32[]{:S(2)}) %collective-permute-start) | collective-permute-done | bytes 57376 | tf_op jit(solution)/shard_map/ppermute | solution.py:404
  43.6 0.0 copy-done
  43.6 1.0 %shard_map.133 = (bf16[32,1024]{1,0:T(8,128)(2,1)S(1)}, bf16[16,64,128]{2,1,0:T(8,128)(2,1)S(1)}) custom-call(bf16[32,896]{1,0:T(8,128)(2,1)S(1)} %get-tuple-element.14.mine_ref, bf16[32,896]{1,0:T(8,128)(2,1)S(1)} %collective-permute-done.theirs_ref, bf16[2,1024,768]{2,1,0:T(8,128)(2,1)S(1)} %copy-done, ...), custom_call_target="tpu_custom_call", output_to_operand_aliasing={{1}: (3, {})} | custom-call | tf_op jit(solution)/shard_map/pallas_call | solution.py:441
  44.6 0.3 collective-permute-start.2
  44.9 4.1 %collective-permute-done.2 = bf16[32,1024]{1,0:T(8,128)(2,1)S(1)} collective-permute-done((bf16[32,1024]{1,0:T(8,128)(2,1)S(1)}, bf16[32,1024]{1,0:T(8,128)(2,1)S(1)}, u32[]{:S(2)}, u32[]{:S(2)}) %collective-permute-start.2) | collective-permute-done | bytes 65568 | tf_op jit(solution)/shard_map/ppermute | solution.py:404
  49.0 0.6 %collective-permute-start.5 = (bf16[32,1024]{1,0:T(8,128)(2,1)S(1)}, bf16[32,1024]{1,0:T(8,128)(2,1)S(1)}, u32[]{:S(2)}, u32[]{:S(2)}) collective-permute-start(bf16[32,1024]{1,0:T(8,128)(2,1)S(1)} %add.9.refs_0_), channel_id=1, source_target_pairs={{0,12},{2,14},{4,8},{6,10},{8,4},{10,6},{12,0},{14,2},{1,13},{3,15... | collective-permute-start | bytes 196616 | tf_op jit(solution)/shard_map/ppermute | solution.py:404
  49.6 0.8 %collective-permute-start.4 = (bf16[32,1024]{1,0:T(8,128)(2,1)S(1)}, bf16[32,1024]{1,0:T(8,128)(2,1)S(1)}, u32[]{:S(2)}, u32[]{:S(2)}) collective-permute-start(bf16[32,1024]{1,0:T(8,128)(2,1)S(1)} %add.9.refs_0_), channel_id=1, source_target_pairs={{0,8},{2,10},{4,12},{6,14},{8,0},{10,2},{12,4},{14,6},{1,9},{3,11}... | collective-permute-start | bytes 196616 | tf_op jit(solution)/shard_map/ppermute | solution.py:404
  50.4 3.1 %collective-permute-start.3 = (bf16[32,1024]{1,0:T(8,128)(2,1)S(1)}, bf16[32,1024]{1,0:T(8,128)(2,1)S(1)}, u32[]{:S(2)}, u32[]{:S(2)}) collective-permute-start(bf16[32,1024]{1,0:T(8,128)(2,1)S(1)} %add.9.refs_0_), channel_id=1, source_target_pairs={{0,4},{2,6},{4,0},{6,2},{8,12},{10,14},{12,8},{14,10},{1,5},{3,7},... | collective-permute-start | bytes 196616 | tf_op jit(solution)/shard_map/ppermute | solution.py:404
  53.4 0.0 copy-done.5
  53.4 0.0 copy-done.6
  53.4 0.5 bitcast_add_fusion.refs_6_
  53.9 0.0 copy-start.1
  53.9 1.5 %collective-permute-done.5.refs_3_ = bf16[32,1024]{1,0:T(8,128)(2,1)S(1)} collective-permute-done((bf16[32,1024]{1,0:T(8,128)(2,1)S(1)}, bf16[32,1024]{1,0:T(8,128)(2,1)S(1)}, u32[]{:S(2)}, u32[]{:S(2)}) %collective-permute-start.5) | collective-permute-done | bytes 65568 | tf_op jit(solution)/shard_map/ppermute | solution.py:404
  55.4 1.3 %collective-permute-done.4.refs_2_ = bf16[32,1024]{1,0:T(8,128)(2,1)S(1)} collective-permute-done((bf16[32,1024]{1,0:T(8,128)(2,1)S(1)}, bf16[32,1024]{1,0:T(8,128)(2,1)S(1)}, u32[]{:S(2)}, u32[]{:S(2)}) %collective-permute-start.4) | collective-permute-done | bytes 65568 | tf_op jit(solution)/shard_map/ppermute | solution.py:404
  56.7 0.0 collective-permute-done.3.refs_1_
  56.7 1.1 %shard_map.134 = (f32[16,1024]{1,0:T(8,128)}, f32[2,4,768]{2,1,0:T(4,128)S(1)}, f32[2,4,768]{2,1,0:T(4,128)S(1)}) custom-call(bf16[32,1024]{1,0:T(8,128)(2,1)S(1)} %add.9.refs_0_, bf16[32,1024]{1,0:T(8,128)(2,1)S(1)} %collective-permute-done.3.refs_1_, bf16[32,1024]{1,0:T(8,128)(2,1)S(1)} %collective-permute-done.4.refs_2_, ...), custom_call_target="tpu_custom_call" | custom-call | tf_op jit(solution)/shard_map/pallas_call | solution.py:455
  57.8 0.0 collective-permute-start.6
  57.8 1.2 %collective-permute-done.6 = f32[2,4,768]{2,1,0:T(4,128)S(1)} collective-permute-done((f32[2,4,768]{2,1,0:T(4,128)S(1)}, f32[2,4,768]{2,1,0:T(4,128)S(1)}, u32[]{:S(2)}, u32[]{:S(2)}) %collective-permute-start.6) | collective-permute-done | bytes 24608 | tf_op jit(solution)/shard_map/ppermute | solution.py:404
  59.0 0.6 %sub.3 = f32[2,4,768]{2,1,0:T(4,128)} subtract(f32[2,4,768]{2,1,0:T(4,128)S(1)} %get-tuple-element.20, f32[2,4,768]{2,1,0:T(4,128)S(1)} %collective-permute-done.6) | non-fusion elementwise | flops 6144 | bytes 73728 | tf_op jit(solution)/shard_map/sub | solution.py:466
  59.6 0.0 copy-done.1
  (1 shorter events, 0.0 us)
Async XLA Ops:
  0.6 41.6 %copy-start.2 = (bf16[2,4,768]{2,1,0:T(4,128)(2,1)S(1)}, bf16[2,4,768]{2,1,0:T(4,128)(2,1)}, u32[]{:S(2)}) copy-start(bf16[2,4,768]{2,1,0:T(4,128)(2,1)} %trial_ref.3) | copy-start | bytes 36868
  0.6 41.6 %copy-start.3 = (f32[768]{0:T(1024)S(1)}, f32[768]{0:T(1024)}, u32[]{:S(2)}) copy-start(f32[768]{0:T(1024)} %kinetic_ref.3) | copy-start | bytes 9220
  0.7 42.9 %copy-start = (bf16[2,1024,768]{2,1,0:T(8,128)(2,1)S(1)}, bf16[2,1024,768]{2,1,0:T(8,128)(2,1)}, u32[]{:S(2)}) copy-start(bf16[2,1024,768]{2,1,0:T(8,128)(2,1)} %refs_4_.1) | copy-start | bytes 9437188
  2.2 15.2 %all-to-all-start = ((bf16[8,16,768]{2,1,0:T(8,128)(2,1)}), bf16[8,16,768]{2,1,0:T(8,128)(2,1)S(1)}, u32[]{:S(2)}, u32[]{:S(2)}) async-start(bf16[8,16,768]{2,1,0:T(8,128)(2,1)} %shard_map.130), calls=%async_computation | async-start | bytes 393216 | tf_op jit(solution)/shard_map/all_to_all | solution.py:424
  17.4 0.7 %copy-start.4 = (bf16[8,16,768]{2,1,0:T(8,128)(2,1)}, bf16[8,16,768]{2,1,0:T(8,128)(2,1)S(1)}, u32[]{:S(2)}) copy-start(bf16[8,16,768]{2,1,0:T(8,128)(2,1)S(1)} %all-to-all-done.waves_ref) | copy-start | bytes 589828
  31.5 10.7 %all-to-all-start.1 = ((bf16[8,8,1024]{2,1,0:T(8,128)(2,1)}), bf16[8,8,1024]{2,1,0:T(8,128)(2,1)S(1)}, u32[]{:S(2)}, u32[]{:S(2)}) async-start(bf16[8,8,1024]{2,1,0:T(8,128)(2,1)} %get-tuple-element.13), calls=%async_computation.1 | async-start | bytes 262144 | tf_op jit(solution)/shard_map/all_to_all | solution.py:428
  34.9 7.4 %collective-permute-start.1 = (bf16[16,64,128]{2,1,0:T(8,128)(2,1)}, bf16[16,64,128]{2,1,0:T(8,128)(2,1)S(1)}, u32[]{:S(2)}, u32[]{:S(2)}) collective-permute-start(bf16[16,64,128]{2,1,0:T(8,128)(2,1)} %get-tuple-element.15), channel_id=1, source_target_pairs={{0,1},{1,0},{2,3},{3,2},{4,5},{5,4},{6,7},{7,6},{8,9},{9,8},{10,11... | collective-permute-start | bytes 786440 | tf_op jit(solution)/shard_map/ppermute | solution.py:404
  42.2 11.2 %copy-start.5 = (f32[64,16,128]{2,1,0:T(8,128)S(1)}, f32[64,16,128]{2,1,0:T(8,128)}, u32[]{:S(2)}) copy-start(f32[64,16,128]{2,1,0:T(8,128)} %param.14) | copy-start | bytes 1572868
  42.2 11.2 %copy-start.6 = (f32[16,64,128]{2,1,0:T(8,128)S(1)}, f32[16,64,128]{2,1,0:T(8,128)}, u32[]{:S(2)}) copy-start(f32[16,64,128]{2,1,0:T(8,128)} %get-tuple-element.18) | copy-start | bytes 1572868
  42.3 1.3 %collective-permute-start = (bf16[32,896]{1,0:T(8,128)(2,1)S(1)}, bf16[32,896]{1,0:T(8,128)(2,1)S(1)}, u32[]{:S(2)}, u32[]{:S(2)}) collective-permute-start(bf16[32,896]{1,0:T(8,128)(2,1)S(1)} %get-tuple-element.14.mine_ref), channel_id=1, source_target_pairs={{0,1},{1,0},{2,3},{3,2},{4,5},{5,4},{6,7},{7,6},{8,9},{9,8},{10,11... | collective-permute-start | bytes 172040 | tf_op jit(solution)/shard_map/ppermute | solution.py:404
  44.6 4.3 %collective-permute-start.2 = (bf16[32,1024]{1,0:T(8,128)(2,1)S(1)}, bf16[32,1024]{1,0:T(8,128)(2,1)S(1)}, u32[]{:S(2)}, u32[]{:S(2)}) collective-permute-start(bf16[32,1024]{1,0:T(8,128)(2,1)S(1)} %get-tuple-element.16), channel_id=1, source_target_pairs={{0,2},{2,0},{4,6},{6,4},{8,10},{10,8},{12,14},{14,12},{1,3},{3,1},... | collective-permute-start | bytes 196616 | tf_op jit(solution)/shard_map/ppermute | solution.py:404
  49.0 6.5 %collective-permute-start.5 = (bf16[32,1024]{1,0:T(8,128)(2,1)S(1)}, bf16[32,1024]{1,0:T(8,128)(2,1)S(1)}, u32[]{:S(2)}, u32[]{:S(2)}) collective-permute-start(bf16[32,1024]{1,0:T(8,128)(2,1)S(1)} %add.9.refs_0_), channel_id=1, source_target_pairs={{0,12},{2,14},{4,8},{6,10},{8,4},{10,6},{12,0},{14,2},{1,13},{3,15... | collective-permute-start | bytes 196616 | tf_op jit(solution)/shard_map/ppermute | solution.py:404
  49.6 7.1 %collective-permute-start.4 = (bf16[32,1024]{1,0:T(8,128)(2,1)S(1)}, bf16[32,1024]{1,0:T(8,128)(2,1)S(1)}, u32[]{:S(2)}, u32[]{:S(2)}) collective-permute-start(bf16[32,1024]{1,0:T(8,128)(2,1)S(1)} %add.9.refs_0_), channel_id=1, source_target_pairs={{0,8},{2,10},{4,12},{6,14},{8,0},{10,2},{12,4},{14,6},{1,9},{3,11}... | collective-permute-start | bytes 196616 | tf_op jit(solution)/shard_map/ppermute | solution.py:404
  50.4 6.4 %collective-permute-start.3 = (bf16[32,1024]{1,0:T(8,128)(2,1)S(1)}, bf16[32,1024]{1,0:T(8,128)(2,1)S(1)}, u32[]{:S(2)}, u32[]{:S(2)}) collective-permute-start(bf16[32,1024]{1,0:T(8,128)(2,1)S(1)} %add.9.refs_0_), channel_id=1, source_target_pairs={{0,4},{2,6},{4,0},{6,2},{8,12},{10,14},{12,8},{14,10},{1,5},{3,7},... | collective-permute-start | bytes 196616 | tf_op jit(solution)/shard_map/ppermute | solution.py:404
  53.9 5.7 %copy-start.1 = (f32[64,16,128]{2,1,0:T(8,128)}, f32[64,16,128]{2,1,0:T(8,128)S(1)}, u32[]{:S(2)}) copy-start(f32[64,16,128]{2,1,0:T(8,128)S(1)} %bitcast_add_fusion.refs_6_) | copy-start | bytes 1572868
  57.8 1.2 %collective-permute-start.6 = (f32[2,4,768]{2,1,0:T(4,128)S(1)}, f32[2,4,768]{2,1,0:T(4,128)S(1)}, u32[]{:S(2)}, u32[]{:S(2)}) collective-permute-start(f32[2,4,768]{2,1,0:T(4,128)S(1)} %get-tuple-element.21), channel_id=1, source_target_pairs={{0,1},{1,0},{2,3},{3,2},{4,5},{5,4},{6,7},{7,6},{8,9},{9,8},{10,11... | collective-permute-start | bytes 73736 | tf_op jit(solution)/shard_map/ppermute | solution.py:404

commit v6 on v5

--- a/solution.py
+++ b/solution.py
@@ -57,10 +57,12 @@
     first = lax.div(cells, width_second * width_third)
     second = lax.rem(lax.div(cells, width_third), width_second)
     third = lax.rem(cells, width_third)
-    unused = jnp.zeros((packet_ref.shape[1] - 2 * bands - 3, cells.shape[1]), jnp.int32)
-    place = jnp.concatenate([first, second, third, unused]).astype(F32)
-    trial = [trial_ref[part].astype(F32) for part in range(2)]
-    packet = jnp.concatenate([*trial, place]).astype(BF16)
+    middle = cells.shape[1] // 2
+    halves = [part for row in (first, second, third) for part in (row[:, :middle], row[:, middle:])]
+    unused = jnp.zeros((2 * bands - 6, middle), jnp.int32)
+    place = jnp.concatenate([*halves, unused]).astype(F32)
+    trial = jnp.concatenate([trial_ref[part].astype(F32) for part in range(2)])
+    packet = jnp.concatenate([trial, place], axis=1).astype(BF16)
     for p in range(devices):
         packet_ref[p] = packet
 
@@ -88,7 +90,8 @@
     other_ref,
     done,
 ):
-    devices, _, count = waves_ref.shape
+    devices, _, length = waves_ref.shape
+    count = 2 * length // 3
     fetch = pltpu.make_async_copy(potential_in, potential_ref, done.at[2])
     fetch.start()
     rows, width_first, width_third = potential_ref.shape
@@ -115,31 +118,40 @@
 
     squares = []
 
+    zero, one = jnp.zeros((), BF16), jnp.ones((), BF16)
+    line = lax.broadcasted_iota(jnp.int32, (slab, count), 0).astype(F32).astype(BF16)
+
+    def level(row):
+        return jnp.broadcast_to(row, (slab, count)).astype(BF16)
+
+    def one_hot(row):
+        target = level(row)
+        tiles = [line + jnp.asarray(at, BF16) == target for at in range(0, LANES, slab)]
+        return jnp.concatenate([jnp.where(tile, one, zero) for tile in tiles])
+
     def place(p):
         waves = waves_ref[p].astype(F32)
-        place = waves[2 * bands : 2 * bands + 8].astype(jnp.int32)
-        first, second, third = place[0:1], place[1:2], place[2:3]
-        line = lax.broadcasted_iota(jnp.int32, (LANES, count), 0)
-        pick = jnp.where(line == second, 1.0, 0.0).astype(BF16)
-        turn = jnp.dot(near, pick, preferred_element_type=F32)
-        pick = jnp.where(line == third, 1.0, 0.0).astype(BF16)
+        first, second, third = [
+            jnp.concatenate([waves[i : i + 1, count:], waves[i + 1 : i + 2, count:]], axis=1)
+            for i in (0, 2, 4)
+        ]
+        turn = jnp.dot(near, one_hot(second), preferred_element_type=F32)
+        pick = one_hot(third)
         phase_s[p] = jnp.dot(
             third_ref[...], jnp.concatenate([pick, pick]), preferred_element_type=F32
         )
         centre = turn[rows : rows + 2] + turn[rows + 2 : rows + 4]
         centres.append(centre)
-        real, imag = waves[:bands], waves[bands : 2 * bands]
+        real, imag = waves[:bands, :count], waves[bands:, :count]
         squares.append(real * real + imag * imag)
         turned_real = real * centre[0:1] - imag * centre[1:2]
         turned_imag = real * centre[1:2] + imag * centre[0:1]
-        inside = lax.broadcasted_iota(jnp.int32, (slab, count), 0) == first
-        sign = jnp.where(lax.rem(third, 2) == 0, 1.0, -1.0)
-        near_turn, far_turn = turn[:rows], turn[:rows] * sign
+        inside = line == level(first)
+        sign = level(jnp.where(lax.rem(third.astype(jnp.int32), 2) == 0, 1.0, -1.0))
         for k in range(rows):
-            at = slice(k * slab, (k + 1) * slab)
-            select_s[p, at, :] = jnp.where(inside, near_turn[k : k + 1], 0.0).astype(BF16)
-            at = slice(full + k * slab, full + (k + 1) * slab)
-            select_s[p, at, :] = jnp.where(inside, far_turn[k : k + 1], 0.0).astype(BF16)
+            chosen = jnp.where(inside, level(turn[k : k + 1]), zero)
+            select_s[p, k * slab : (k + 1) * slab, :] = chosen
+            select_s[p, full + k * slab : full + (k + 1) * slab, :] = chosen * sign
         return turned_real, turned_imag
 
     def weigh(p, g, turned):
@@ -251,7 +263,7 @@
         store.start()
 
     waves = waves_ref[me].astype(F32)
-    real, imag = waves[:bands], waves[bands : 2 * bands]
+    real, imag = waves[:bands, :count], waves[bands:, :count]
     kinetic = kinetic_ref[...].reshape(1, count)
     moving = jnp.sum((real * real + imag * imag) * kinetic, axis=1, keepdims=True)
     energy = []
@@ -267,7 +279,7 @@
         low = (value - high.astype(F32)).astype(BF16)
         both = jnp.concatenate([high.astype(F32), low.astype(F32)])
         scalars.append(jnp.broadcast_to(both, (2 * bands, LANES)))
-    scalars = jnp.concatenate(scalars, axis=1).astype(BF16)
+    scalars = jnp.where(low_lanes, *scalars).astype(BF16)
 
     for p in range(devices):
         cosines, sines = phase_s[p, :fold], phase_s[p, fold:]
@@ -290,14 +302,16 @@
         cosine, sine = centres[p][0:1], centres[p][1:2]
         result = jnp.concatenate([real * cosine + imag * sine, imag * cosine - real * sine])
         sent_ref[p, :, :count] = result.astype(BF16)
-        sent_ref[p, :, count:] = scalars
+        sent_ref[p, :, count : count + LANES] = scalars
+        sent_ref[p, :, count + LANES :] = jnp.zeros_like(scalars)
 
     for store in stores:
         store.wait()
 
 
 def on_grid(waves, potential, kinetic, occupation, bands, width_second):
-    devices, _, count = waves.shape
+    devices, _, length = waves.shape
+    count = 2 * length // 3
     rows, width_first, width_third = potential.shape
     slab = width_first // devices
     tables = wave_tables(devices, rows, width_first, width_second, width_third)
@@ -336,7 +350,7 @@
     total = sum(arrived_ref[p].astype(F32) for p in range(devices))
     applied = total[:, :count]
     scalars = total[:bands, count:] + total[bands:, count:]
-    ratio = scalars[:, 0:1] / (scalars[:, LANES : LANES + 1] + EPSILON)
+    ratio = scalars[:, 0:1] / (scalars[:, LANES // 2 : LANES // 2 + 1] + EPSILON)
     kinetic = kinetic_ref[...].reshape(1, count)
     damping = 1.0 / (1.0 + kinetic)
     trial = jnp.concatenate([trial_ref[part].astype(F32) for part in range(2)])
@@ -416,7 +430,7 @@
     params = pltpu.CompilerParams(vmem_limit_bytes=16 * 1024 * 1024)
     packets = pl.pallas_call(
         functools.partial(pack_kernel, bands, devices, width_second, width_third),
-        out_shape=jax.ShapeDtypeStruct((devices, 16, count), BF16),
+        out_shape=jax.ShapeDtypeStruct((devices, block, 3 * count // 2), BF16),
         in_specs=[vmem] * 2,
         out_specs=vmem,
         compiler_params=pltpu.CompilerParams(vmem_limit_bytes=56 * 1024 * 1024),
@@ -483,7 +497,7 @@
         and width_second == LANES
         and width_third == LANES
         and bands == 4
-        and trial_block.shape[2] // devices % LANES == 0
+        and trial_block.shape[2] // devices % (2 * LANES) == 0
     )
 
 

time: 60 us -> 59 us (0.983)
  no operation moved by 1% of the time
where the time goes in v6:
time: 59 us; the launch traced here: 58.7 us
  waiting for transfers between devices  21.4 us (36%)
  Pallas kernels  16.8 us (28%)
  starting transfers between devices  15.4 us (26%)
  local copies, waits for them, and re-layouts  3.24 us (5%)
  other arithmetic  1.1 us (2%)
  between operations  0.74 us (1%)
    pallas_call x1, Pallas kernels, on_grid(): pl.pallas_call(functools.partial(grid_kernel, bands), out_shape=(jax.Shap...  13 us
    ppermute x7, waiting for transfers between devices, swap(): return lax.ppermute(values, axis, [(i, i ^ bit) for i in range(size)])  9.28 us
    all_to_all x1, starting transfers between devices, in_waves(): lax.all_to_all(packets, 'pw', split_axis=0, concat_axis=0, tiled=True)  7.25 us
    all_to_all x1, waiting for transfers between devices, in_waves(): lax.all_to_all(partial, 'pw', split_axis=0, concat_axis=0, tiled=True)  7.2 us
    all_to_all x1, waiting for transfers between devices, in_waves(): lax.all_to_all(packets, 'pw', split_axis=0, concat_axis=0, tiled=True)  4.9 us
    ppermute x7, starting transfers between devices, swap(): return lax.ppermute(values, axis, [(i, i ^ bit) for i in range(size)])  4.81 us
    all_to_all x1, starting transfers between devices, in_waves(): lax.all_to_all(partial, 'pw', split_axis=0, concat_axis=0, tiled=True)  3.38 us
    unnamed x15, local copies, waits for them, and re-layouts  3.24 us
  transfers between devices with their start and end apart: 9, of which 7 were waited for; matrix products, arithmetic and copies ran while one was open for 5% of the time, Pallas kernels for 0%

profile of v6, /device:TPU:0, one launch (start us, length us, event | category | flops | bytes accessed | tf_op | source)
XLA Modules:
  0.0 58.7 jit_solution(13447705941991021410)
XLA Ops:
  0.6 0.0 copy-start.2
  0.6 0.0 copy-start.3
  0.7 0.0 copy-start
  0.7 1.5 %shard_map.130 = bf16[8,8,1152]{2,1,0:T(8,128)(2,1)} custom-call(bf16[2,4,768]{2,1,0:T(4,128)(2,1)} %trial_ref.3, s32[768]{0:T(1024)} %cells_ref.1), custom_call_target="tpu_custom_call" | custom-call | tf_op jit(solution)/shard_map/pallas_call | solution.py:431
  2.2 7.3 %all-to-all-start = ((bf16[8,8,1152]{2,1,0:T(8,128)(2,1)}), bf16[8,8,1152]{2,1,0:T(8,128)(2,1)S(1)}, u32[]{:S(2)}, u32[]{:S(2)}) async-start(bf16[8,8,1152]{2,1,0:T(8,128)(2,1)} %shard_map.130), calls=%async_computation | async-start | bytes 294912 | tf_op jit(solution)/shard_map/all_to_all | solution.py:438
  9.5 2.5 %copy.23 = f32[128,16,128]{2,0,1:T(8,128)} copy(f32[128,16,128]{2,1,0:T(8,128)} %param.13) | data formatting | bytes 2097152 | tf_op args[2]
  12.0 4.9 %all-to-all-done.waves_ref = bf16[8,8,1152]{2,1,0:T(8,128)(2,1)S(1)} async-done(((bf16[8,8,1152]{2,1,0:T(8,128)(2,1)}), bf16[8,8,1152]{2,1,0:T(8,128)(2,1)S(1)}, u32[]{:S(2)}, u32[]{:S(2)}) %all-to-all-start) | async-done | bytes 147488 | tf_op jit(solution)/shard_map/all_to_all | solution.py:438
  16.9 0.0 copy-start.4
  16.9 0.7 %copy-done.4 = bf16[8,8,1152]{2,1,0:T(8,128)(2,1)} copy-done((bf16[8,8,1152]{2,1,0:T(8,128)(2,1)}, bf16[8,8,1152]{2,1,0:T(8,128)(2,1)S(1)}, u32[]{:S(2)}) %copy-start.4) | copy-done | bytes 147480
  17.6 13.0 %shard_map.131 = (bf16[8,8,1024]{2,1,0:T(8,128)(2,1)}, f32[16,64,128]{2,1,0:T(8,128)}, bf16[16,64,128]{2,1,0:T(8,128)(2,1)}) custom-call(bf16[8,8,1152]{2,1,0:T(8,128)(2,1)} %copy-done.4, bf16[8,32,128]{2,1,0:T(8,128)(2,1)} %constant.8.clone.second_ref, bf16[128,256]{1,0:T(8,128)(2,1)} %constant.9.clone.third_ref, bf16[256,256]{1,0:T(8,128)(2,1)} %constant.10.clone.back_ref, ...), custom_call_target="tpu_custom_call" | custom-call | tf_op jit(solution)/shard_map/pallas_call | solution.py:322
  30.6 3.4 %all-to-all-start.1 = ((bf16[8,8,1024]{2,1,0:T(8,128)(2,1)}), bf16[8,8,1024]{2,1,0:T(8,128)(2,1)S(1)}, u32[]{:S(2)}, u32[]{:S(2)}) async-start(bf16[8,8,1024]{2,1,0:T(8,128)(2,1)} %get-tuple-element.13), calls=%async_computation.1 | async-start | bytes 262144 | tf_op jit(solution)/shard_map/all_to_all | solution.py:442
  34.0 0.1 collective-permute-start.1
  34.0 7.2 %all-to-all-done.1.arrived_ref = bf16[8,8,1024]{2,1,0:T(8,128)(2,1)S(1)} async-done(((bf16[8,8,1024]{2,1,0:T(8,128)(2,1)}), bf16[8,8,1024]{2,1,0:T(8,128)(2,1)S(1)}, u32[]{:S(2)}, u32[]{:S(2)}) %all-to-all-start.1) | async-done | bytes 131104 | tf_op jit(solution)/shard_map/all_to_all | solution.py:442
  41.2 0.0 copy-done.2
  41.2 0.0 copy-done.3
  41.2 0.0 copy-start.5
  41.3 0.0 copy-start.6
  41.3 0.2 shard_map.132
  41.4 0.0 collective-permute-start
  41.4 0.0 collective-permute-done.1.received_ref
  41.5 1.2 %collective-permute-done.theirs_ref = bf16[32,896]{1,0:T(8,128)(2,1)S(1)} collective-permute-done((bf16[32,896]{1,0:T(8,128)(2,1)S(1)}, bf16[32,896]{1,0:T(8,128)(2,1)S(1)}, u32[]{:S(2)}, u32[]{:S(2)}) %collective-permute-start) | collective-permute-done | bytes 57376 | tf_op jit(solution)/shard_map/ppermute | solution.py:418
  42.7 0.0 copy-done
  42.7 1.0 %shard_map.133 = (bf16[32,1024]{1,0:T(8,128)(2,1)S(1)}, bf16[16,64,128]{2,1,0:T(8,128)(2,1)S(1)}) custom-call(bf16[32,896]{1,0:T(8,128)(2,1)S(1)} %get-tuple-element.14.mine_ref, bf16[32,896]{1,0:T(8,128)(2,1)S(1)} %collective-permute-done.theirs_ref, bf16[2,1024,768]{2,1,0:T(8,128)(2,1)S(1)} %copy-done, ...), custom_call_target="tpu_custom_call", output_to_operand_aliasing={{1}: (3, {})} | custom-call | tf_op jit(solution)/shard_map/pallas_call | solution.py:455
  43.7 0.3 collective-permute-start.2
  44.0 4.1 %collective-permute-done.2 = bf16[32,1024]{1,0:T(8,128)(2,1)S(1)} collective-permute-done((bf16[32,1024]{1,0:T(8,128)(2,1)S(1)}, bf16[32,1024]{1,0:T(8,128)(2,1)S(1)}, u32[]{:S(2)}, u32[]{:S(2)}) %collective-permute-start.2) | collective-permute-done | bytes 65568 | tf_op jit(solution)/shard_map/ppermute | solution.py:418
  48.1 0.6 %collective-permute-start.5 = (bf16[32,1024]{1,0:T(8,128)(2,1)S(1)}, bf16[32,1024]{1,0:T(8,128)(2,1)S(1)}, u32[]{:S(2)}, u32[]{:S(2)}) collective-permute-start(bf16[32,1024]{1,0:T(8,128)(2,1)S(1)} %add.9.refs_0_), channel_id=1, source_target_pairs={{0,12},{2,14},{4,8},{6,10},{8,4},{10,6},{12,0},{14,2},{1,13},{3,15... | collective-permute-start | bytes 196616 | tf_op jit(solution)/shard_map/ppermute | solution.py:418
  48.7 0.8 %collective-permute-start.4 = (bf16[32,1024]{1,0:T(8,128)(2,1)S(1)}, bf16[32,1024]{1,0:T(8,128)(2,1)S(1)}, u32[]{:S(2)}, u32[]{:S(2)}) collective-permute-start(bf16[32,1024]{1,0:T(8,128)(2,1)S(1)} %add.9.refs_0_), channel_id=1, source_target_pairs={{0,8},{2,10},{4,12},{6,14},{8,0},{10,2},{12,4},{14,6},{1,9},{3,11}... | collective-permute-start | bytes 196616 | tf_op jit(solution)/shard_map/ppermute | solution.py:418
  49.5 3.1 %collective-permute-start.3 = (bf16[32,1024]{1,0:T(8,128)(2,1)S(1)}, bf16[32,1024]{1,0:T(8,128)(2,1)S(1)}, u32[]{:S(2)}, u32[]{:S(2)}) collective-permute-start(bf16[32,1024]{1,0:T(8,128)(2,1)S(1)} %add.9.refs_0_), channel_id=1, source_target_pairs={{0,4},{2,6},{4,0},{6,2},{8,12},{10,14},{12,8},{14,10},{1,5},{3,7},... | collective-permute-start | bytes 196616 | tf_op jit(solution)/shard_map/ppermute | solution.py:418
  52.5 0.0 copy-done.5
  52.5 0.0 copy-done.6
  52.5 0.5 bitcast_add_fusion.refs_6_
  53.0 0.0 copy-start.1
  53.0 1.5 %collective-permute-done.5.refs_3_ = bf16[32,1024]{1,0:T(8,128)(2,1)S(1)} collective-permute-done((bf16[32,1024]{1,0:T(8,128)(2,1)S(1)}, bf16[32,1024]{1,0:T(8,128)(2,1)S(1)}, u32[]{:S(2)}, u32[]{:S(2)}) %collective-permute-start.5) | collective-permute-done | bytes 65568 | tf_op jit(solution)/shard_map/ppermute | solution.py:418
  54.5 1.3 %collective-permute-done.4.refs_2_ = bf16[32,1024]{1,0:T(8,128)(2,1)S(1)} collective-permute-done((bf16[32,1024]{1,0:T(8,128)(2,1)S(1)}, bf16[32,1024]{1,0:T(8,128)(2,1)S(1)}, u32[]{:S(2)}, u32[]{:S(2)}) %collective-permute-start.4) | collective-permute-done | bytes 65568 | tf_op jit(solution)/shard_map/ppermute | solution.py:418
  55.8 0.0 collective-permute-done.3.refs_1_
  55.8 1.1 %shard_map.134 = (f32[16,1024]{1,0:T(8,128)}, f32[2,4,768]{2,1,0:T(4,128)S(1)}, f32[2,4,768]{2,1,0:T(4,128)S(1)}) custom-call(bf16[32,1024]{1,0:T(8,128)(2,1)S(1)} %add.9.refs_0_, bf16[32,1024]{1,0:T(8,128)(2,1)S(1)} %collective-permute-done.3.refs_1_, bf16[32,1024]{1,0:T(8,128)(2,1)S(1)} %collective-permute-done.4.refs_2_, ...), custom_call_target="tpu_custom_call" | custom-call | tf_op jit(solution)/shard_map/pallas_call | solution.py:469
  56.9 0.0 collective-permute-start.6
  56.9 1.2 %collective-permute-done.6 = f32[2,4,768]{2,1,0:T(4,128)S(1)} collective-permute-done((f32[2,4,768]{2,1,0:T(4,128)S(1)}, f32[2,4,768]{2,1,0:T(4,128)S(1)}, u32[]{:S(2)}, u32[]{:S(2)}) %collective-permute-start.6) | collective-permute-done | bytes 24608 | tf_op jit(solution)/shard_map/ppermute | solution.py:418
  58.1 0.6 %sub.3 = f32[2,4,768]{2,1,0:T(4,128)} subtract(f32[2,4,768]{2,1,0:T(4,128)S(1)} %get-tuple-element.20, f32[2,4,768]{2,1,0:T(4,128)S(1)} %collective-permute-done.6) | non-fusion elementwise | flops 6144 | bytes 73728 | tf_op jit(solution)/shard_map/sub | solution.py:480
  58.7 0.0 copy-done.1
  (1 shorter events, 0.0 us)
Async XLA Ops:
  0.6 40.6 %copy-start.2 = (bf16[2,4,768]{2,1,0:T(4,128)(2,1)S(1)}, bf16[2,4,768]{2,1,0:T(4,128)(2,1)}, u32[]{:S(2)}) copy-start(bf16[2,4,768]{2,1,0:T(4,128)(2,1)} %trial_ref.3) | copy-start | bytes 36868
  0.6 40.6 %copy-start.3 = (f32[768]{0:T(1024)S(1)}, f32[768]{0:T(1024)}, u32[]{:S(2)}) copy-start(f32[768]{0:T(1024)} %kinetic_ref.3) | copy-start | bytes 9220
  0.7 42.0 %copy-start = (bf16[2,1024,768]{2,1,0:T(8,128)(2,1)S(1)}, bf16[2,1024,768]{2,1,0:T(8,128)(2,1)}, u32[]{:S(2)}) copy-start(bf16[2,1024,768]{2,1,0:T(8,128)(2,1)} %refs_4_.1) | copy-start | bytes 9437188
  2.2 14.7 %all-to-all-start = ((bf16[8,8,1152]{2,1,0:T(8,128)(2,1)}), bf16[8,8,1152]{2,1,0:T(8,128)(2,1)S(1)}, u32[]{:S(2)}, u32[]{:S(2)}) async-start(bf16[8,8,1152]{2,1,0:T(8,128)(2,1)} %shard_map.130), calls=%async_computation | async-start | bytes 294912 | tf_op jit(solution)/shard_map/all_to_all | solution.py:438
  16.9 0.7 %copy-start.4 = (bf16[8,8,1152]{2,1,0:T(8,128)(2,1)}, bf16[8,8,1152]{2,1,0:T(8,128)(2,1)S(1)}, u32[]{:S(2)}) copy-start(bf16[8,8,1152]{2,1,0:T(8,128)(2,1)S(1)} %all-to-all-done.waves_ref) | copy-start | bytes 442372
  30.6 10.7 %all-to-all-start.1 = ((bf16[8,8,1024]{2,1,0:T(8,128)(2,1)}), bf16[8,8,1024]{2,1,0:T(8,128)(2,1)S(1)}, u32[]{:S(2)}, u32[]{:S(2)}) async-start(bf16[8,8,1024]{2,1,0:T(8,128)(2,1)} %get-tuple-element.13), calls=%async_computation.1 | async-start | bytes 262144 | tf_op jit(solution)/shard_map/all_to_all | solution.py:442
  34.0 7.5 %collective-permute-start.1 = (bf16[16,64,128]{2,1,0:T(8,128)(2,1)}, bf16[16,64,128]{2,1,0:T(8,128)(2,1)S(1)}, u32[]{:S(2)}, u32[]{:S(2)}) collective-permute-start(bf16[16,64,128]{2,1,0:T(8,128)(2,1)} %get-tuple-element.15), channel_id=1, source_target_pairs={{0,1},{1,0},{2,3},{3,2},{4,5},{5,4},{6,7},{7,6},{8,9},{9,8},{10,11... | collective-permute-start | bytes 786440 | tf_op jit(solution)/shard_map/ppermute | solution.py:418
  41.2 11.3 %copy-start.5 = (f32[64,16,128]{2,1,0:T(8,128)S(1)}, f32[64,16,128]{2,1,0:T(8,128)}, u32[]{:S(2)}) copy-start(f32[64,16,128]{2,1,0:T(8,128)} %param.14) | copy-start | bytes 1572868
  41.3 11.3 %copy-start.6 = (f32[16,64,128]{2,1,0:T(8,128)S(1)}, f32[16,64,128]{2,1,0:T(8,128)}, u32[]{:S(2)}) copy-start(f32[16,64,128]{2,1,0:T(8,128)} %get-tuple-element.18) | copy-start | bytes 1572868
  41.4 1.2 %collective-permute-start = (bf16[32,896]{1,0:T(8,128)(2,1)S(1)}, bf16[32,896]{1,0:T(8,128)(2,1)S(1)}, u32[]{:S(2)}, u32[]{:S(2)}) collective-permute-start(bf16[32,896]{1,0:T(8,128)(2,1)S(1)} %get-tuple-element.14.mine_ref), channel_id=1, source_target_pairs={{0,1},{1,0},{2,3},{3,2},{4,5},{5,4},{6,7},{7,6},{8,9},{9,8},{10,11... | collective-permute-start | bytes 172040 | tf_op jit(solution)/shard_map/ppermute | solution.py:418
  43.7 4.3 %collective-permute-start.2 = (bf16[32,1024]{1,0:T(8,128)(2,1)S(1)}, bf16[32,1024]{1,0:T(8,128)(2,1)S(1)}, u32[]{:S(2)}, u32[]{:S(2)}) collective-permute-start(bf16[32,1024]{1,0:T(8,128)(2,1)S(1)} %get-tuple-element.16), channel_id=1, source_target_pairs={{0,2},{2,0},{4,6},{6,4},{8,10},{10,8},{12,14},{14,12},{1,3},{3,1},... | collective-permute-start | bytes 196616 | tf_op jit(solution)/shard_map/ppermute | solution.py:418
  48.1 6.5 %collective-permute-start.5 = (bf16[32,1024]{1,0:T(8,128)(2,1)S(1)}, bf16[32,1024]{1,0:T(8,128)(2,1)S(1)}, u32[]{:S(2)}, u32[]{:S(2)}) collective-permute-start(bf16[32,1024]{1,0:T(8,128)(2,1)S(1)} %add.9.refs_0_), channel_id=1, source_target_pairs={{0,12},{2,14},{4,8},{6,10},{8,4},{10,6},{12,0},{14,2},{1,13},{3,15... | collective-permute-start | bytes 196616 | tf_op jit(solution)/shard_map/ppermute | solution.py:418
  48.7 7.1 %collective-permute-start.4 = (bf16[32,1024]{1,0:T(8,128)(2,1)S(1)}, bf16[32,1024]{1,0:T(8,128)(2,1)S(1)}, u32[]{:S(2)}, u32[]{:S(2)}) collective-permute-start(bf16[32,1024]{1,0:T(8,128)(2,1)S(1)} %add.9.refs_0_), channel_id=1, source_target_pairs={{0,8},{2,10},{4,12},{6,14},{8,0},{10,2},{12,4},{14,6},{1,9},{3,11}... | collective-permute-start | bytes 196616 | tf_op jit(solution)/shard_map/ppermute | solution.py:418
  49.5 6.4 %collective-permute-start.3 = (bf16[32,1024]{1,0:T(8,128)(2,1)S(1)}, bf16[32,1024]{1,0:T(8,128)(2,1)S(1)}, u32[]{:S(2)}, u32[]{:S(2)}) collective-permute-start(bf16[32,1024]{1,0:T(8,128)(2,1)S(1)} %add.9.refs_0_), channel_id=1, source_target_pairs={{0,4},{2,6},{4,0},{6,2},{8,12},{10,14},{12,8},{14,10},{1,5},{3,7},... | collective-permute-start | bytes 196616 | tf_op jit(solution)/shard_map/ppermute | solution.py:418
  53.0 5.7 %copy-start.1 = (f32[64,16,128]{2,1,0:T(8,128)}, f32[64,16,128]{2,1,0:T(8,128)S(1)}, u32[]{:S(2)}) copy-start(f32[64,16,128]{2,1,0:T(8,128)S(1)} %bitcast_add_fusion.refs_6_) | copy-start | bytes 1572868
  56.9 1.2 %collective-permute-start.6 = (f32[2,4,768]{2,1,0:T(4,128)S(1)}, f32[2,4,768]{2,1,0:T(4,128)S(1)}, u32[]{:S(2)}, u32[]{:S(2)}) collective-permute-start(f32[2,4,768]{2,1,0:T(4,128)S(1)} %get-tuple-element.21), channel_id=1, source_target_pairs={{0,1},{1,0},{2,3},{3,2},{4,5},{5,4},{6,7},{7,6},{8,9},{9,8},{10,11... | collective-permute-start | bytes 73736 | tf_op jit(solution)/shard_map/ppermute | solution.py:418

commit v7 on v6

--- a/solution.py
+++ b/solution.py
@@ -396,12 +396,11 @@
 
 
 def project_kernel(bands, parts, *refs):
-    terms, (all_ref, rest_ref, _, correlation_ref, own_ref, sent_ref) = refs[:parts], refs[parts:]
+    terms, (all_ref, rest_ref, _, own_ref, sent_ref) = refs[:parts], refs[parts:]
     block = 2 * bands
     first = lax.axis_index("band") == 0
-    total = sum(term[...].astype(F32) for term in terms)
-    correlation_ref[...] = total[: 2 * block]
-    coefficients = total[2 * block :].astype(BF16)
+    total = sum(term[2 * block :].astype(F32) for term in terms)
+    coefficients = total.astype(BF16)
     one = jnp.dot(coefficients, all_ref[0], preferred_element_type=F32)
     two = jnp.dot(coefficients, all_ref[1], preferred_element_type=F32)
     real = one[:block] - two[block:]
@@ -466,15 +465,15 @@
     density = rest_density + (density_own + received.astype(F32)).transpose(1, 0, 2)
     near = sums + swap(sums, "pw", 1)
     terms = [near] + [swap(near, "pw", step) for step in range(2, devices, 2)]
-    correlation, own, sent = pl.pallas_call(
+    correlation = sum(term[: 2 * block].astype(F32) for term in terms)
+    own, sent = pl.pallas_call(
         functools.partial(project_kernel, bands, len(terms)),
         out_shape=(
-            jax.ShapeDtypeStruct((2 * block, states), F32),
             jax.ShapeDtypeStruct((2, bands, count), F32),
             jax.ShapeDtypeStruct((2, bands, count), F32),
         ),
         in_specs=[vmem] * (len(terms) + 2) + [anywhere],
-        out_specs=(vmem, vmem, vmem),
+        out_specs=(vmem, vmem),
         compiler_params=params,
     )(*terms, all_bands, rest, density)
     correction = own - swap(sent, "band", 1)

time: 59 us -> 58.6 us (level)
  waiting for transfers between devices: 21.4 us -> 20.7 us
  other arithmetic: 1.1 us -> 1.75 us
    ppermute x7, waiting for transfers between devices: 9.28 us -> 8.62 us  [swap(): return lax.ppermute(values, axis, [(i, i ^ bit) for i in range(size)])]
    transpose x0 -> x1, other arithmetic: none -> 0.65 us  [in_waves(): correlation = correlation.reshape(2, block, states).transpose(0, 2, 1)]
  transfers between devices with their start and end apart: 9 -> 9, of which waited for: 7 -> 7; matrix products, arithmetic and copies ran while one was open for 5% -> 6% of each run, Pallas kernels for 0% -> 0%
where the time goes in v7:
time: 58.6 us; the launch traced here: 58.2 us
  waiting for transfers between devices  20.7 us (35%)
  Pallas kernels  16.3 us (28%)
  starting transfers between devices  15.5 us (26%)
  local copies, waits for them, and re-layouts  3.24 us (6%)
  other arithmetic  1.75 us (3%)
  between operations  0.75 us (1%)
    pallas_call x1, Pallas kernels, on_grid(): pl.pallas_call(functools.partial(grid_kernel, bands), out_shape=(jax.Shap...  13 us
    ppermute x7, waiting for transfers between devices, swap(): return lax.ppermute(values, axis, [(i, i ^ bit) for i in range(size)])  8.62 us
    all_to_all x1, starting transfers between devices, in_waves(): lax.all_to_all(packets, 'pw', split_axis=0, concat_axis=0, tiled=True)  7.25 us
    all_to_all x1, waiting for transfers between devices, in_waves(): lax.all_to_all(partial, 'pw', split_axis=0, concat_axis=0, tiled=True)  7.2 us
    all_to_all x1, waiting for transfers between devices, in_waves(): lax.all_to_all(packets, 'pw', split_axis=0, concat_axis=0, tiled=True)  4.9 us
    ppermute x7, starting transfers between devices, swap(): return lax.ppermute(values, axis, [(i, i ^ bit) for i in range(size)])  4.88 us
    all_to_all x1, starting transfers between devices, in_waves(): lax.all_to_all(partial, 'pw', split_axis=0, concat_axis=0, tiled=True)  3.38 us
    unnamed x15, local copies, waits for them, and re-layouts  3.24 us
  transfers between devices with their start and end apart: 9, of which 7 were waited for; matrix products, arithmetic and copies ran while one was open for 6% of the time, Pallas kernels for 0%

profile of v7, /device:TPU:0, one launch (start us, length us, event | category | flops | bytes accessed | tf_op | source)
XLA Modules:
  0.0 58.2 jit_solution(9368858536169120762)
XLA Ops:
  0.6 0.0 copy-start.2
  0.6 0.0 copy-start.3
  0.7 0.0 copy-start
  0.7 1.5 %shard_map.130 = bf16[8,8,1152]{2,1,0:T(8,128)(2,1)} custom-call(bf16[2,4,768]{2,1,0:T(4,128)(2,1)} %trial_ref.3, s32[768]{0:T(1024)} %cells_ref.1), custom_call_target="tpu_custom_call" | custom-call | tf_op jit(solution)/shard_map/pallas_call | solution.py:430
  2.2 7.3 %all-to-all-start = ((bf16[8,8,1152]{2,1,0:T(8,128)(2,1)}), bf16[8,8,1152]{2,1,0:T(8,128)(2,1)S(1)}, u32[]{:S(2)}, u32[]{:S(2)}) async-start(bf16[8,8,1152]{2,1,0:T(8,128)(2,1)} %shard_map.130), calls=%async_computation | async-start | bytes 294912 | tf_op jit(solution)/shard_map/all_to_all | solution.py:437
  9.5 2.5 %copy.23 = f32[128,16,128]{2,0,1:T(8,128)} copy(f32[128,16,128]{2,1,0:T(8,128)} %param.13) | data formatting | bytes 2097152 | tf_op args[2]
  12.0 4.9 %all-to-all-done.waves_ref = bf16[8,8,1152]{2,1,0:T(8,128)(2,1)S(1)} async-done(((bf16[8,8,1152]{2,1,0:T(8,128)(2,1)}), bf16[8,8,1152]{2,1,0:T(8,128)(2,1)S(1)}, u32[]{:S(2)}, u32[]{:S(2)}) %all-to-all-start) | async-done | bytes 147488 | tf_op jit(solution)/shard_map/all_to_all | solution.py:437
  16.9 0.0 copy-start.4
  16.9 0.7 %copy-done.4 = bf16[8,8,1152]{2,1,0:T(8,128)(2,1)} copy-done((bf16[8,8,1152]{2,1,0:T(8,128)(2,1)}, bf16[8,8,1152]{2,1,0:T(8,128)(2,1)S(1)}, u32[]{:S(2)}) %copy-start.4) | copy-done | bytes 147480
  17.6 13.0 %shard_map.131 = (bf16[8,8,1024]{2,1,0:T(8,128)(2,1)}, f32[16,64,128]{2,1,0:T(8,128)}, bf16[16,64,128]{2,1,0:T(8,128)(2,1)}) custom-call(bf16[8,8,1152]{2,1,0:T(8,128)(2,1)} %copy-done.4, bf16[8,32,128]{2,1,0:T(8,128)(2,1)} %constant.8.clone.second_ref, bf16[128,256]{1,0:T(8,128)(2,1)} %constant.9.clone.third_ref, bf16[256,256]{1,0:T(8,128)(2,1)} %constant.10.clone.back_ref, ...), custom_call_target="tpu_custom_call" | custom-call | tf_op jit(solution)/shard_map/pallas_call | solution.py:322
  30.6 3.4 %all-to-all-start.1 = ((bf16[8,8,1024]{2,1,0:T(8,128)(2,1)}), bf16[8,8,1024]{2,1,0:T(8,128)(2,1)S(1)}, u32[]{:S(2)}, u32[]{:S(2)}) async-start(bf16[8,8,1024]{2,1,0:T(8,128)(2,1)} %get-tuple-element.12), calls=%async_computation.1 | async-start | bytes 262144 | tf_op jit(solution)/shard_map/all_to_all | solution.py:441
  34.0 0.1 collective-permute-start.1
  34.0 7.2 %all-to-all-done.1.arrived_ref = bf16[8,8,1024]{2,1,0:T(8,128)(2,1)S(1)} async-done(((bf16[8,8,1024]{2,1,0:T(8,128)(2,1)}), bf16[8,8,1024]{2,1,0:T(8,128)(2,1)S(1)}, u32[]{:S(2)}, u32[]{:S(2)}) %all-to-all-start.1) | async-done | bytes 131104 | tf_op jit(solution)/shard_map/all_to_all | solution.py:441
  41.2 0.0 copy-done.2
  41.2 0.0 copy-done.3
  41.2 0.0 copy-start.5
  41.3 0.0 copy-start.6
  41.3 0.2 shard_map.132
  41.4 0.0 collective-permute-start
  41.4 0.0 collective-permute-done.1.received_ref
  41.5 1.2 %collective-permute-done.theirs_ref = bf16[32,896]{1,0:T(8,128)(2,1)S(1)} collective-permute-done((bf16[32,896]{1,0:T(8,128)(2,1)S(1)}, bf16[32,896]{1,0:T(8,128)(2,1)S(1)}, u32[]{:S(2)}, u32[]{:S(2)}) %collective-permute-start) | collective-permute-done | bytes 57376 | tf_op jit(solution)/shard_map/ppermute | solution.py:417
  42.7 0.0 copy-done
  42.7 1.0 %shard_map.133 = (bf16[32,1024]{1,0:T(8,128)(2,1)S(1)}, bf16[16,64,128]{2,1,0:T(8,128)(2,1)S(1)}) custom-call(bf16[32,896]{1,0:T(8,128)(2,1)S(1)} %get-tuple-element.13.mine_ref, bf16[32,896]{1,0:T(8,128)(2,1)S(1)} %collective-permute-done.theirs_ref, bf16[2,1024,768]{2,1,0:T(8,128)(2,1)S(1)} %copy-done, ...), custom_call_target="tpu_custom_call", output_to_operand_aliasing={{1}: (3, {})} | custom-call | tf_op jit(solution)/shard_map/pallas_call | solution.py:454
  43.7 0.3 collective-permute-start.2
  44.0 4.1 %collective-permute-done.2 = bf16[32,1024]{1,0:T(8,128)(2,1)S(1)} collective-permute-done((bf16[32,1024]{1,0:T(8,128)(2,1)S(1)}, bf16[32,1024]{1,0:T(8,128)(2,1)S(1)}, u32[]{:S(2)}, u32[]{:S(2)}) %collective-permute-start.2) | collective-permute-done | bytes 65568 | tf_op jit(solution)/shard_map/ppermute | solution.py:417
  48.1 0.6 %collective-permute-start.5 = (bf16[32,1024]{1,0:T(8,128)(2,1)S(1)}, bf16[32,1024]{1,0:T(8,128)(2,1)S(1)}, u32[]{:S(2)}, u32[]{:S(2)}) collective-permute-start(bf16[32,1024]{1,0:T(8,128)(2,1)S(1)} %add.18.refs_0_), channel_id=1, source_target_pairs={{0,12},{2,14},{4,8},{6,10},{8,4},{10,6},{12,0},{14,2},{1,13},{3,15... | collective-permute-start | bytes 196616 | tf_op jit(solution)/shard_map/ppermute | solution.py:417
  48.7 0.8 %collective-permute-start.4 = (bf16[32,1024]{1,0:T(8,128)(2,1)S(1)}, bf16[32,1024]{1,0:T(8,128)(2,1)S(1)}, u32[]{:S(2)}, u32[]{:S(2)}) collective-permute-start(bf16[32,1024]{1,0:T(8,128)(2,1)S(1)} %add.18.refs_0_), channel_id=1, source_target_pairs={{0,8},{2,10},{4,12},{6,14},{8,0},{10,2},{12,4},{14,6},{1,9},{3,11}... | collective-permute-start | bytes 196616 | tf_op jit(solution)/shard_map/ppermute | solution.py:417
  49.5 3.1 %collective-permute-start.3 = (bf16[32,1024]{1,0:T(8,128)(2,1)S(1)}, bf16[32,1024]{1,0:T(8,128)(2,1)S(1)}, u32[]{:S(2)}, u32[]{:S(2)}) collective-permute-start(bf16[32,1024]{1,0:T(8,128)(2,1)S(1)} %add.18.refs_0_), channel_id=1, source_target_pairs={{0,4},{2,6},{4,0},{6,2},{8,12},{10,14},{12,8},{14,10},{1,5},{3,7},... | collective-permute-start | bytes 196616 | tf_op jit(solution)/shard_map/ppermute | solution.py:417
  52.5 0.0 copy-done.5
  52.5 0.0 copy-done.6
  52.5 0.5 bitcast_add_fusion.refs_6_
  53.0 0.0 copy-start.1
  53.0 1.5 %collective-permute-done.5.refs_3_ = bf16[32,1024]{1,0:T(8,128)(2,1)S(1)} collective-permute-done((bf16[32,1024]{1,0:T(8,128)(2,1)S(1)}, bf16[32,1024]{1,0:T(8,128)(2,1)S(1)}, u32[]{:S(2)}, u32[]{:S(2)}) %collective-permute-start.5) | collective-permute-done | bytes 65568 | tf_op jit(solution)/shard_map/ppermute | solution.py:417
  54.5 1.3 %collective-permute-done.4.refs_2_ = bf16[32,1024]{1,0:T(8,128)(2,1)S(1)} collective-permute-done((bf16[32,1024]{1,0:T(8,128)(2,1)S(1)}, bf16[32,1024]{1,0:T(8,128)(2,1)S(1)}, u32[]{:S(2)}, u32[]{:S(2)}) %collective-permute-start.4) | collective-permute-done | bytes 65568 | tf_op jit(solution)/shard_map/ppermute | solution.py:417
  55.8 0.0 collective-permute-done.3.refs_1_
  55.8 0.5 shard_map.134
  56.4 0.1 collective-permute-start.6
  56.4 0.6 %add_bitcast_fusion = f32[2,1024,8]{1,2,0:T(8,128)} fusion(bf16[32,1024]{1,0:T(8,128)(2,1)S(1)} %collective-permute-done.5.refs_3_, bf16[32,1024]{1,0:T(8,128)(2,1)S(1)} %collective-permute-done.4.refs_2_, bf16[32,1024]{1,0:T(8,128)(2,1)S(1)} %collective-permute-done.3.refs_1_, bf16[32,1024]{1,0:T(8,128)(2,1)S(1)} %add.18.refs_0_), kind=kLoop, calls=%fused_computation.3 | loop fusion | flops 114688 | bytes 196608 | tf_op jit(solution)/shard_map/transpose | solution.py:480
  57.1 0.5 collective-permute-done.6
  57.6 0.6 %sub.3 = f32[2,4,768]{2,1,0:T(4,128)} subtract(f32[2,4,768]{2,1,0:T(4,128)S(1)} %get-tuple-element.19, f32[2,4,768]{2,1,0:T(4,128)S(1)} %collective-permute-done.6) | non-fusion elementwise | flops 6144 | bytes 73728 | tf_op jit(solution)/shard_map/sub | solution.py:479
  58.2 0.0 copy-done.1
  (1 shorter events, 0.0 us)
Async XLA Ops:
  0.6 40.6 %copy-start.2 = (bf16[2,4,768]{2,1,0:T(4,128)(2,1)S(1)}, bf16[2,4,768]{2,1,0:T(4,128)(2,1)}, u32[]{:S(2)}) copy-start(bf16[2,4,768]{2,1,0:T(4,128)(2,1)} %trial_ref.3) | copy-start | bytes 36868
  0.6 40.6 %copy-start.3 = (f32[768]{0:T(1024)S(1)}, f32[768]{0:T(1024)}, u32[]{:S(2)}) copy-start(f32[768]{0:T(1024)} %kinetic_ref.3) | copy-start | bytes 9220
  0.7 42.0 %copy-start = (bf16[2,1024,768]{2,1,0:T(8,128)(2,1)S(1)}, bf16[2,1024,768]{2,1,0:T(8,128)(2,1)}, u32[]{:S(2)}) copy-start(bf16[2,1024,768]{2,1,0:T(8,128)(2,1)} %refs_4_.1) | copy-start | bytes 9437188
  2.2 14.7 %all-to-all-start = ((bf16[8,8,1152]{2,1,0:T(8,128)(2,1)}), bf16[8,8,1152]{2,1,0:T(8,128)(2,1)S(1)}, u32[]{:S(2)}, u32[]{:S(2)}) async-start(bf16[8,8,1152]{2,1,0:T(8,128)(2,1)} %shard_map.130), calls=%async_computation | async-start | bytes 294912 | tf_op jit(solution)/shard_map/all_to_all | solution.py:437
  16.9 0.7 %copy-start.4 = (bf16[8,8,1152]{2,1,0:T(8,128)(2,1)}, bf16[8,8,1152]{2,1,0:T(8,128)(2,1)S(1)}, u32[]{:S(2)}) copy-start(bf16[8,8,1152]{2,1,0:T(8,128)(2,1)S(1)} %all-to-all-done.waves_ref) | copy-start | bytes 442372
  30.6 10.7 %all-to-all-start.1 = ((bf16[8,8,1024]{2,1,0:T(8,128)(2,1)}), bf16[8,8,1024]{2,1,0:T(8,128)(2,1)S(1)}, u32[]{:S(2)}, u32[]{:S(2)}) async-start(bf16[8,8,1024]{2,1,0:T(8,128)(2,1)} %get-tuple-element.12), calls=%async_computation.1 | async-start | bytes 262144 | tf_op jit(solution)/shard_map/all_to_all | solution.py:441
  34.0 7.5 %collective-permute-start.1 = (bf16[16,64,128]{2,1,0:T(8,128)(2,1)}, bf16[16,64,128]{2,1,0:T(8,128)(2,1)S(1)}, u32[]{:S(2)}, u32[]{:S(2)}) collective-permute-start(bf16[16,64,128]{2,1,0:T(8,128)(2,1)} %get-tuple-element.14), channel_id=1, source_target_pairs={{0,1},{1,0},{2,3},{3,2},{4,5},{5,4},{6,7},{7,6},{8,9},{9,8},{10,11... | collective-permute-start | bytes 786440 | tf_op jit(solution)/shard_map/ppermute | solution.py:417
  41.2 11.3 %copy-start.5 = (f32[64,16,128]{2,1,0:T(8,128)S(1)}, f32[64,16,128]{2,1,0:T(8,128)}, u32[]{:S(2)}) copy-start(f32[64,16,128]{2,1,0:T(8,128)} %param.14) | copy-start | bytes 1572868
  41.3 11.3 %copy-start.6 = (f32[16,64,128]{2,1,0:T(8,128)S(1)}, f32[16,64,128]{2,1,0:T(8,128)}, u32[]{:S(2)}) copy-start(f32[16,64,128]{2,1,0:T(8,128)} %get-tuple-element.17) | copy-start | bytes 1572868
  41.4 1.2 %collective-permute-start = (bf16[32,896]{1,0:T(8,128)(2,1)S(1)}, bf16[32,896]{1,0:T(8,128)(2,1)S(1)}, u32[]{:S(2)}, u32[]{:S(2)}) collective-permute-start(bf16[32,896]{1,0:T(8,128)(2,1)S(1)} %get-tuple-element.13.mine_ref), channel_id=1, source_target_pairs={{0,1},{1,0},{2,3},{3,2},{4,5},{5,4},{6,7},{7,6},{8,9},{9,8},{10,11... | collective-permute-start | bytes 172040 | tf_op jit(solution)/shard_map/ppermute | solution.py:417
  43.7 4.3 %collective-permute-start.2 = (bf16[32,1024]{1,0:T(8,128)(2,1)S(1)}, bf16[32,1024]{1,0:T(8,128)(2,1)S(1)}, u32[]{:S(2)}, u32[]{:S(2)}) collective-permute-start(bf16[32,1024]{1,0:T(8,128)(2,1)S(1)} %get-tuple-element.15), channel_id=1, source_target_pairs={{0,2},{2,0},{4,6},{6,4},{8,10},{10,8},{12,14},{14,12},{1,3},{3,1},... | collective-permute-start | bytes 196616 | tf_op jit(solution)/shard_map/ppermute | solution.py:417
  48.1 6.5 %collective-permute-start.5 = (bf16[32,1024]{1,0:T(8,128)(2,1)S(1)}, bf16[32,1024]{1,0:T(8,128)(2,1)S(1)}, u32[]{:S(2)}, u32[]{:S(2)}) collective-permute-start(bf16[32,1024]{1,0:T(8,128)(2,1)S(1)} %add.18.refs_0_), channel_id=1, source_target_pairs={{0,12},{2,14},{4,8},{6,10},{8,4},{10,6},{12,0},{14,2},{1,13},{3,15... | collective-permute-start | bytes 196616 | tf_op jit(solution)/shard_map/ppermute | solution.py:417
  48.7 7.1 %collective-permute-start.4 = (bf16[32,1024]{1,0:T(8,128)(2,1)S(1)}, bf16[32,1024]{1,0:T(8,128)(2,1)S(1)}, u32[]{:S(2)}, u32[]{:S(2)}) collective-permute-start(bf16[32,1024]{1,0:T(8,128)(2,1)S(1)} %add.18.refs_0_), channel_id=1, source_target_pairs={{0,8},{2,10},{4,12},{6,14},{8,0},{10,2},{12,4},{14,6},{1,9},{3,11}... | collective-permute-start | bytes 196616 | tf_op jit(solution)/shard_map/ppermute | solution.py:417
  49.5 6.4 %collective-permute-start.3 = (bf16[32,1024]{1,0:T(8,128)(2,1)S(1)}, bf16[32,1024]{1,0:T(8,128)(2,1)S(1)}, u32[]{:S(2)}, u32[]{:S(2)}) collective-permute-start(bf16[32,1024]{1,0:T(8,128)(2,1)S(1)} %add.18.refs_0_), channel_id=1, source_target_pairs={{0,4},{2,6},{4,0},{6,2},{8,12},{10,14},{12,8},{14,10},{1,5},{3,7},... | collective-permute-start | bytes 196616 | tf_op jit(solution)/shard_map/ppermute | solution.py:417
  53.0 5.2 %copy-start.1 = (f32[64,16,128]{2,1,0:T(8,128)}, f32[64,16,128]{2,1,0:T(8,128)S(1)}, u32[]{:S(2)}) copy-start(f32[64,16,128]{2,1,0:T(8,128)S(1)} %bitcast_add_fusion.refs_6_) | copy-start | bytes 1572868
  56.4 1.3 %collective-permute-start.6 = (f32[2,4,768]{2,1,0:T(4,128)S(1)}, f32[2,4,768]{2,1,0:T(4,128)S(1)}, u32[]{:S(2)}, u32[]{:S(2)}) collective-permute-start(f32[2,4,768]{2,1,0:T(4,128)S(1)} %get-tuple-element.20), channel_id=1, source_target_pairs={{0,1},{1,0},{2,3},{3,2},{4,5},{5,4},{6,7},{7,6},{8,9},{9,8},{10,11... | collective-permute-start | bytes 73736 | tf_op jit(solution)/shard_map/ppermute | solution.py:417

commit v8 on v7

--- a/solution.py
+++ b/solution.py
@@ -45,10 +45,11 @@
     third_table = np.concatenate(split_pair(values), axis=1)
     first = np.arange(width_first)
     angles = (np.outer(first, first) % width_first) * (2 * math.pi / width_first)
-    cosines = np.cos(angles) / math.sqrt(width_first)
-    sines = np.sin(angles) / math.sqrt(width_first)
-    back = np.block([[cosines, -sines], [sines, cosines]]).astype(BF16)
-    fore = np.block([[cosines, sines], [-sines, cosines]]).astype(BF16)
+    cosines, sines = np.cos(angles), np.sin(angles)
+    scale = 2.0 ** -math.ceil(math.log2(width_first) / 2)
+    back = (np.block([[cosines, -sines], [sines, cosines]]) * scale).astype(BF16)
+    scale = 1.0 / (width_first * scale)
+    fore = (np.block([[cosines, sines], [-sines, cosines]]) * scale).astype(BF16)
     return second_table, third_table, back, fore
 
 
@@ -107,11 +108,13 @@
     full = rows * slab
     groups = bands // 2
     low_lanes = lax.broadcasted_iota(jnp.int32, (1, width_third), 1) < fold
+    lift = 2.0 ** (2 * math.ceil(math.log2(width_first) / 2)) / width_first
     energies = [jnp.zeros((8, width_third), F32) for _ in range(groups)]
     weights = [
         jnp.where(
             low_lanes, occupation_ref[2 * g].astype(F32), occupation_ref[2 * g + 1].astype(F32)
         )
+        * lift
         for g in range(groups)
     ]
     centres = []
@@ -271,7 +274,7 @@
         for part in (jnp.where(low_lanes, values, 0.0), jnp.where(low_lanes, 0.0, values)):
             energy.append(jnp.sum(part, axis=(0, 1), keepdims=True))
     energy = jnp.concatenate(energy)
-    numerator = moving + energy
+    numerator = moving + lift * energy
     denominator = jnp.sum(square, axis=1, keepdims=True) * (1.0 / devices)
     scalars = []
     for value in (numerator, denominator):

time: 58.6 us -> 58.6 us (level)
  no operation moved by 1% of the time
where the time goes in v8:
time: 58.6 us; the launch traced here: 58.3 us
  waiting for transfers between devices  20.7 us (35%)
  Pallas kernels  16.3 us (28%)
  starting transfers between devices  15.5 us (26%)
  local copies, waits for them, and re-layouts  3.24 us (6%)
  other arithmetic  1.75 us (3%)
  between operations  0.75 us (1%)
    pallas_call x1, Pallas kernels, on_grid(): pl.pallas_call(functools.partial(grid_kernel, bands), out_shape=(jax.Shap...  13 us
    ppermute x7, waiting for transfers between devices, swap(): return lax.ppermute(values, axis, [(i, i ^ bit) for i in range(size)])  8.62 us
    all_to_all x1, starting transfers between devices, in_waves(): lax.all_to_all(packets, 'pw', split_axis=0, concat_axis=0, tiled=True)  7.25 us
    all_to_all x1, waiting for transfers between devices, in_waves(): lax.all_to_all(partial, 'pw', split_axis=0, concat_axis=0, tiled=True)  7.2 us
    all_to_all x1, waiting for transfers between devices, in_waves(): lax.all_to_all(packets, 'pw', split_axis=0, concat_axis=0, tiled=True)  4.9 us
    ppermute x7, starting transfers between devices, swap(): return lax.ppermute(values, axis, [(i, i ^ bit) for i in range(size)])  4.89 us
    all_to_all x1, starting transfers between devices, in_waves(): lax.all_to_all(partial, 'pw', split_axis=0, concat_axis=0, tiled=True)  3.38 us
    unnamed x15, local copies, waits for them, and re-layouts  3.24 us
  transfers between devices with their start and end apart: 9, of which 7 were waited for; matrix products, arithmetic and copies ran while one was open for 6% of the time, Pallas kernels for 0%

profile of v8, /device:TPU:0, one launch (start us, length us, event | category | flops | bytes accessed | tf_op | source)
XLA Modules:
  0.0 58.3 jit_solution(2897245634920407013)
XLA Ops:
  0.6 0.0 copy-start.2
  0.6 0.0 copy-start.3
  0.7 0.0 copy-start
  0.7 1.5 %shard_map.130 = bf16[8,8,1152]{2,1,0:T(8,128)(2,1)} custom-call(bf16[2,4,768]{2,1,0:T(4,128)(2,1)} %trial_ref.3, s32[768]{0:T(1024)} %cells_ref.1), custom_call_target="tpu_custom_call" | custom-call | tf_op jit(solution)/shard_map/pallas_call | solution.py:433
  2.2 7.3 %all-to-all-start = ((bf16[8,8,1152]{2,1,0:T(8,128)(2,1)}), bf16[8,8,1152]{2,1,0:T(8,128)(2,1)S(1)}, u32[]{:S(2)}, u32[]{:S(2)}) async-start(bf16[8,8,1152]{2,1,0:T(8,128)(2,1)} %shard_map.130), calls=%async_computation | async-start | bytes 294912 | tf_op jit(solution)/shard_map/all_to_all | solution.py:440
  9.5 2.5 %copy.23 = f32[128,16,128]{2,0,1:T(8,128)} copy(f32[128,16,128]{2,1,0:T(8,128)} %param.13) | data formatting | bytes 2097152 | tf_op args[2]
  12.0 4.9 %all-to-all-done.waves_ref = bf16[8,8,1152]{2,1,0:T(8,128)(2,1)S(1)} async-done(((bf16[8,8,1152]{2,1,0:T(8,128)(2,1)}), bf16[8,8,1152]{2,1,0:T(8,128)(2,1)S(1)}, u32[]{:S(2)}, u32[]{:S(2)}) %all-to-all-start) | async-done | bytes 147488 | tf_op jit(solution)/shard_map/all_to_all | solution.py:440
  16.9 0.0 copy-start.4
  16.9 0.7 %copy-done.4 = bf16[8,8,1152]{2,1,0:T(8,128)(2,1)} copy-done((bf16[8,8,1152]{2,1,0:T(8,128)(2,1)}, bf16[8,8,1152]{2,1,0:T(8,128)(2,1)S(1)}, u32[]{:S(2)}) %copy-start.4) | copy-done | bytes 147480
  17.6 13.0 %shard_map.131 = (bf16[8,8,1024]{2,1,0:T(8,128)(2,1)}, f32[16,64,128]{2,1,0:T(8,128)}, bf16[16,64,128]{2,1,0:T(8,128)(2,1)}) custom-call(bf16[8,8,1152]{2,1,0:T(8,128)(2,1)} %copy-done.4, bf16[8,32,128]{2,1,0:T(8,128)(2,1)} %constant.8.clone.second_ref, bf16[128,256]{1,0:T(8,128)(2,1)} %constant.9.clone.third_ref, bf16[256,256]{1,0:T(8,128)(2,1)} %constant.10.clone.back_ref, ...), custom_call_target="tpu_custom_call" | custom-call | tf_op jit(solution)/shard_map/pallas_call | solution.py:325
  30.6 3.4 %all-to-all-start.1 = ((bf16[8,8,1024]{2,1,0:T(8,128)(2,1)}), bf16[8,8,1024]{2,1,0:T(8,128)(2,1)S(1)}, u32[]{:S(2)}, u32[]{:S(2)}) async-start(bf16[8,8,1024]{2,1,0:T(8,128)(2,1)} %get-tuple-element.12), calls=%async_computation.1 | async-start | bytes 262144 | tf_op jit(solution)/shard_map/all_to_all | solution.py:444
  34.0 0.1 collective-permute-start.1
  34.1 7.2 %all-to-all-done.1.arrived_ref = bf16[8,8,1024]{2,1,0:T(8,128)(2,1)S(1)} async-done(((bf16[8,8,1024]{2,1,0:T(8,128)(2,1)}), bf16[8,8,1024]{2,1,0:T(8,128)(2,1)S(1)}, u32[]{:S(2)}, u32[]{:S(2)}) %all-to-all-start.1) | async-done | bytes 131104 | tf_op jit(solution)/shard_map/all_to_all | solution.py:444
  41.3 0.0 copy-done.2
  41.3 0.0 copy-done.3
  41.3 0.0 copy-start.5
  41.3 0.0 copy-start.6
  41.3 0.2 shard_map.132
  41.5 0.0 collective-permute-start
  41.5 0.0 collective-permute-done.1.received_ref
  41.5 1.2 %collective-permute-done.theirs_ref = bf16[32,896]{1,0:T(8,128)(2,1)S(1)} collective-permute-done((bf16[32,896]{1,0:T(8,128)(2,1)S(1)}, bf16[32,896]{1,0:T(8,128)(2,1)S(1)}, u32[]{:S(2)}, u32[]{:S(2)}) %collective-permute-start) | collective-permute-done | bytes 57376 | tf_op jit(solution)/shard_map/ppermute | solution.py:420
  42.7 0.0 copy-done
  42.7 1.0 %shard_map.133 = (bf16[32,1024]{1,0:T(8,128)(2,1)S(1)}, bf16[16,64,128]{2,1,0:T(8,128)(2,1)S(1)}) custom-call(bf16[32,896]{1,0:T(8,128)(2,1)S(1)} %get-tuple-element.13.mine_ref, bf16[32,896]{1,0:T(8,128)(2,1)S(1)} %collective-permute-done.theirs_ref, bf16[2,1024,768]{2,1,0:T(8,128)(2,1)S(1)} %copy-done, ...), custom_call_target="tpu_custom_call", output_to_operand_aliasing={{1}: (3, {})} | custom-call | tf_op jit(solution)/shard_map/pallas_call | solution.py:457
  43.7 0.3 collective-permute-start.2
  44.0 4.0 %collective-permute-done.2 = bf16[32,1024]{1,0:T(8,128)(2,1)S(1)} collective-permute-done((bf16[32,1024]{1,0:T(8,128)(2,1)S(1)}, bf16[32,1024]{1,0:T(8,128)(2,1)S(1)}, u32[]{:S(2)}, u32[]{:S(2)}) %collective-permute-start.2) | collective-permute-done | bytes 65568 | tf_op jit(solution)/shard_map/ppermute | solution.py:420
  48.1 0.6 %collective-permute-start.5 = (bf16[32,1024]{1,0:T(8,128)(2,1)S(1)}, bf16[32,1024]{1,0:T(8,128)(2,1)S(1)}, u32[]{:S(2)}, u32[]{:S(2)}) collective-permute-start(bf16[32,1024]{1,0:T(8,128)(2,1)S(1)} %add.18.refs_0_), channel_id=1, source_target_pairs={{0,12},{2,14},{4,8},{6,10},{8,4},{10,6},{12,0},{14,2},{1,13},{3,15... | collective-permute-start | bytes 196616 | tf_op jit(solution)/shard_map/ppermute | solution.py:420
  48.7 0.8 %collective-permute-start.4 = (bf16[32,1024]{1,0:T(8,128)(2,1)S(1)}, bf16[32,1024]{1,0:T(8,128)(2,1)S(1)}, u32[]{:S(2)}, u32[]{:S(2)}) collective-permute-start(bf16[32,1024]{1,0:T(8,128)(2,1)S(1)} %add.18.refs_0_), channel_id=1, source_target_pairs={{0,8},{2,10},{4,12},{6,14},{8,0},{10,2},{12,4},{14,6},{1,9},{3,11}... | collective-permute-start | bytes 196616 | tf_op jit(solution)/shard_map/ppermute | solution.py:420
  49.5 3.1 %collective-permute-start.3 = (bf16[32,1024]{1,0:T(8,128)(2,1)S(1)}, bf16[32,1024]{1,0:T(8,128)(2,1)S(1)}, u32[]{:S(2)}, u32[]{:S(2)}) collective-permute-start(bf16[32,1024]{1,0:T(8,128)(2,1)S(1)} %add.18.refs_0_), channel_id=1, source_target_pairs={{0,4},{2,6},{4,0},{6,2},{8,12},{10,14},{12,8},{14,10},{1,5},{3,7},... | collective-permute-start | bytes 196616 | tf_op jit(solution)/shard_map/ppermute | solution.py:420
  52.6 0.0 copy-done.5
  52.6 0.0 copy-done.6
  52.6 0.5 bitcast_add_fusion.refs_6_
  53.0 0.0 copy-start.1
  53.0 1.5 %collective-permute-done.5.refs_3_ = bf16[32,1024]{1,0:T(8,128)(2,1)S(1)} collective-permute-done((bf16[32,1024]{1,0:T(8,128)(2,1)S(1)}, bf16[32,1024]{1,0:T(8,128)(2,1)S(1)}, u32[]{:S(2)}, u32[]{:S(2)}) %collective-permute-start.5) | collective-permute-done | bytes 65568 | tf_op jit(solution)/shard_map/ppermute | solution.py:420
  54.6 1.3 %collective-permute-done.4.refs_2_ = bf16[32,1024]{1,0:T(8,128)(2,1)S(1)} collective-permute-done((bf16[32,1024]{1,0:T(8,128)(2,1)S(1)}, bf16[32,1024]{1,0:T(8,128)(2,1)S(1)}, u32[]{:S(2)}, u32[]{:S(2)}) %collective-permute-start.4) | collective-permute-done | bytes 65568 | tf_op jit(solution)/shard_map/ppermute | solution.py:420
  55.9 0.0 collective-permute-done.3.refs_1_
  55.9 0.5 shard_map.134
  56.4 0.1 collective-permute-start.6
  56.5 0.6 %add_bitcast_fusion = f32[2,1024,8]{1,2,0:T(8,128)} fusion(bf16[32,1024]{1,0:T(8,128)(2,1)S(1)} %collective-permute-done.5.refs_3_, bf16[32,1024]{1,0:T(8,128)(2,1)S(1)} %collective-permute-done.4.refs_2_, bf16[32,1024]{1,0:T(8,128)(2,1)S(1)} %collective-permute-done.3.refs_1_, bf16[32,1024]{1,0:T(8,128)(2,1)S(1)} %add.18.refs_0_), kind=kLoop, calls=%fused_computation.3 | loop fusion | flops 114688 | bytes 196608 | tf_op jit(solution)/shard_map/transpose | solution.py:483
  57.1 0.5 collective-permute-done.6
  57.7 0.6 %sub.3 = f32[2,4,768]{2,1,0:T(4,128)} subtract(f32[2,4,768]{2,1,0:T(4,128)S(1)} %get-tuple-element.19, f32[2,4,768]{2,1,0:T(4,128)S(1)} %collective-permute-done.6) | non-fusion elementwise | flops 6144 | bytes 73728 | tf_op jit(solution)/shard_map/sub | solution.py:482
  58.3 0.0 copy-done.1
  (1 shorter events, 0.0 us)
Async XLA Ops:
  0.6 40.7 %copy-start.2 = (bf16[2,4,768]{2,1,0:T(4,128)(2,1)S(1)}, bf16[2,4,768]{2,1,0:T(4,128)(2,1)}, u32[]{:S(2)}) copy-start(bf16[2,4,768]{2,1,0:T(4,128)(2,1)} %trial_ref.3) | copy-start | bytes 36868
  0.6 40.6 %copy-start.3 = (f32[768]{0:T(1024)S(1)}, f32[768]{0:T(1024)}, u32[]{:S(2)}) copy-start(f32[768]{0:T(1024)} %kinetic_ref.3) | copy-start | bytes 9220
  0.7 42.1 %copy-start = (bf16[2,1024,768]{2,1,0:T(8,128)(2,1)S(1)}, bf16[2,1024,768]{2,1,0:T(8,128)(2,1)}, u32[]{:S(2)}) copy-start(bf16[2,1024,768]{2,1,0:T(8,128)(2,1)} %refs_4_.1) | copy-start | bytes 9437188
  2.2 14.7 %all-to-all-start = ((bf16[8,8,1152]{2,1,0:T(8,128)(2,1)}), bf16[8,8,1152]{2,1,0:T(8,128)(2,1)S(1)}, u32[]{:S(2)}, u32[]{:S(2)}) async-start(bf16[8,8,1152]{2,1,0:T(8,128)(2,1)} %shard_map.130), calls=%async_computation | async-start | bytes 294912 | tf_op jit(solution)/shard_map/all_to_all | solution.py:440
  16.9 0.7 %copy-start.4 = (bf16[8,8,1152]{2,1,0:T(8,128)(2,1)}, bf16[8,8,1152]{2,1,0:T(8,128)(2,1)S(1)}, u32[]{:S(2)}) copy-start(bf16[8,8,1152]{2,1,0:T(8,128)(2,1)S(1)} %all-to-all-done.waves_ref) | copy-start | bytes 442372
  30.6 10.7 %all-to-all-start.1 = ((bf16[8,8,1024]{2,1,0:T(8,128)(2,1)}), bf16[8,8,1024]{2,1,0:T(8,128)(2,1)S(1)}, u32[]{:S(2)}, u32[]{:S(2)}) async-start(bf16[8,8,1024]{2,1,0:T(8,128)(2,1)} %get-tuple-element.12), calls=%async_computation.1 | async-start | bytes 262144 | tf_op jit(solution)/shard_map/all_to_all | solution.py:444
  34.0 7.5 %collective-permute-start.1 = (bf16[16,64,128]{2,1,0:T(8,128)(2,1)}, bf16[16,64,128]{2,1,0:T(8,128)(2,1)S(1)}, u32[]{:S(2)}, u32[]{:S(2)}) collective-permute-start(bf16[16,64,128]{2,1,0:T(8,128)(2,1)} %get-tuple-element.14), channel_id=1, source_target_pairs={{0,1},{1,0},{2,3},{3,2},{4,5},{5,4},{6,7},{7,6},{8,9},{9,8},{10,11... | collective-permute-start | bytes 786440 | tf_op jit(solution)/shard_map/ppermute | solution.py:420
  41.3 11.3 %copy-start.5 = (f32[64,16,128]{2,1,0:T(8,128)S(1)}, f32[64,16,128]{2,1,0:T(8,128)}, u32[]{:S(2)}) copy-start(f32[64,16,128]{2,1,0:T(8,128)} %param.14) | copy-start | bytes 1572868
  41.3 11.3 %copy-start.6 = (f32[16,64,128]{2,1,0:T(8,128)S(1)}, f32[16,64,128]{2,1,0:T(8,128)}, u32[]{:S(2)}) copy-start(f32[16,64,128]{2,1,0:T(8,128)} %get-tuple-element.17) | copy-start | bytes 1572868
  41.5 1.2 %collective-permute-start = (bf16[32,896]{1,0:T(8,128)(2,1)S(1)}, bf16[32,896]{1,0:T(8,128)(2,1)S(1)}, u32[]{:S(2)}, u32[]{:S(2)}) collective-permute-start(bf16[32,896]{1,0:T(8,128)(2,1)S(1)} %get-tuple-element.13.mine_ref), channel_id=1, source_target_pairs={{0,1},{1,0},{2,3},{3,2},{4,5},{5,4},{6,7},{7,6},{8,9},{9,8},{10,11... | collective-permute-start | bytes 172040 | tf_op jit(solution)/shard_map/ppermute | solution.py:420
  43.7 4.3 %collective-permute-start.2 = (bf16[32,1024]{1,0:T(8,128)(2,1)S(1)}, bf16[32,1024]{1,0:T(8,128)(2,1)S(1)}, u32[]{:S(2)}, u32[]{:S(2)}) collective-permute-start(bf16[32,1024]{1,0:T(8,128)(2,1)S(1)} %get-tuple-element.15), channel_id=1, source_target_pairs={{0,2},{2,0},{4,6},{6,4},{8,10},{10,8},{12,14},{14,12},{1,3},{3,1},... | collective-permute-start | bytes 196616 | tf_op jit(solution)/shard_map/ppermute | solution.py:420
  48.1 6.5 %collective-permute-start.5 = (bf16[32,1024]{1,0:T(8,128)(2,1)S(1)}, bf16[32,1024]{1,0:T(8,128)(2,1)S(1)}, u32[]{:S(2)}, u32[]{:S(2)}) collective-permute-start(bf16[32,1024]{1,0:T(8,128)(2,1)S(1)} %add.18.refs_0_), channel_id=1, source_target_pairs={{0,12},{2,14},{4,8},{6,10},{8,4},{10,6},{12,0},{14,2},{1,13},{3,15... | collective-permute-start | bytes 196616 | tf_op jit(solution)/shard_map/ppermute | solution.py:420
  48.7 7.1 %collective-permute-start.4 = (bf16[32,1024]{1,0:T(8,128)(2,1)S(1)}, bf16[32,1024]{1,0:T(8,128)(2,1)S(1)}, u32[]{:S(2)}, u32[]{:S(2)}) collective-permute-start(bf16[32,1024]{1,0:T(8,128)(2,1)S(1)} %add.18.refs_0_), channel_id=1, source_target_pairs={{0,8},{2,10},{4,12},{6,14},{8,0},{10,2},{12,4},{14,6},{1,9},{3,11}... | collective-permute-start | bytes 196616 | tf_op jit(solution)/shard_map/ppermute | solution.py:420
  49.5 6.4 %collective-permute-start.3 = (bf16[32,1024]{1,0:T(8,128)(2,1)S(1)}, bf16[32,1024]{1,0:T(8,128)(2,1)S(1)}, u32[]{:S(2)}, u32[]{:S(2)}) collective-permute-start(bf16[32,1024]{1,0:T(8,128)(2,1)S(1)} %add.18.refs_0_), channel_id=1, source_target_pairs={{0,4},{2,6},{4,0},{6,2},{8,12},{10,14},{12,8},{14,10},{1,5},{3,7},... | collective-permute-start | bytes 196616 | tf_op jit(solution)/shard_map/ppermute | solution.py:420
  53.0 5.2 %copy-start.1 = (f32[64,16,128]{2,1,0:T(8,128)}, f32[64,16,128]{2,1,0:T(8,128)S(1)}, u32[]{:S(2)}) copy-start(f32[64,16,128]{2,1,0:T(8,128)S(1)} %bitcast_add_fusion.refs_6_) | copy-start | bytes 1572868
  56.4 1.3 %collective-permute-start.6 = (f32[2,4,768]{2,1,0:T(4,128)S(1)}, f32[2,4,768]{2,1,0:T(4,128)S(1)}, u32[]{:S(2)}, u32[]{:S(2)}) collective-permute-start(f32[2,4,768]{2,1,0:T(4,128)S(1)} %get-tuple-element.20), channel_id=1, source_target_pairs={{0,1},{1,0},{2,3},{3,2},{4,5},{5,4},{6,7},{7,6},{8,9},{9,8},{10,11... | collective-permute-start | bytes 73736 | tf_op jit(solution)/shard_map/ppermute | solution.py:420
